TPU v7x, 32 devices: a whole 2x2x4 slice. The times are simulated.
32 devices in a mesh: grp: 2 (over y), tile: 16 (over z, x, core).
Axes of the slice: x: 2, y: 2, z: 4, core: 2. Of those that a mesh axis runs over, the one named last changes fastest.
Arguments:
- fields: bfloat16 [6, 128, 128, 256], P('grp', 'tile'), parts along dimension 0, may hold values from -6 to 6
- seam_tile: int32 [3, 16, 2], P(None, 'tile'), may hold values from 0 to 47, as said below
- seam_code: int32 [3, 16, 2], P(None, 'tile'), may hold values from 0 to 3
- encoder_weight: bfloat16 [3, 3, 256, 256], replicated, may hold values from -0.125 to 0.125
- encoder_bias: float32 [256], replicated, may hold values from -3 to 3
- middle_weight: bfloat16 [3, 3, 256, 256], replicated, may hold values from -0.125 to 0.125
- middle_bias: float32 [256], replicated, may hold values from -3 to 3
- upconv_weight: bfloat16 [2, 2, 256, 256], replicated, may hold values from -0.375 to 0.375
- upconv_bias: float32 [256], replicated, may hold values from -3 to 3
- decoder_weight: bfloat16 [3, 3, 512, 256], replicated, may hold values from -0.09375 to 0.09375
- decoder_offset_bias: float32 [256], replicated, may hold values from -3 to 3
Outputs:
- decoded: bfloat16 [6, 128, 128, 256], P('grp', 'tile'), parts along dimension 0
There are 2 independent parts, one for each index of `grp`. A program takes and returns all parts, laid end to end along the dimension named above; an argument that names none is the same for every part. Nothing has to cross between parts.
Inputs may be any that keep to these rules, and one draw needn't show every extreme that they name: `seam_tile`: for each side, the 12 faces (cycle, face) name 12 different partner faces; all 4 tiles of one face side share the partner face and the code, and strip s names the tile of strip s of the partner face, or of strip 4 - 1 - s where the code is 2 or more.
All inputs are finite; a program needn't handle non-finite values.
Results may differ from a plain program's by a relative error of at most 0.0048.
Values may be sent and summed in bfloat16 or wider, within the bound.
No kernel may reach another device: no remote copies, remote signals or barrier semaphores. Data moves between devices by JAX's collectives and lax.ppermute only.
A program may use at most 128 MiB of HBM per device.

v0:
```python
import jax
import jax.numpy as jnp
from jax import lax
from jax.sharding import PartitionSpec as P


def with_halo(shard, sides, width):
    for axis, dim in sides:
        devices, length = (lax.axis_size(axis), shard.shape[dim])
        up = [(i, (i + 1) % devices) for i in range(devices)]
        down = [(j, i) for i, j in up]
        last = lax.slice_in_dim(shard, length - width, length, axis=dim)
        first = lax.slice_in_dim(shard, 0, width, axis=dim)
        before = lax.ppermute(last, axis, up)
        after = lax.ppermute(first, axis, down)
        shard = jnp.concatenate([before, shard, after], axis=dim)
    return shard


def gelu_tanh(values):
    return jax.nn.gelu(values, approximate=True)


def blank_edge_rows(extended, top_face, bottom_face):
    upper_row = extended[..., :1, :, :]
    lower_row = extended[..., -1:, :, :]
    upper_row = jnp.where(top_face, jnp.zeros_like(upper_row), upper_row)
    lower_row = jnp.where(bottom_face, jnp.zeros_like(lower_row), lower_row)
    return jnp.concatenate([upper_row, extended[..., 1:-1, :, :], lower_row], axis=-3)


def boundary_columns(extended):
    return jnp.stack([extended[..., :, 0, :], extended[..., :, -1, :]], axis=-3)


def pick_partner(flattened, partners, seam_codes):
    chosen = flattened[partners]
    column_bit = (seam_codes % 2)[..., None, None]
    single = jnp.where(column_bit == 0, chosen[..., 0, :, :], chosen[..., 1, :, :])
    mirror_flag = (seam_codes // 2)[..., None, None]
    return jnp.where(mirror_flag == 1, single[..., ::-1, :], single)


def attach_columns(extended, picked):
    left_col = picked[..., 0, :, :][..., :, None, :]
    right_col = picked[..., 1, :, :][..., :, None, :]
    return jnp.concatenate([left_col, extended, right_col], axis=-2)


def convolve(padded, weight, bias):
    leading = padded.shape[:-3]
    rows_out = padded.shape[-3] - 2
    cols_out = padded.shape[-2] - 2
    chans_in = padded.shape[-1]
    chans_out = weight.shape[-1]
    accumulated = jnp.zeros(leading + (rows_out, cols_out, chans_out), jnp.float32)
    for row_tap in range(3):
        for col_tap in range(3):
            window = padded[..., row_tap : row_tap + rows_out, col_tap : col_tap + cols_out, :]
            product = jnp.dot(
                window.reshape(-1, chans_in),
                weight[row_tap, col_tap],
                preferred_element_type=jnp.float32,
            )
            accumulated = accumulated + product.reshape(accumulated.shape)
    return accumulated + bias


def coarsen_grid(sphere_map):
    leading = sphere_map.shape[:-3]
    rows_in, cols_in, chans_in = sphere_map.shape[-3:]
    values = sphere_map.astype(jnp.float32).reshape(
        leading + (rows_in // 2, 2, cols_in // 2, 2, chans_in)
    )
    return jnp.mean(values, axis=(-4, -2)).astype(jnp.bfloat16)


def upsample(coarse, weight, bias):
    leading = coarse.shape[:-3]
    rows_in, cols_in, chans_in = coarse.shape[-3:]
    chans_out = weight.shape[-1]
    flattened = coarse.reshape(-1, chans_in)
    phases = []
    for row_phase in range(2):
        phase_row = []
        for col_phase in range(2):
            product = jnp.dot(
                flattened, weight[row_phase, col_phase], preferred_element_type=jnp.float32
            )
            phase_row.append(product.reshape(leading + (rows_in, cols_in, chans_out)))
        phases.append(
            jnp.stack(phase_row, axis=-2).reshape(leading + (rows_in, 2 * cols_in, chans_out))
        )
    full = jnp.stack(phases, axis=-3).reshape(leading + (2 * rows_in, 2 * cols_in, chans_out))
    return (full + bias).astype(jnp.bfloat16)


def flatten_gathered(gathered):
    return gathered.reshape((-1,) + gathered.shape[2:])


def on_device(
    fields,
    seam_tile,
    seam_code,
    encoder_weight,
    encoder_bias,
    middle_weight,
    middle_bias,
    upconv_weight,
    upconv_bias,
    decoder_weight,
    decoder_offset_bias,
):
    strip_count = lax.axis_size("tile") // 4
    strip_index = (lax.axis_index("tile") + strip_count // 2) % strip_count
    top_face = strip_index == 0
    bottom_face = strip_index == strip_count - 1
    partners = seam_tile[:, 0, :]
    seam_codes = seam_code[:, 0, :]
    extended = blank_edge_rows(with_halo(fields, (("tile", 1),), 1), top_face, bottom_face)
    gathered = lax.all_gather(boundary_columns(extended)[:, None], "tile", axis=1, tiled=True)
    padded = attach_columns(
        extended, pick_partner(flatten_gathered(gathered), partners, seam_codes)
    )
    shortcut_map = gelu_tanh(convolve(padded, encoder_weight, encoder_bias)).astype(jnp.bfloat16)
    averaged_map = coarsen_grid(shortcut_map)
    extended = blank_edge_rows(with_halo(averaged_map, (("tile", 1),), 1), top_face, bottom_face)
    gathered = lax.all_gather(boundary_columns(extended)[:, None], "tile", axis=1, tiled=True)
    padded = attach_columns(
        extended, pick_partner(flatten_gathered(gathered), partners, seam_codes)
    )
    coarse = gelu_tanh(convolve(padded, middle_weight, middle_bias)).astype(jnp.bfloat16)
    upsampled = upsample(coarse, upconv_weight, upconv_bias)
    joined = jnp.concatenate([upsampled, shortcut_map], axis=-1)
    joined_ext = blank_edge_rows(with_halo(joined, (("tile", 1),), 1), top_face, bottom_face)
    gathered = lax.all_gather(boundary_columns(joined_ext)[:, None], "tile", axis=1, tiled=True)
    padded = attach_columns(
        joined_ext, pick_partner(flatten_gathered(gathered), partners, seam_codes)
    )
    return convolve(padded, decoder_weight, decoder_offset_bias).astype(jnp.bfloat16)


def solution(mesh):
    return jax.shard_map(
        on_device,
        mesh=mesh,
        in_specs=(
            P("grp", "tile", None, None),
            P(None, "tile", None),
            P(None, "tile", None),
            P(),
            P(),
            P(),
            P(),
            P(),
            P(),
            P(),
            P(),
        ),
        out_specs=P("grp", "tile", None, None),
        check_vma=False,
    )
```

profile of v0, /device:TPU:1, one launch (start us, length us, event | category | flops | bytes accessed | tf_op | source)
XLA Modules:
  0.0 164.5 jit_solution(4642079154385857864)
XLA Ops:
  0.0 1.0 fusion.168
  1.1 2.7 %collective-permute-start = (bf16[3,1,128,256]{3,2,1,0:T(8,128)(2,1)S(1)}, bf16[3,1,128,256]{3,2,1,0:T(8,128)(2,1)S(1)}, u32[]{:S(2)}, u32[]{:S(2)}) collective-permute-start(bf16[3,1,128,256]{3,2,1,0:T(8,128)(2,1)S(1)} %get-tuple-element.15), channel_id=1, source_target_pairs={{0,1},{1,2},{2,3},{3,4},{4,5},{5,6},{6,7},{7,8},{8,9},{9,10},{10,1... | collective-permute-start | bytes 589832 | tf_op jit(solution)/shard_map/ppermute | solution.py:14
  3.7 0.7 compare_select_fusion
  4.4 3.8 %fusion.131 = f32[3,8,128,256]{3,2,1,0:T(8,128)} fusion(bf16[3,8,128,256]{3,2,1,0:T(8,128)(2,1)} %param.11, bf16[3,3,256,256]{3,2,1,0:T(8,128)(2,1)} %param.14), kind=kOutput, calls=%fused_computation.154 | convolution fusion | flops 402653184 | bytes 4849664 | tf_op jit(solution)/shard_map/dot_general | solution.py:60
  8.6 2.3 %collective-permute-done.1 = bf16[3,1,128,256]{3,2,1,0:T(8,128)(2,1)S(1)} collective-permute-done((bf16[3,1,128,256]{3,2,1,0:T(8,128)(2,1)S(1)}, bf16[3,1,128,256]{3,2,1,0:T(8,128)(2,1)S(1)}, u32[]{:S(2)}, u32[]{:S(2)}) %collective-permute-start.1) | collective-permute-done | bytes 196640 | tf_op jit(solution)/shard_map/ppermute | solution.py:15
  10.9 3.1 %fusion.40 = f32[3,8,128,256]{3,2,1,0:T(8,128)} fusion(bf16[3,1,128,256]{3,2,1,0:T(8,128)(2,1)S(1)} %broadcast_select_fusion.2, bf16[3,8,128,256]{3,2,1,0:T(8,128)(2,1)S(1)} %copy-done, bf16[3,3,256,256]{3,2,1,0:T(8,128)(2,1)} %param.14), kind=kOutput, calls=%fused_computation.51 | convolution fusion | flops 406192128 | bytes 5046272 | tf_op jit(solution)/shard_map/dot_general | solution.py:60
  14.1 3.2 %fusion.36 = f32[3,8,128,256]{3,2,1,0:T(8,128)} fusion(bf16[3,8,128,256]{3,2,1,0:T(8,128)(2,1)S(1)} %copy-done, bf16[3,1,128,256]{3,2,1,0:T(8,128)(2,1)S(1)} %broadcast_select_fusion.3, bf16[3,3,256,256]{3,2,1,0:T(8,128)(2,1)} %param.14), kind=kOutput, calls=%fused_computation.47 | convolution fusion | flops 406192128 | bytes 5046272 | tf_op jit(solution)/shard_map/dot_general | solution.py:60
  17.4 22.1 %all-gather = bf16[3,32,10,256]{3,0,2,1:T(4,128)(2,1)S(1)} all-gather(bf16[3,2,10,256]{3,0,2,1:T(4,128)(2,1)S(1)} %pad_maximum_fusion.13), channel_id=2, replica_groups=mesh['grp'=2,'tile'=16] {'tile'}, dimensions={1}, use_global_device_ids=true | all-gather | bytes 522240 | tf_op jit(solution)/shard_map/all_gather | solution.py:122
  39.6 0.2 reshape.236
  39.8 0.7 gather_fusion
  40.9 1.1 pad_maximum_fusion.2
  42.1 0.6 fusion.50
  42.7 0.6 fusion.54
  43.3 0.6 fusion.48
  43.9 0.6 fusion.52
  44.5 0.6 fusion.56
  45.1 1.3 copy-done.1
  46.4 4.6 %fusion.19 = bf16[3,8,128,256]{3,2,1,0:T(8,128)(2,1)S(1)} fusion(f32[3,8,128,256]{3,2,1,0:T(8,128)} %fusion.40, f32[3,8,128,256]{3,2,1,0:T(8,128)S(1)} %fusion.48, f32[3,8,128,256]{3,2,1,0:T(8,128)S(1)} %fusion.50, f32[3,8,128,256]{3,2,1,0:T(8,128)S(1)} %copy-done.1, f32[3,8,128,256]{3,2,1,0:T(8,128)S(1)} %fusion.52, f32[3,8,128,256]{3,2,1,0:T(8,128)S(1)} %fusion.54, ...), kind=kOutput, calls=%fused_computation.25 | convolution fusion | flops 416808960 | bytes 28443648 | tf_op jit(solution)/shard_map/dot_general | solution.py:60
  51.0 3.0 %reshape.243 = f32[3,4,2,64,2,256]{5,4,3,2,1,0:T(2,128)} reshape(bf16[3,8,128,256]{3,2,1,0:T(8,128)(2,1)S(1)} %fusion.19) | data formatting | bytes 4718592 | tf_op jit(solution)/shard_map/reshape | solution.py:72
  54.0 4.3 %reduce_sum.9 = f32[3,4,64,256]{3,2,1,0:T(8,128)S(1)} reduce(f32[3,4,2,64,2,256]{5,4,3,2,1,0:T(2,128)} %reshape.243, f32[]{:T(128)} %constant.78.clone.1), dimensions={2,4}, to_apply=%region_0.1 | reduce | flops 589824 | bytes 3932164 | tf_op jit(solution)/shard_map/reduce_sum | solution.py:75
  58.5 0.5 collective-permute-start.3
  59.0 1.2 fusion.121
  60.2 2.4 %collective-permute-done.3 = bf16[3,1,64,256]{3,2,1,0:T(8,128)(2,1)S(1)} collective-permute-done((bf16[3,1,64,256]{3,2,1,0:T(8,128)(2,1)S(1)}, bf16[3,1,64,256]{3,2,1,0:T(8,128)(2,1)S(1)}, u32[]{:S(2)}, u32[]{:S(2)}) %collective-permute-start.3) | collective-permute-done | bytes 98336 | tf_op jit(solution)/shard_map/ppermute | solution.py:15
  62.7 21.7 %all-gather.1 = bf16[3,32,6,256]{3,2,0,1:T(8,128)(2,1)S(1)} all-gather(bf16[3,2,6,256]{3,2,0,1:T(8,128)(2,1)S(1)} %pad_maximum_fusion.17), channel_id=3, replica_groups=mesh['grp'=2,'tile'=16] {'tile'}, dimensions={1}, use_global_device_ids=true | all-gather | bytes 313344 | tf_op jit(solution)/shard_map/all_gather | solution.py:129
  84.6 0.6 gather_fusion.1
  85.5 0.4 maximum_maximum_fusion.2
  85.9 1.2 fusion.81
  87.1 0.2 fusion.85
  87.3 0.3 fusion.89
  87.6 0.3 fusion.79
  87.9 0.3 fusion.83
  88.2 0.3 fusion.87
  88.5 0.4 fusion.64
  88.9 0.3 copy-done.11
  89.1 0.5 fusion.72
  89.6 0.5 copy-done.5
  90.2 0.3 convolution_bitcast_fusion
  90.4 0.3 convolution_bitcast_fusion.1
  90.7 0.3 convolution_bitcast_fusion.2
  91.0 0.3 convolution_bitcast_fusion.3
  91.3 1.0 copy.159
  92.4 0.1 pad_maximum_fusion.3
  92.5 1.0 copy.158
  93.5 0.7 pad_maximum_fusion.1
  94.3 0.5 copy.160
  95.0 0.4 add_convert_fusion.1
  95.4 0.4 collective-permute-start.5
  95.8 1.4 collective-permute-start.4
  97.2 3.6 %fusion.32 = f32[3,8,128,256]{3,2,1,0:T(8,128)} fusion(bf16[3,8,128,256]{3,2,1,0:T(8,128)(2,1)S(1)} %fusion.19, bf16[3,8,128,256]{3,2,1,0:T(8,128)(2,1)S(1)} %add_convert_fusion.1, bf16[3,3,512,256]{3,2,1,0:T(8,128)(2,1)} %param.20), kind=kOutput, calls=%fused_computation.39 | convolution fusion | flops 811597824 | bytes 6553600 | tf_op jit(solution)/shard_map/dot_general | solution.py:60
  100.8 6.1 %collective-permute-done.5 = bf16[3,1,128,512]{3,2,1,0:T(8,128)(2,1)S(1)} collective-permute-done((bf16[3,1,128,512]{3,2,1,0:T(8,128)(2,1)S(1)}, bf16[3,1,128,512]{3,2,1,0:T(8,128)(2,1)S(1)}, u32[]{:S(2)}, u32[]{:S(2)}) %collective-permute-start.5) | collective-permute-done | bytes 393248 | tf_op jit(solution)/shard_map/ppermute | solution.py:15
  106.9 3.6 %fusion.6 = f32[3,8,128,256]{3,2,1,0:T(8,128)} fusion(bf16[3,1,128,512]{3,2,1,0:T(8,128)(2,1)S(1)} %broadcast_select_fusion, bf16[3,8,128,256]{3,2,1,0:T(8,128)(2,1)S(1)} %fusion.19, bf16[3,8,128,256]{3,2,1,0:T(8,128)(2,1)S(1)} %add_convert_fusion.1, bf16[3,3,512,256]{3,2,1,0:T(8,128)(2,1)} %param.20), kind=kOutput, calls=%fused_computation.12 | convolution fusion | flops 815923200 | bytes 6946816 | tf_op jit(solution)/shard_map/dot_general | solution.py:60
  110.6 3.7 %fusion = f32[3,8,128,256]{3,2,1,0:T(8,128)} fusion(bf16[3,8,128,256]{3,2,1,0:T(8,128)(2,1)S(1)} %fusion.19, bf16[3,8,128,256]{3,2,1,0:T(8,128)(2,1)S(1)} %add_convert_fusion.1, bf16[3,1,128,512]{3,2,1,0:T(8,128)(2,1)S(1)} %broadcast_select_fusion.1, bf16[3,3,512,256]{3,2,1,0:T(8,128)(2,1)} %param.20), kind=kOutput, calls=%fused_computation.6 | convolution fusion | flops 815923200 | bytes 6946816 | tf_op jit(solution)/shard_map/dot_general | solution.py:60
  114.4 21.5 %all-gather.2 = bf16[3,32,10,512]{3,0,2,1:T(4,128)(2,1)S(1)} all-gather(bf16[3,2,10,512]{3,0,2,1:T(4,128)(2,1)S(1)} %pad_maximum_fusion.8), channel_id=4, replica_groups=mesh['grp'=2,'tile'=16] {'tile'}, dimensions={1}, use_global_device_ids=true | all-gather | bytes 1044480 | tf_op jit(solution)/shard_map/all_gather | solution.py:137
  135.9 1.3 copy.163
  137.3 3.2 %reshape.241 = bf16[48,2,10,512]{3,1,0,2:T(2,128)(2,1)} reshape(bf16[3,32,10,512]{3,1,0,2:T(8,128)(2,1)} %copy.163) | data formatting | bytes 1966080 | tf_op jit(solution)/shard_map/reshape | solution.py:99
  140.5 2.7 %gather_fusion.2 = bf16[6,2,10,512]{3,1,2,0:T(2,128)(2,1)} fusion(bf16[48,2,10,512]{3,1,0,2:T(2,128)(2,1)} %reshape.241, s32[1024]{0:T(1024)S(1)} %pad_clamp_fusion), kind=kCustom, calls=%fused_computation.2 | custom fusion | bytes 245784 | tf_op jit(solution)/shard_map/gather | solution.py:37
  143.1 1.2 fusion.170
  144.9 3.4 %pad_maximum_fusion = (bf16[3,10,129,512]{3,2,1,0:T(8,128)(2,1)S(1)}, bf16[3,10,129,512]{3,2,1,0:T(8,128)(2,1)S(1)}) fusion(bf16[3,10,1,512]{3,2,1,0:T(2,128)(2,1)S(1)} %copy.169, bf16[3,1,128,512]{3,2,1,0:T(8,128)(2,1)S(1)} %broadcast_select_fusion, bf16[3,8,128,256]{3,2,1,0:T(8,128)(2,1)S(1)} %fusion.19, bf16[3,8,128,256]{3,2,1,0:T(8,128)(2,1)S(1)} %add_convert_fusion.1, ...), kind=kLoop, calls=%fused_computation.5 | loop fusion | flops 39628800 | bytes 11919360 | tf_op jit(solution)/shard_map/concatenate | solution.py:47
  148.3 2.7 %fusion.24 = f32[3,8,128,256]{3,2,1,0:T(8,128)} fusion(bf16[3,10,129,512]{3,2,1,0:T(8,128)(2,1)S(1)} %get-tuple-element.5, bf16[3,3,512,256]{3,2,1,0:T(8,128)(2,1)S(1)} %copy-done.6), kind=kOutput, calls=%fused_computation.30 | convolution fusion | flops 805306368 | bytes 6553600 | tf_op jit(solution)/shard_map/dot_general | solution.py:60
  151.0 2.6 %fusion.28 = f32[3,8,128,256]{3,2,1,0:T(8,128)} fusion(bf16[3,10,129,512]{3,2,1,0:T(8,128)(2,1)S(1)} %get-tuple-element.5, bf16[3,3,512,256]{3,2,1,0:T(8,128)(2,1)S(1)} %copy-done.6), kind=kOutput, calls=%fused_computation.34 | convolution fusion | flops 805306368 | bytes 6553600 | tf_op jit(solution)/shard_map/dot_general | solution.py:60
  153.6 1.0 fusion.22
  154.6 1.0 fusion.26
  155.6 1.0 fusion.30
  156.6 7.9 %add_convert_fusion = bf16[3,8,128,256]{3,2,1,0:T(8,128)(2,1)} fusion(f32[3,8,128,256]{3,2,1,0:T(8,128)} %fusion.6, f32[3,8,128,256]{3,2,1,0:T(8,128)S(1)} %fusion.22, f32[3,8,128,256]{3,2,1,0:T(8,128)} %fusion.24, f32[3,8,128,256]{3,2,1,0:T(8,128)} %fusion.32, f32[3,8,128,256]{3,2,1,0:T(8,128)S(1)} %fusion.26, f32[3,8,128,256]{3,2,1,0:T(8,128)} %fusion.28, ...), kind=kOutput, calls=%fused_computation.43 | convolution fusion | flops 813170688 | bytes 30147584 | tf_op jit(solution)/shard_map/dot_general | solution.py:60
  (75 shorter events, 3.0 us)
Async XLA Ops:
  1.1 13.0 %collective-permute-start = (bf16[3,1,128,256]{3,2,1,0:T(8,128)(2,1)S(1)}, bf16[3,1,128,256]{3,2,1,0:T(8,128)(2,1)S(1)}, u32[]{:S(2)}, u32[]{:S(2)}) collective-permute-start(bf16[3,1,128,256]{3,2,1,0:T(8,128)(2,1)S(1)} %get-tuple-element.15), channel_id=1, source_target_pairs={{0,1},{1,2},{2,3},{3,4},{4,5},{5,6},{6,7},{7,8},{8,9},{9,10},{10,1... | collective-permute-start | bytes 589832 | tf_op jit(solution)/shard_map/ppermute | solution.py:14
  3.7 7.2 %collective-permute-start.1 = (bf16[3,1,128,256]{3,2,1,0:T(8,128)(2,1)S(1)}, bf16[3,1,128,256]{3,2,1,0:T(8,128)(2,1)S(1)}, u32[]{:S(2)}, u32[]{:S(2)}) collective-permute-start(bf16[3,1,128,256]{3,2,1,0:T(8,128)(2,1)S(1)} %get-tuple-element.16), channel_id=1, source_target_pairs={{1,0},{2,1},{3,2},{4,3},{5,4},{6,5},{7,6},{8,7},{9,8},{10,9},{11,1... | collective-permute-start | bytes 589832 | tf_op jit(solution)/shard_map/ppermute | solution.py:15
  4.4 3.8 %copy-start.10 = (s32[3,1,2]{0,2,1:T(2,128)S(1)}, s32[3,1,2]{0,2,1:T(2,128)}, u32[]{:S(2)}) copy-start(s32[3,1,2]{0,2,1:T(2,128)} %param.13) | copy-start | bytes 76
  4.4 6.5 %copy-start = (bf16[3,8,128,256]{3,2,1,0:T(8,128)(2,1)S(1)}, bf16[3,8,128,256]{3,2,1,0:T(8,128)(2,1)}, u32[]{:S(2)}) copy-start(bf16[3,8,128,256]{3,2,1,0:T(8,128)(2,1)} %param.11) | copy-start | bytes 4718596
  40.9 1.3 copy-start.3
  44.5 1.9 %copy-start.1 = (f32[3,8,128,256]{3,2,1,0:T(8,128)S(1)}, f32[3,8,128,256]{3,2,1,0:T(8,128)}, u32[]{:S(2)}) copy-start(f32[3,8,128,256]{3,2,1,0:T(8,128)} %fusion.131) | copy-start | bytes 9437188
  44.5 1.9 %copy-start.8 = (f32[256]{0:T(256)S(1)}, f32[256]{0:T(256)}, u32[]{:S(2)}) copy-start(f32[256]{0:T(256)} %param.15) | copy-start | bytes 3076
  58.4 1.7 %collective-permute-start.2 = (bf16[3,1,64,256]{3,2,1,0:T(8,128)(2,1)S(1)}, bf16[3,1,64,256]{3,2,1,0:T(8,128)(2,1)S(1)}, u32[]{:S(2)}, u32[]{:S(2)}) collective-permute-start(bf16[3,1,64,256]{3,2,1,0:T(8,128)(2,1)S(1)} %get-tuple-element.21), channel_id=1, source_target_pairs={{0,1},{1,2},{2,3},{3,4},{4,5},{5,6},{6,7},{7,8},{8,9},{9,10},{10,1... | collective-permute-start | bytes 294920 | tf_op jit(solution)/shard_map/ppermute | solution.py:14
  58.5 4.1 %collective-permute-start.3 = (bf16[3,1,64,256]{3,2,1,0:T(8,128)(2,1)S(1)}, bf16[3,1,64,256]{3,2,1,0:T(8,128)(2,1)S(1)}, u32[]{:S(2)}, u32[]{:S(2)}) collective-permute-start(bf16[3,1,64,256]{3,2,1,0:T(8,128)(2,1)S(1)} %get-tuple-element.22), channel_id=1, source_target_pairs={{1,0},{2,1},{3,2},{4,3},{5,4},{6,5},{7,6},{8,7},{9,8},{10,9},{11,1... | collective-permute-start | bytes 294920 | tf_op jit(solution)/shard_map/ppermute | solution.py:15
  85.2 1.9 %copy-start.4 = (bf16[3,3,256,256]{3,2,1,0:T(8,128)(2,1)S(1)}, bf16[3,3,256,256]{3,2,1,0:T(8,128)(2,1)}, u32[]{:S(2)}) copy-start(bf16[3,3,256,256]{3,2,1,0:T(8,128)(2,1)} %param.16) | copy-start | bytes 3538948
  88.4 0.7 copy-start.11
  89.1 1.0 copy-start.5
  94.3 0.7 copy-start.9
  95.4 11.5 %collective-permute-start.5 = (bf16[3,1,128,512]{3,2,1,0:T(8,128)(2,1)S(1)}, bf16[3,1,128,512]{3,2,1,0:T(8,128)(2,1)S(1)}, u32[]{:S(2)}, u32[]{:S(2)}) collective-permute-start(bf16[3,1,128,512]{3,2,1,0:T(8,128)(2,1)S(1)} %get-tuple-element.10), channel_id=1, source_target_pairs={{1,0},{2,1},{3,2},{4,3},{5,4},{6,5},{7,6},{8,7},{9,8},{10,9},{11,1... | collective-permute-start | bytes 1179656 | tf_op jit(solution)/shard_map/ppermute | solution.py:15
  95.8 14.7 %collective-permute-start.4 = (bf16[3,1,128,512]{3,2,1,0:T(8,128)(2,1)S(1)}, bf16[3,1,128,512]{3,2,1,0:T(8,128)(2,1)S(1)}, u32[]{:S(2)}, u32[]{:S(2)}) collective-permute-start(bf16[3,1,128,512]{3,2,1,0:T(8,128)(2,1)S(1)} %get-tuple-element.9), channel_id=1, source_target_pairs={{0,1},{1,2},{2,3},{3,4},{4,5},{5,6},{6,7},{7,8},{8,9},{9,10},{10,1... | collective-permute-start | bytes 1179656 | tf_op jit(solution)/shard_map/ppermute | solution.py:14
  110.5 3.8 %copy-start.2 = (bf16[3,1,128,512]{3,2,1,0:T(8,128)(2,1)}, bf16[3,1,128,512]{3,2,1,0:T(8,128)(2,1)S(1)}, u32[]{:S(2)}) copy-start(bf16[3,1,128,512]{3,2,1,0:T(8,128)(2,1)S(1)} %broadcast_select_fusion.1) | copy-start | bytes 1179652
  144.9 3.4 %copy-start.6 = (bf16[3,3,512,256]{3,2,1,0:T(8,128)(2,1)S(1)}, bf16[3,3,512,256]{3,2,1,0:T(8,128)(2,1)}, u32[]{:S(2)}) copy-start(bf16[3,3,512,256]{3,2,1,0:T(8,128)(2,1)} %param.20) | copy-start | bytes 7077892
  155.6 1.0 copy-start.7
where the time goes:
time: 165 us; the launch traced here: 164 us
  blocking collectives  65.3 us (40%)
  matrix products  50.2 us (30%)
  local copies, waits for them, and re-layouts  20.2 us (12%)
  other arithmetic  12.4 us (8%)
  waiting for transfers between devices  10.8 us (7%)
  starting transfers between devices  5.01 us (3%)
    dot_general x27, matrix products, convolve(): jnp.dot(window.reshape(-1, chans_in), weight[row_tap, col_tap], preferred...  49.1 us
    all_gather x2, blocking collectives, on_device(): lax.all_gather(boundary_columns(extended)[:, None], 'tile', axis=1, tiled...  43.8 us
    all_gather x1, blocking collectives, on_device(): lax.all_gather(boundary_columns(joined_ext)[:, None], 'tile', axis=1, til...  21.5 us
    ppermute x3, waiting for transfers between devices, with_halo(): after = lax.ppermute(first, axis, down)  10.8 us
    concatenate x3, other arithmetic, attach_columns(): return jnp.concatenate([left_col, extended, right_col], axis=-2)  4.9 us
    reduce_sum x1, other arithmetic, coarsen_grid(): return jnp.mean(values, axis=(-4, -2)).astype(jnp.bfloat16)  4.28 us
    ppermute x3, starting transfers between devices, with_halo(): before = lax.ppermute(last, axis, up)  4.1 us
    gather x3, local copies, waits for them, and re-layouts, pick_partner(): chosen = flattened[partners]  4.01 us
  transfers between devices with their start and end apart: 6, of which 3 were waited for; matrix products, arithmetic and copies ran while one was open for 10% of the time, Pallas kernels for 0%

commit v1 on v0

v1 whole, which is shorter than its diff:
```python
import functools

import jax
import jax.numpy as jnp
from jax import lax
from jax.experimental import pallas as pl
from jax.experimental.pallas import tpu as pltpu
from jax.sharding import PartitionSpec as P

F32 = jnp.float32
BF16 = jnp.bfloat16
FACES = 4
MIB = 1 << 20


def dot(a, b):
    return jnp.dot(a, b, preferred_element_type=F32)


def gelu(x):
    return 0.5 * x * (1.0 + jnp.tanh(0.7978845608 * (x + 0.044715 * x * x * x)))


def rows_iota(n):
    return lax.broadcasted_iota(jnp.int32, (n, 1), 0)


class Layout:
    def __init__(self, tiles, height, depth, base, payload):
        self.tiles = tiles
        self.strips = tiles // FACES
        self.height = height
        self.depth = depth
        self.base = base
        self.payload = payload
        self.joint = self.strips == 4
        self.stride = height + (depth if self.joint else 2 * depth)

    def source(self, strip, flip, face, column, row):
        height, last = self.height, self.strips - 1
        strip = jnp.where(flip == 1, last - strip, strip)
        row = jnp.where(flip == 1, height - 1 - row, row)
        upper = jnp.where(strip >= self.strips // 2, 1, 0)
        odd = lax.rem(strip, 2)
        above = row < 0
        below = row >= height
        away = jnp.where(above, -row, row - (height - 1))
        near = (above & (odd == 1)) | (below & (odd == 0))
        missing = (above & (strip == 0)) | (below & (strip == last))
        own = (face * 2 + upper) * self.payload
        start = self.base + column * self.stride
        inside = own + start + row
        beside = own + start + height + away - 1
        if self.joint:
            across = (face * 2 + 1 - upper) * self.payload + start
            far = across + jnp.where(above, height - away, away - 1)
        else:
            far = beside + self.depth
        place = jnp.where(above | below, jnp.where(near, beside, far), inside)
        return jnp.where(missing, -1, place)


def strip_of(tiles):
    strips = tiles // FACES
    return lax.rem(lax.axis_index("tile") + strips // 2, strips)


def seam_of(tile_ref, code_ref, tiles, cycle, side):
    strips = tiles // FACES
    partner = tile_ref[cycle, 0, side]
    code = code_ref[cycle, 0, side]
    other = lax.div(partner, tiles)
    place = partner - other * tiles + strips // 2
    face = lax.rem(lax.div(place, strips), FACES)
    return other, face, lax.rem(code, 2), lax.div(code, 2)


def pick(targets, table):
    wanted = jnp.concatenate(targets, axis=0)
    shape = (wanted.shape[0], table.shape[0])
    lanes = lax.broadcasted_iota(jnp.int32, shape, 1)
    chooser = jnp.where(lanes == wanted, 1.0, 0.0).astype(BF16)
    return dot(chooser, table).astype(BF16)


def shifted_sum(taps, cols):
    left, middle, right = taps
    n = middle.shape[0]
    place = lax.broadcasted_iota(jnp.int32, middle.shape, 0) & (cols - 1)
    left = jnp.where(place == 0, 0.0, pltpu.roll(left, 1, 0))
    right = jnp.where(place == cols - 1, 0.0, pltpu.roll(right, n - 1, 0))
    return middle + left + right


def stack_taps(stacked, row_of, rows):
    depth = stacked.shape[-1] // 3
    for row in range(-1, rows + 1):
        value = row_of(row)
        for tap in range(3):
            at = row + 1 - tap
            if 0 <= at < rows:
                stacked[at, :, tap * depth : (tap + 1) * depth] = value


def column_taps(lhs, weight_ref):
    depth = weight_ref.shape[2]
    return [
        dot(lhs, weight_ref[:, tap].reshape(3 * depth, weight_ref.shape[3]))
        for tap in range(3)
    ]


def halo_rows(rows_ref, near, odd, height):
    zero = jnp.zeros_like(near)
    upper = jnp.where(odd == 1, near, zero)
    lower = jnp.where(odd == 1, zero, near)

    def row_of(row):
        if row < 0:
            return upper
        if row >= height:
            return lower
        return rows_ref[0, row]

    return row_of


def column_sum(parts, cycle, height):
    at = cycle * 16
    return sum(parts[tap][at + tap : at + tap + height] for tap in range(3))


def pack_fields(layout, left_ref, right_ref, near_ref, far_ref, tile_ref, code_ref, out_ref, scratch):
    height = layout.height
    cols = near_ref.shape[1]
    cycles = near_ref.shape[0]
    block = left_ref.shape[2]
    scratch[...] = jnp.zeros_like(scratch)
    lanes = lax.broadcasted_iota(jnp.int32, (1, scratch.shape[1]), 1)
    noted = jnp.zeros((1, scratch.shape[1]), F32)
    for cycle in range(cycles):
        for side in range(2):
            column = cycle * 2 + side
            start = column * layout.stride
            ref, at = ((left_ref, 0), (right_ref, block - 1))[side]
            for row in range(height):
                scratch[start + row : start + row + 1] = ref[cycle, row].astype(F32)[at : at + 1]
            halos = [near_ref] if layout.joint else [near_ref, far_ref]
            for k, halo in enumerate(halos):
                first = 0 if side == 0 else cols - 16
                value = halo[cycle, first : first + 16].astype(F32)
                pos = 0 if side == 0 else 15
                scratch[start + height + k : start + height + k + 1] = value[pos : pos + 1]
            other, face, side_bit, flip = seam_of(tile_ref, code_ref, layout.tiles, cycle, side)
            number = (other * FACES + face) * 4 + flip * 2 + side_bit
            noted = jnp.where(lanes == column, number.astype(F32), noted)
    table = 2 * cycles * layout.stride
    scratch[table : table + 1] = noted
    packed = scratch[...].astype(BF16)
    for member in range(out_ref.shape[0]):
        out_ref[member] = packed


def encode(tiles, x_ref, near_ref, w_ref, b_ref, skip_ref, pre_row_ref, pre_col_ref, stacked):
    height, cols = x_ref.shape[1:3]
    odd = lax.rem(strip_of(tiles), 2)
    stack_taps(stacked, halo_rows(x_ref, near_ref[0], odd, height), height)
    chunk = 4
    for first in range(0, height, chunk):
        lhs = stacked[first : first + chunk].reshape(chunk * cols, stacked.shape[2])
        total = shifted_sum(column_taps(lhs, w_ref), cols) + b_ref[...]
        skip_ref[0, first : first + chunk] = gelu(total).astype(BF16).reshape(chunk, cols, -1)
        for row in range(chunk):
            at = row * cols
            pre_col_ref[0, 0, first + row : first + row + 1] = total[at : at + 1]
            pre_col_ref[0, 1, first + row : first + row + 1] = total[at + cols - 1 : at + cols]
        if first == 0:
            @pl.when(odd == 0)
            def _():
                pre_row_ref[0] = total[:cols]
        if first + chunk == height:
            @pl.when(odd == 1)
            def _():
                pre_row_ref[0] = total[(chunk - 1) * cols :]


def mend(layout, recv_ref, far_ref, w_ref, b_ref, skip_ref, pre_row_ref, pre_col_ref, tile_ref, code_ref,
         out_ref, pooled_ref, near_out, far_out):
    tiles, height = layout.tiles, layout.height
    cycles, _, cols, chans = skip_ref.shape
    strip = strip_of(tiles)
    odd = lax.rem(strip, 2)
    ends = (strip == 0) | (strip == layout.strips - 1)
    row_iota = rows_iota(16) - 1
    targets = []
    for side in range(2):
        for cycle in range(cycles):
            other, face, side_bit, flip = seam_of(tile_ref, code_ref, tiles, cycle, side)
            place = layout.source(strip, flip, face, other * 2 + side_bit, row_iota)
            targets.append(jnp.where(row_iota <= height, place, -1))
    pads = pick(targets, recv_ref[...])
    half = pads.shape[0] // 2
    seams = [
        [dot(pads[side * half : (side + 1) * half], w_ref[tap, 2 * side]) for tap in range(3)]
        for side in range(2)
    ]
    far_at = jnp.where(odd == 1, height - 1, 0)
    far_tap = jnp.where(odd == 1, 2, 0)
    far = far_ref[...].reshape(cycles * cols, chans)
    far = jnp.where(ends, jnp.zeros_like(far), far)
    far_sum = shifted_sum([dot(far, w_ref[far_tap, tap]) for tap in range(3)], cols)
    iota8 = lax.broadcasted_iota(jnp.int32, (height, chans), 0)
    iota16 = lax.broadcasted_iota(jnp.int32, (16, chans), 0)
    for cycle in range(cycles):
        extra = far_sum[cycle * cols : (cycle + 1) * cols]
        out_ref[cycle] = skip_ref[cycle]
        out_ref[cycle, far_at] = gelu(pre_row_ref[cycle] + extra).astype(BF16)
        for side in range(2):
            total = pre_col_ref[cycle, side] + column_sum(seams[side], cycle, height)
            corner = extra[:1] if side == 0 else extra[cols - 1 :]
            total = gelu(total + jnp.where(iota8 == far_at, corner, 0.0))
            first, at = (0, 0) if side == 0 else (cols - 16, 15)
            for row in range(height):
                block = out_ref[cycle, row, first : first + 16].astype(F32)
                block = jnp.where(iota16 == at, total[row : row + 1], block)
                out_ref[cycle, row, first : first + 16] = block.astype(BF16)
    fine = lax.broadcasted_iota(jnp.int32, (cols // 2, 2 * cols), 1) & (cols - 1)
    coarse = lax.broadcasted_iota(jnp.int32, (cols // 2, 2 * cols), 0)
    mean = jnp.where(lax.shift_right_logical(fine, 1) == coarse, 0.25, 0.0).astype(BF16)
    for cycle in range(cycles):
        for row in range(height // 2):
            pair = out_ref[cycle, 2 * row : 2 * row + 2].reshape(2 * cols, chans)
            pooled_ref[cycle, row] = dot(mean, pair).astype(BF16)
    low = height // 2 - 1
    for cycle in range(cycles):
        for ref, at_top in ((near_out, odd == 1), (far_out, odd == 0)):
            ref[cycle, :cols] = out_ref[cycle, jnp.where(at_top, 0, height - 1)]
            ref[cycle, cols : cols + cols // 2] = pooled_ref[cycle, jnp.where(at_top, 0, low)]
            ref[cycle, cols + cols // 2 :] = pooled_ref[cycle, jnp.where(at_top, 1, low - 1)]


def pack_skip(coarse, fine, left_ref, right_ref, pooled_ref, near_ref, far_ref, out_ref, scratch):
    cycles = near_ref.shape[0]
    cols = near_ref.shape[1] // 2
    half = cols // 2
    scratch[...] = jnp.zeros_like(scratch)
    halos = [near_ref] if coarse.joint else [near_ref, far_ref]

    def block(ref, at):
        first = at // 16 * 16
        return ref[first : first + 16].astype(F32)[at - first : at - first + 1]

    for cycle in range(cycles):
        for side in range(2):
            for depth in range(2):
                at = depth if side == 0 else half - 1 - depth
                start = coarse.base + ((cycle * 2 + side) * 2 + depth) * coarse.stride
                for row in range(coarse.height):
                    scratch[start + row : start + row + 1] = block(pooled_ref.at[cycle, row], at)
                for k, halo in enumerate(halos):
                    for away in range(2):
                        put = start + coarse.height + 2 * k + away
                        scratch[put : put + 1] = block(halo.at[cycle], cols + away * half + at)
            start = fine.base + (cycle * 2 + side) * fine.stride
            ref, at = (left_ref, 0) if side == 0 else (right_ref, 15)
            for row in range(fine.height):
                scratch[start + row : start + row + 1] = block(ref.at[cycle, row], at)
            for k, halo in enumerate(halos):
                put = start + fine.height + k
                scratch[put : put + 1] = block(halo.at[cycle], 0 if side == 0 else cols - 1)
    packed = scratch[...].astype(BF16)
    for member in range(out_ref.shape[0]):
        out_ref[member] = packed


def decode_skip(tiles, x_ref, near_ref, w_ref, out_ref, stacked):
    height, cols = x_ref.shape[1:3]
    odd = lax.rem(strip_of(tiles), 2)
    near = near_ref[0, :cols]
    stack_taps(stacked, halo_rows(x_ref, near, odd, height), height)
    chunk = 4
    for first in range(0, height, chunk):
        lhs = stacked[first : first + chunk].reshape(chunk * cols, stacked.shape[2])
        total = shifted_sum(column_taps(lhs, w_ref), cols)
        out_ref[0, first : first + chunk] = total.reshape(chunk, cols, -1)


def decode(coarse_at, fine_at, tab_ref, tile_ref, code_ref, recv_ref, pre_ref, pooled_ref, near_ref, far_ref,
           wm_ref, bm_ref, u_ref, bu_ref, wd_ref, bd_ref, out_ref,
           pooled_pads, fine_sums, stacked, upper, joined):
    tiles, strips = coarse_at.tiles, coarse_at.strips
    height, cols, chans = out_ref.shape[1:]
    low, half = height // 2, cols // 2
    cycle_now = pl.program_id(0)
    cycles = 3
    strip = strip_of(tiles)
    odd = lax.rem(strip, 2)
    first_strip, last_strip = strip == 0, strip == strips - 1
    ends = first_strip | last_strip

    @pl.when(cycle_now == 0)
    def _():
        rows8 = rows_iota(8) - 2
        rows16 = rows_iota(16) - 1
        aligned, taps, skips, sides, flips, strips_at = [], [[], [], []], [], [], [], []
        for side in range(2):
            for cycle in range(cycles):
                other, face, side_bit, flip = seam_of(tile_ref, code_ref, tiles, cycle, side)
                column = other * 2 + side_bit
                aligned.append(coarse_at.source(strip, flip, face, column * 2, rows8))
                place = fine_at.source(strip, flip, face, column, rows16)
                skips.append(jnp.where(rows16 <= height, place, -1))
                there = jnp.where(flip == 1, strips - 1 - strip, strip)
                number = tab_ref[face * 2, column]
                beyond = lax.div(number, 4)
                code = lax.rem(number, 4)
                other2, face2 = lax.div(beyond, FACES), lax.rem(beyond, FACES)
                column2 = other2 * 2 + lax.rem(code, 2)
                pad = coarse_at.source(there, lax.div(code, 2), face2, column2 * 2, rows8)
                edge = coarse_at.source(there, 0, face, column * 2, rows8)
                inner = coarse_at.source(there, 0, face, column * 2 + 1, rows8)
                taps[0].append(jnp.where(side_bit == 0, pad, inner))
                taps[1].append(edge)
                taps[2].append(jnp.where(side_bit == 0, inner, pad))
                sides.append(side_bit)
                flips.append(flip)
                strips_at.append(there)
        got = pick(aligned + taps[0] + taps[1] + taps[2] + skips, recv_ref[...])
        n = 8 * 2 * cycles
        own = got[:n]
        for side in range(2):
            part = own[side * n // 2 : (side + 1) * n // 2]
            sums = [dot(part, wm_ref[tap, 2 * side]) for tap in range(3)]
            for cycle in range(cycles):
                at = cycle * 8
                total = sum(sums[tap][at + tap : at + tap + 6] for tap in range(3))
                pooled_pads[cycle, side, 0:6] = total
        there = got[n : 4 * n]
        rows = [
            sum(dot(there[tap * n : (tap + 1) * n], wm_ref[row, tap]) for tap in range(3))
            for row in range(3)
        ]
        total = pltpu.roll(rows[0], 1, 0) + rows[1] + pltpu.roll(rows[2], n - 1, 0)
        at8 = lax.broadcasted_iota(jnp.int32, (8, chans), 0) - 2
        keep = jnp.concatenate(
            [
                jnp.where(((at8 < 0) & (s == 0)) | ((at8 >= low) & (s == strips - 1)), 0.0, 1.0)
                for s in strips_at
            ],
            axis=0,
        )
        right = jnp.concatenate([jnp.where(at8 > -99, b, 0) for b in sides], axis=0) == 1
        column = (gelu(total + bm_ref[...]) * keep).astype(BF16)
        phases = []
        for a in range(2):
            both = [dot(column, u_ref[a, b]) for b in range(2)]
            value = (jnp.where(right, both[1], both[0]) + bu_ref[...]) * keep
            phases.append(value.astype(BF16))
        places = []
        for k in range(2 * cycles):
            fine = jnp.where(flips[k] == 1, height - 1 - rows16, rows16)
            a = fine & 1
            place = a * n + k * 8 + lax.shift_right_arithmetic(fine - a, 1) + 2
            places.append(jnp.where(rows16 <= height, place, -1))
        column = pick(places, jnp.concatenate(phases, axis=0))
        skip_column = got[4 * n :]
        half_rows = 16 * cycles
        for side in range(2):
            part = slice(side * half_rows, (side + 1) * half_rows)
            sums = [
                dot(column[part], wd_ref[tap, 2 * side, :chans])
                + dot(skip_column[part], wd_ref[tap, 2 * side, chans:])
                for tap in range(3)
            ]
            for cycle in range(cycles):
                fine_sums[cycle, side] = column_sum(sums, cycle, height)

    near, far = near_ref[0], far_ref[0]
    far = jnp.where(ends, jnp.zeros_like(far), far)
    top = jnp.where(odd == 1, near, far)
    bottom = jnp.where(odd == 1, far, near)

    def pooled_row(row):
        if row < -1:
            return top[cols + half :]
        if row < 0:
            return top[cols : cols + half]
        if row < low:
            return pooled_ref[0, row]
        if row == low:
            return bottom[cols : cols + half]
        return bottom[cols + half :]

    stack_taps(upper, lambda row: pooled_row(row - 1), low + 2)
    lhs = upper[...].reshape((low + 2) * half, 3 * chans)
    total = shifted_sum(column_taps(lhs, wm_ref), half)
    total = total.reshape(low + 2, half, chans)
    place = lax.broadcasted_iota(jnp.int32, (half, chans), 0)
    rows = []
    for row in range(low + 2):
        value = total[row] + bm_ref[...]
        value = value + jnp.where(place == 0, pooled_pads[cycle_now, 0, row : row + 1], 0.0)
        value = value + jnp.where(place == half - 1, pooled_pads[cycle_now, 1, row : row + 1], 0.0)
        value = gelu(value)
        if row == 0:
            value = jnp.where(first_strip, 0.0, value)
        if row == low + 1:
            value = jnp.where(last_strip, 0.0, value)
        rows.append(value.astype(BF16))
    for a in range(2):
        part = jnp.concatenate(rows[1:] if a == 0 else rows[:-1], axis=0)
        for b in range(2):
            value = dot(part, u_ref[a, b]) + bu_ref[...]
            for k in range(low + 1):
                at = 2 * k + 1 - a
                for lane in range(0, chans, 128):
                    part_of = value[k * half : (k + 1) * half, lane : lane + 128]
                    joined[at, lane // 128, pl.ds(b, half, 2), :] = part_of

    def fine_row(row):
        value = jnp.concatenate([joined[row + 1, k] for k in range(chans // 128)], axis=1)
        if row < 0:
            value = jnp.where(first_strip, 0.0, value)
        if row >= height:
            value = jnp.where(last_strip, 0.0, value)
        return value.astype(BF16)

    stack_taps(stacked, fine_row, height)
    far_at = jnp.where(odd == 1, height - 1, 0)
    far_tap = jnp.where(odd == 1, 2, 0)
    extra = shifted_sum([dot(far[:cols], wd_ref[far_tap, tap, chans:]) for tap in range(3)], cols)
    pre_ref[0, far_at] = pre_ref[0, far_at] + extra
    edge = lax.broadcasted_iota(jnp.int32, (cols, chans), 0)
    chunk = 4
    for first in range(0, height, chunk):
        lhs = stacked[first : first + chunk].reshape(chunk * cols, 3 * chans)
        weights = [wd_ref[:, tap, :chans].reshape(3 * chans, chans) for tap in range(3)]
        total = shifted_sum([dot(lhs, w) for w in weights], cols)
        total = total.reshape(chunk, cols, chans)
        for row in range(chunk):
            at = first + row
            value = total[row] + pre_ref[0, at] + bd_ref[...]
            value = value + jnp.where(edge == 0, fine_sums[cycle_now, 0, at : at + 1], 0.0)
            value = value + jnp.where(edge == cols - 1, fine_sums[cycle_now, 1, at : at + 1], 0.0)
            out_ref[0, at] = value.astype(BF16)


def whole(shape):
    return pl.BlockSpec(shape, lambda *_: (0,) * len(shape))


def per_cycle(shape):
    return pl.BlockSpec((1,) + shape[1:], lambda c: (c,) + (0,) * (len(shape) - 1))


def smem():
    return pl.BlockSpec(memory_space=pltpu.SMEM)


def params(mib):
    return pltpu.CompilerParams(vmem_limit_bytes=mib * MIB)


def on_device(tiles, fields, seam_tile, seam_code, encoder_weight, encoder_bias, middle_weight,
              middle_bias, upconv_weight, upconv_bias, decoder_weight, decoder_offset_bias):
    cycles, height, cols, chans = fields.shape
    low, half = height // 2, cols // 2
    strips = tiles // FACES
    joint = strips == 4

    def strip(t):
        return (t + strips // 2) % strips

    near_pairs, far_pairs = [], []
    for t in range(tiles):
        pairs = near_pairs if strip(t) % 2 == 0 else far_pairs
        after = (t + 1) % tiles
        pairs += [(t, after), (after, t)]

    def tile_at(face, s):
        return (face * strips + s - strips // 2) % tiles

    groups = [
        [tile_at(face, s) for face in range(FACES) for s in (k, strips - 1 - k)]
        for k in range(strips // 2)
    ]
    members = 2 * FACES

    def share(x):
        return lax.all_to_all(x, "tile", 0, 0, tiled=True, axis_index_groups=groups)

    spec = Layout(tiles, height, 1, 0, 0)
    spec.payload = (2 * cycles * spec.stride + 1 + 15) // 16 * 16
    coarse_at = Layout(tiles, low, 2, 0, 0)
    fine_at = Layout(tiles, height, 1, 4 * cycles * coarse_at.stride, 0)
    payload = (fine_at.base + 2 * cycles * fine_at.stride + 15) // 16 * 16
    coarse_at.payload = fine_at.payload = payload

    odd = strip_of(tiles) % 2 == 1
    top, bottom = fields[:, 0], fields[:, -1]
    near = lax.ppermute(jnp.where(odd, top, bottom), "tile", near_pairs)
    far = lax.ppermute(jnp.where(odd, bottom, top), "tile", far_pairs)
    eb, mb, ub, db = (b.reshape(1, chans) for b in (encoder_bias, middle_bias, upconv_bias, decoder_offset_bias))

    edge = (cycles, height, 16, chans)
    row_shape = (cycles, cols, chans)
    left_edge = pl.BlockSpec(edge, lambda *_: (0, 0, 0, 0))
    right_edge = pl.BlockSpec(edge, lambda *_: (0, 0, cols // 16 - 1, 0))
    packed = pl.pallas_call(
        functools.partial(pack_fields, spec),
        out_shape=jax.ShapeDtypeStruct((members, spec.payload, chans), BF16),
        grid=(1,),
        in_specs=[left_edge, right_edge, whole(row_shape), whole(row_shape), smem(), smem()],
        out_specs=whole((members, spec.payload, chans)),
        scratch_shapes=[pltpu.VMEM((spec.payload, chans), F32)],
        compiler_params=params(16),
        name="pack_fields",
    )(fields, fields, near, near if joint else far, seam_tile, seam_code)
    recv = share(packed)
    table = recv[:, 2 * cycles * spec.stride, : 2 * cycles].astype(jnp.int32)

    tall = (cycles, height, cols, chans)
    wshape = (3, 3, chans, chans)
    conv_cost = pl.CostEstimate(
        flops=2 * cycles * height * cols * 9 * chans * chans, bytes_accessed=8 * MIB, transcendentals=0
    )
    skip, pre_row, pre_col = pl.pallas_call(
        functools.partial(encode, tiles),
        out_shape=[
            jax.ShapeDtypeStruct(tall, BF16),
            jax.ShapeDtypeStruct(row_shape, F32),
            jax.ShapeDtypeStruct((cycles, 2, height, chans), F32),
        ],
        grid=(cycles,),
        in_specs=[per_cycle(tall), per_cycle(row_shape), whole(wshape), whole((1, chans))],
        out_specs=[per_cycle(tall), per_cycle(row_shape), per_cycle((cycles, 2, height, chans))],
        scratch_shapes=[pltpu.VMEM((height, cols, 3 * chans), BF16)],
        compiler_params=params(24),
        cost_estimate=conv_cost,
        name="encode",
    )(fields, near, encoder_weight, eb)

    wide = (cycles, 2 * cols, chans)
    skip, pooled, near_out, far_out = pl.pallas_call(
        functools.partial(mend, spec),
        out_shape=[
            jax.ShapeDtypeStruct(tall, BF16),
            jax.ShapeDtypeStruct((cycles, low, half, chans), BF16),
            jax.ShapeDtypeStruct(wide, BF16),
            jax.ShapeDtypeStruct(wide, BF16),
        ],
        in_specs=[pl.BlockSpec(memory_space=pltpu.VMEM)] * 7 + [smem(), smem()],
        compiler_params=params(24),
        name="mend",
    )(recv.reshape(-1, chans), far, encoder_weight, eb, skip, pre_row, pre_col, seam_tile, seam_code)

    near2 = lax.ppermute(near_out, "tile", near_pairs)
    far2 = lax.ppermute(far_out, "tile", far_pairs)
    packed = pl.pallas_call(
        functools.partial(pack_skip, coarse_at, fine_at),
        out_shape=jax.ShapeDtypeStruct((members, payload, chans), BF16),
        grid=(1,),
        in_specs=[left_edge, right_edge, whole((cycles, low, half, chans)), whole(wide), whole(wide)],
        out_specs=whole((members, payload, chans)),
        scratch_shapes=[pltpu.VMEM((payload, chans), F32)],
        compiler_params=params(16),
        name="pack_skip",
    )(skip, skip, pooled, near2, near2 if joint else far2)
    recv2 = share(packed)

    pre = pl.pallas_call(
        functools.partial(decode_skip, tiles),
        out_shape=jax.ShapeDtypeStruct(tall, F32),
        grid=(cycles,),
        in_specs=[
            per_cycle(tall),
            per_cycle(wide),
            pl.BlockSpec(wshape, lambda c: (0, 0, 1, 0)),
        ],
        out_specs=per_cycle(tall),
        scratch_shapes=[pltpu.VMEM((height, cols, 3 * chans), BF16)],
        compiler_params=params(24),
        cost_estimate=conv_cost,
        name="decode_skip",
    )(skip, near2, decoder_weight)

    return pl.pallas_call(
        functools.partial(decode, coarse_at, fine_at),
        out_shape=jax.ShapeDtypeStruct(tall, BF16),
        grid=(cycles,),
        in_specs=[
            smem(),
            smem(),
            smem(),
            whole((members * payload, chans)),
            per_cycle(tall),
            per_cycle((cycles, low, half, chans)),
            per_cycle(wide),
            per_cycle(wide),
            whole(wshape),
            whole((1, chans)),
            whole((2, 2, chans, chans)),
            whole((1, chans)),
            whole((3, 3, 2 * chans, chans)),
            whole((1, chans)),
        ],
        out_specs=per_cycle(tall),
        scratch_shapes=[
            pltpu.VMEM((cycles, 2, 8, chans), F32),
            pltpu.VMEM((cycles, 2, height, chans), F32),
            pltpu.VMEM((height, cols, 3 * chans), BF16),
            pltpu.VMEM((low + 2, half, 3 * chans), BF16),
            pltpu.VMEM((height + 2, chans // 128, cols, 128), F32),
        ],
        compiler_params=params(40),
        name="decode",
    )(table, seam_tile, seam_code, recv2.reshape(-1, chans), pre, pooled, near2, far2,
      middle_weight, mb, upconv_weight, ub, decoder_weight, db)


def solution(mesh):
    return jax.shard_map(
        functools.partial(on_device, mesh.shape["tile"]),
        mesh=mesh,
        in_specs=(P("grp", "tile", None, None), P(None, "tile", None), P(None, "tile", None)) + (P(),) * 8,
        out_specs=P("grp", "tile", None, None),
        check_vma=False,
    )
```

time: 165 us -> 76 us (0.46)
  blocking collectives: 65.3 us -> 0 us
  matrix products: 50.2 us -> 0 us
  Pallas kernels: 0 us -> 27.1 us
  starting transfers between devices: 5.01 us -> 17.6 us
  other arithmetic: 12.4 us -> 1.74 us
  waiting for transfers between devices: 10.8 us -> 8.84 us
    all_gather x3 -> x0, blocking collectives: 65.3 us -> none  [the longest x2 43.8 us: on_device(): lax.all_gather(boundary_columns(extended)[:, None], 'tile', axis=1, tiled...]
    dot_general x31 -> x0, matrix products: 50.2 us -> none  [the longest x27 49.1 us: convolve(): jnp.dot(window.reshape(-1, chans_in), weight[row_tap, col_tap], preferred...]
    pallas_call x0 -> x6, Pallas kernels: none -> 27.1 us  [the longest x1 11.2 us: on_device(): pl.pallas_call(functools.partial(decode, coarse_at, fine_at), out_shape=j...]
    unnamed x26 -> x46, local copies, waits for them, and re-layouts: 2.39 us -> 19.8 us
    all_to_all x0 -> x2, starting transfers between devices: none -> 16.3 us  [share(): return lax.all_to_all(x, 'tile', 0, 0, tiled=True, axis_index_groups=groups)]
    reshape x4 -> x0, local copies, waits for them, and re-layouts: 6.49 us -> none  [the longest x3 3.5 us: flatten_gathered(): return gathered.reshape((-1,) + gathered.shape[2:])]
    concatenate x3 -> x0, other arithmetic: 4.9 us -> none  [attach_columns(): return jnp.concatenate([left_col, extended, right_col], axis=-2)]
    reduce_sum x1 -> x0, other arithmetic: 4.28 us -> none  [coarsen_grid(): return jnp.mean(values, axis=(-4, -2)).astype(jnp.bfloat16)]
  transfers between devices with their start and end apart: 6 -> 6, of which waited for: 3 -> 2; matrix products, arithmetic and copies ran while one was open for 10% -> 2% of each run, Pallas kernels for 0% -> 14%
where the time goes in v1:
time: 76 us; the launch traced here: 75.2 us
  Pallas kernels  27.1 us (36%)
  local copies, waits for them, and re-layouts  19.8 us (26%)
  starting transfers between devices  17.6 us (23%)
  waiting for transfers between devices  8.84 us (12%)
  other arithmetic  1.74 us (2%)
    unnamed x46, local copies, waits for them, and re-layouts  19.8 us
    all_to_all x2, starting transfers between devices, share(): return lax.all_to_all(x, 'tile', 0, 0, tiled=True, axis_index_groups=groups)  16.3 us
    pallas_call x1, Pallas kernels, on_device(): pl.pallas_call(functools.partial(decode, coarse_at, fine_at), out_shape=j...  11.2 us
    ppermute x1, waiting for transfers between devices, on_device(): far2 = lax.ppermute(far_out, 'tile', far_pairs)  7.23 us
    pallas_call x1, Pallas kernels, on_device(): pl.pallas_call(functools.partial(encode, tiles), out_shape=[jax.ShapeDtyp...  6.54 us
    pallas_call x1, Pallas kernels, on_device(): pl.pallas_call(functools.partial(decode_skip, tiles), out_shape=jax.Shape...  4.31 us
    pallas_call x1, Pallas kernels, on_device(): pl.pallas_call(functools.partial(mend, spec), out_shape=[jax.ShapeDtypeSt...  2.76 us
    select_n x1, other arithmetic, on_device(): far = lax.ppermute(jnp.where(odd, bottom, top), 'tile', far_pairs)  1.73 us
  transfers between devices with their start and end apart: 6, of which 2 were waited for; matrix products, arithmetic and copies ran while one was open for 2% of the time, Pallas kernels for 14%

profile of v1, /device:TPU:1, one launch (start us, length us, event | category | flops | bytes accessed | tf_op | source)
XLA Modules:
  0.0 75.2 jit_solution(12349092473204174976)
XLA Ops:
  0.0 1.7 %fusion.1 = (bf16[3,128,256]{2,1,0:T(8,128)(2,1)}, bf16[3,128,256]{2,1,0:T(8,128)(2,1)S(1)}) fusion(pred[]{:T(512)S(6)} %eq.5, bf16[3,8,128,256]{3,2,1,0:T(8,128)(2,1)} %x_ref.1), kind=kLoop, calls=%fused_computation.3 | loop fusion | flops 196608 | bytes 786433 | tf_op jit(solution)/shard_map/jit(_where)/select_n | solution.py:502
  1.7 0.1 collective-permute-start
  1.8 0.8 %copy.14.tile_ref = s32[3,1,2]{2,1,0:T(1,128)S(1)} copy(s32[3,1,2]{0,2,1:T(2,128)} %param.12) | data formatting | bytes 48 | tf_op args[1]
  2.6 0.8 %copy.15.code_ref = s32[3,1,2]{2,1,0:T(1,128)S(1)} copy(s32[3,1,2]{0,2,1:T(2,128)} %param.13) | data formatting | bytes 48 | tf_op args[2]
  3.3 0.0 collective-permute-done.near_ref.far_ref
  3.3 0.0 copy-start
  3.3 1.4 %copy-done = bf16[3,8,128,256]{3,2,1,0:T(8,128)(2,1)S(1)} copy-done((bf16[3,8,128,256]{3,2,1,0:T(8,128)(2,1)S(1)}, bf16[3,8,128,256]{3,2,1,0:T(8,128)(2,1)}, u32[]{:S(2)}) %copy-start) | copy-done | bytes 1572888
  4.7 0.0 copy-start.1
  4.7 0.0 copy-start.9
  4.7 0.0 copy-start.18
  4.7 1.4 %pack_fields.1 = bf16[8,64,256]{2,1,0:T(8,128)(2,1)} custom-call(bf16[3,8,128,256]{3,2,1,0:T(8,128)(2,1)S(1)} %copy-done, bf16[3,8,128,256]{3,2,1,0:T(8,128)(2,1)S(1)} %copy-done, bf16[3,128,256]{2,1,0:T(8,128)(2,1)S(1)} %collective-permute-done.near_ref.far_ref, bf16[3,128,256]{2,1,0:T(8,128)(2,1)S(1)} %collective-permute-done.near_ref.far_ref, ...), custom_call_target="tpu_custom_call" | custom-call | tf_op jit(solution)/shard_map/pack_fields/pallas_call | solution.py:509
  6.1 8.9 %all-to-all-start = ((bf16[8,64,256]{2,1,0:T(8,128)(2,1)}), bf16[8,64,256]{2,1,0:T(8,128)(2,1)S(1)}, u32[]{:S(2)}, u32[]{:S(2)}) async-start(bf16[8,64,256]{2,1,0:T(8,128)(2,1)} %pack_fields.1), calls=%async_computation | async-start | bytes 524288 | tf_op jit(solution)/shard_map/all_to_all | solution.py:490
  15.0 0.6 collective-permute-start.1
  15.6 0.0 copy-done.1
  15.6 0.0 copy-done.9
  15.6 0.0 copy-done.18
  15.6 6.5 %encode.1 = (bf16[3,8,128,256]{3,2,1,0:T(8,128)(2,1)S(1)}, f32[3,128,256]{2,1,0:T(8,128)S(1)}, f32[3,2,8,256]{3,2,1,0:T(8,128)S(1)}) custom-call(bf16[3,8,128,256]{3,2,1,0:T(8,128)(2,1)S(1)} %copy-done.1, bf16[3,128,256]{2,1,0:T(8,128)(2,1)S(1)} %collective-permute-done.near_ref.far_ref, bf16[3,3,256,256]{3,2,1,0:T(8,128)(2,1)S(1)} %copy-done.9, ...), custom_call_target="tpu_custom_call" | custom-call | flops 3623878656 | bytes 8388608 | tf_op jit(solution)/shard_map/encode/pallas_call | solution.py:527
  22.1 0.0 copy-start.6
  22.1 1.1 %copy-done.6 = bf16[3,8,128,256]{3,2,1,0:T(8,128)(2,1)} copy-done((bf16[3,8,128,256]{3,2,1,0:T(8,128)(2,1)}, bf16[3,8,128,256]{3,2,1,0:T(8,128)(2,1)S(1)}, u32[]{:S(2)}) %copy-start.6) | copy-done | bytes 1572888
  23.3 0.0 copy-start.14
  23.3 0.8 %copy-done.14 = f32[3,128,256]{2,1,0:T(8,128)} copy-done((f32[3,128,256]{2,1,0:T(8,128)}, f32[3,128,256]{2,1,0:T(8,128)S(1)}, u32[]{:S(2)}) %copy-start.14) | copy-done | bytes 393240
  24.0 0.0 copy-start.16
  24.0 0.6 copy-done.16
  24.6 0.0 collective-permute-done.1.far_ref
  24.6 0.0 all-to-all-done
  24.6 0.0 copy-start.7
  24.7 1.4 %copy-done.7 = bf16[3,8,128,256]{3,2,1,0:T(8,128)(2,1)S(1)} copy-done((bf16[3,8,128,256]{3,2,1,0:T(8,128)(2,1)S(1)}, bf16[3,8,128,256]{3,2,1,0:T(8,128)(2,1)}, u32[]{:S(2)}) %copy-start.7) | copy-done | bytes 1572888
  26.1 0.0 copy-start.10
  26.1 1.3 %copy-done.10 = bf16[3,3,256,256]{3,2,1,0:T(8,128)(2,1)S(1)} copy-done((bf16[3,3,256,256]{3,2,1,0:T(8,128)(2,1)S(1)}, bf16[3,3,256,256]{3,2,1,0:T(8,128)(2,1)}, u32[]{:S(2)}) %copy-start.10) | copy-done | bytes 1179672
  27.3 0.0 copy-start.15
  27.3 1.0 %copy-done.15 = f32[3,128,256]{2,1,0:T(8,128)S(1)} copy-done((f32[3,128,256]{2,1,0:T(8,128)S(1)}, f32[3,128,256]{2,1,0:T(8,128)}, u32[]{:S(2)}) %copy-start.15) | copy-done | bytes 393240
  28.3 0.0 copy-start.17
  28.3 0.8 %copy-done.17 = f32[3,2,8,256]{3,2,1,0:T(8,128)S(1)} copy-done((f32[3,2,8,256]{3,2,1,0:T(8,128)S(1)}, f32[3,2,8,256]{3,2,1,0:T(8,128)}, u32[]{:S(2)}) %copy-start.17) | copy-done | bytes 49176
  29.1 2.8 %mend.1 = (bf16[3,8,128,256]{3,2,1,0:T(8,128)(2,1)S(1)}, bf16[3,4,64,256]{3,2,1,0:T(8,128)(2,1)S(1)}, bf16[3,256,256]{2,1,0:T(8,128)(2,1)S(1)}, bf16[3,256,256]{2,1,0:T(8,128)(2,1)}) custom-call(bf16[512,256]{1,0:T(8,128)(2,1)S(1)} %bitcast.22, bf16[3,128,256]{2,1,0:T(8,128)(2,1)S(1)} %collective-permute-done.1.far_ref, ...), custom_call_target="tpu_custom_call" | custom-call | tf_op jit(solution)/shard_map/mend/pallas_call | solution.py:544
  31.9 0.1 collective-permute-start.2
  32.0 1.6 %collective-permute-done.2.near_ref.far_ref = bf16[3,256,256]{2,1,0:T(8,128)(2,1)S(1)} collective-permute-done((bf16[3,256,256]{2,1,0:T(8,128)(2,1)S(1)}, bf16[3,256,256]{2,1,0:T(8,128)(2,1)S(1)}, u32[]{:S(2)}, u32[]{:S(2)}) %collective-permute-start.2) | collective-permute-done | bytes 393248 | tf_op jit(solution)/shard_map/ppermute | solution.py:557
  33.6 0.9 %pack_skip.1 = bf16[8,128,256]{2,1,0:T(8,128)(2,1)} custom-call(bf16[3,8,128,256]{3,2,1,0:T(8,128)(2,1)S(1)} %get-tuple-element.15.left_ref.right_ref.x_ref, bf16[3,8,128,256]{3,2,1,0:T(8,128)(2,1)S(1)} %get-tuple-element.15.left_ref.right_ref.x_ref, bf16[3,4,64,256]{3,2,1,0:T(8,128)(2,1)S(1)} %get-tuple-element.16.pooled_ref, ...), custom_call_target="tpu_custom_call" | custom-call | tf_op jit(solution)/shard_map/pack_skip/pallas_call | solution.py:559
  34.5 7.4 %all-to-all-start.1 = ((bf16[8,128,256]{2,1,0:T(8,128)(2,1)}), bf16[8,128,256]{2,1,0:T(8,128)(2,1)S(1)}, u32[]{:S(2)}, u32[]{:S(2)}) async-start(bf16[8,128,256]{2,1,0:T(8,128)(2,1)} %pack_skip.1), calls=%async_computation.1 | async-start | bytes 1048576 | tf_op jit(solution)/shard_map/all_to_all | solution.py:490
  42.0 0.6 collective-permute-start.3
  42.5 0.0 copy-start.4
  42.6 1.7 %copy-done.4 = bf16[3,3,512,256]{3,2,1,0:T(8,128)(2,1)S(1)} copy-done((bf16[3,3,512,256]{3,2,1,0:T(8,128)(2,1)S(1)}, bf16[3,3,512,256]{3,2,1,0:T(8,128)(2,1)}, u32[]{:S(2)}) %copy-start.4) | copy-done | bytes 2359320
  44.2 0.0 copy-start.11
  44.2 0.0 copy-start.19
  44.2 0.0 copy-start.20
  44.2 0.0 copy-start.21
  44.2 4.3 %decode_skip.1.pre_ref = f32[3,8,128,256]{3,2,1,0:T(8,128)S(1)} custom-call(bf16[3,8,128,256]{3,2,1,0:T(8,128)(2,1)S(1)} %get-tuple-element.15.left_ref.right_ref.x_ref, bf16[3,256,256]{2,1,0:T(8,128)(2,1)S(1)} %collective-permute-done.2.near_ref.far_ref, bf16[3,3,512,256]{3,2,1,0:T(8,128)(2,1)S(1)} %copy-done.4), custom_call_target="tpu_custom_call" | custom-call | flops 3623878656 | bytes 8388608 | tf_op jit(solution)/shard_map/decode_skip/pallas_call | solution.py:571
  48.5 0.0 copy-start.2
  48.6 1.6 %copy-done.2 = f32[3,8,128,256]{3,2,1,0:T(8,128)} copy-done((f32[3,8,128,256]{3,2,1,0:T(8,128)}, f32[3,8,128,256]{3,2,1,0:T(8,128)S(1)}, u32[]{:S(2)}) %copy-start.2) | copy-done | bytes 3145752
  50.2 7.2 %collective-permute-done.3.far_ref = bf16[3,256,256]{2,1,0:T(8,128)(2,1)S(1)} collective-permute-done((bf16[3,256,256]{2,1,0:T(8,128)(2,1)}, bf16[3,256,256]{2,1,0:T(8,128)(2,1)S(1)}, u32[]{:S(2)}, u32[]{:S(2)}) %collective-permute-start.3) | collective-permute-done | bytes 393248 | tf_op jit(solution)/shard_map/ppermute | solution.py:558
  57.4 0.0 copy-start.12
  57.4 0.7 copy-done.12
  58.2 0.0 all-to-all-done.1
  58.2 0.0 copy-done.11
  58.2 0.0 copy-done.19
  58.2 0.0 copy-done.20
  58.2 0.0 copy-done.21
  58.2 0.0 copy-start.3
  58.2 1.9 %copy-done.3 = f32[3,8,128,256]{3,2,1,0:T(8,128)S(1)} copy-done((f32[3,8,128,256]{3,2,1,0:T(8,128)S(1)}, f32[3,8,128,256]{3,2,1,0:T(8,128)}, u32[]{:S(2)}) %copy-start.3) | copy-done | bytes 3145752
  60.1 1.7 %copy-done.5 = bf16[3,3,512,256]{3,2,1,0:T(8,128)(2,1)S(1)} copy-done((bf16[3,3,512,256]{3,2,1,0:T(8,128)(2,1)S(1)}, bf16[3,3,512,256]{3,2,1,0:T(8,128)(2,1)}, u32[]{:S(2)}) %copy-start.5) | copy-done | bytes 2359320
  61.7 0.0 copy-start.8
  61.7 1.3 %copy-done.8 = bf16[3,3,256,256]{3,2,1,0:T(8,128)(2,1)S(1)} copy-done((bf16[3,3,256,256]{3,2,1,0:T(8,128)(2,1)S(1)}, bf16[3,3,256,256]{3,2,1,0:T(8,128)(2,1)}, u32[]{:S(2)}) %copy-start.8) | copy-done | bytes 1179672
  63.0 0.0 copy-start.13
  63.0 1.0 %copy-done.13 = bf16[3,256,256]{2,1,0:T(8,128)(2,1)S(1)} copy-done((bf16[3,256,256]{2,1,0:T(8,128)(2,1)S(1)}, bf16[3,256,256]{2,1,0:T(8,128)(2,1)}, u32[]{:S(2)}) %copy-start.13) | copy-done | bytes 393240
  64.0 11.2 %decode.1 = bf16[3,8,128,256]{3,2,1,0:T(8,128)(2,1)} custom-call(s32[8,6]{1,0:T(8,128)S(1)} %bitcast.23, s32[3,1,2]{2,1,0:T(1,128)S(1)} %copy.14.tile_ref, s32[3,1,2]{2,1,0:T(1,128)S(1)} %copy.15.code_ref, bf16[1024,256]{1,0:T(8,128)(2,1)S(1)} %bitcast.21, f32[3,8,128,256]{3,2,1,0:T(8,128)S(1)} %copy-done.3, ...), custom_call_target="tpu_custom_call" | custom-call | tf_op jit(solution)/shard_map/decode/pallas_call | solution.py:587
  (2 shorter events, 0.0 us)
Async XLA Ops:
  1.7 1.6 %collective-permute-start = (bf16[3,128,256]{2,1,0:T(8,128)(2,1)S(1)}, bf16[3,128,256]{2,1,0:T(8,128)(2,1)S(1)}, u32[]{:S(2)}, u32[]{:S(2)}) collective-permute-start(bf16[3,128,256]{2,1,0:T(8,128)(2,1)S(1)} %get-tuple-element.20), channel_id=1, source_target_pairs={{0,1},{1,0},{2,3},{3,2},{4,5},{5,4},{6,7},{7,6},{8,9},{9,8},{10,11... | collective-permute-start | bytes 589832 | tf_op jit(solution)/shard_map/ppermute | solution.py:501
  3.3 1.4 %copy-start = (bf16[3,8,128,256]{3,2,1,0:T(8,128)(2,1)S(1)}, bf16[3,8,128,256]{3,2,1,0:T(8,128)(2,1)}, u32[]{:S(2)}) copy-start(bf16[3,8,128,256]{3,2,1,0:T(8,128)(2,1)} %x_ref.1) | copy-start | bytes 4718596
  4.7 10.8 %copy-start.1 = (bf16[3,8,128,256]{3,2,1,0:T(8,128)(2,1)S(1)}, bf16[3,8,128,256]{3,2,1,0:T(8,128)(2,1)}, u32[]{:S(2)}) copy-start(bf16[3,8,128,256]{3,2,1,0:T(8,128)(2,1)} %x_ref.1) | copy-start | bytes 4718596
  4.7 10.8 %copy-start.9 = (bf16[3,3,256,256]{3,2,1,0:T(8,128)(2,1)S(1)}, bf16[3,3,256,256]{3,2,1,0:T(8,128)(2,1)}, u32[]{:S(2)}) copy-start(bf16[3,3,256,256]{3,2,1,0:T(8,128)(2,1)} %w_ref.4) | copy-start | bytes 3538948
  4.7 10.8 %copy-start.18 = (f32[256]{0:T(256)S(1)}, f32[256]{0:T(256)}, u32[]{:S(2)}) copy-start(f32[256]{0:T(256)} %param.15) | copy-start | bytes 3076
  6.1 18.5 %all-to-all-start = ((bf16[8,64,256]{2,1,0:T(8,128)(2,1)}), bf16[8,64,256]{2,1,0:T(8,128)(2,1)S(1)}, u32[]{:S(2)}, u32[]{:S(2)}) async-start(bf16[8,64,256]{2,1,0:T(8,128)(2,1)} %pack_fields.1), calls=%async_computation | async-start | bytes 524288 | tf_op jit(solution)/shard_map/all_to_all | solution.py:490
  15.0 9.6 %collective-permute-start.1 = (bf16[3,128,256]{2,1,0:T(8,128)(2,1)}, bf16[3,128,256]{2,1,0:T(8,128)(2,1)S(1)}, u32[]{:S(2)}, u32[]{:S(2)}) collective-permute-start(bf16[3,128,256]{2,1,0:T(8,128)(2,1)} %get-tuple-element.19), channel_id=1, source_target_pairs={{1,2},{2,1},{3,4},{4,3},{5,6},{6,5},{7,8},{8,7},{9,10},{10,9},{11,... | collective-permute-start | bytes 589832 | tf_op jit(solution)/shard_map/ppermute | solution.py:502
  22.1 1.1 %copy-start.6 = (bf16[3,8,128,256]{3,2,1,0:T(8,128)(2,1)}, bf16[3,8,128,256]{3,2,1,0:T(8,128)(2,1)S(1)}, u32[]{:S(2)}) copy-start(bf16[3,8,128,256]{3,2,1,0:T(8,128)(2,1)S(1)} %get-tuple-element.12.skip_ref) | copy-start | bytes 4718596
  23.3 0.8 %copy-start.14 = (f32[3,128,256]{2,1,0:T(8,128)}, f32[3,128,256]{2,1,0:T(8,128)S(1)}, u32[]{:S(2)}) copy-start(f32[3,128,256]{2,1,0:T(8,128)S(1)} %get-tuple-element.13.pre_row_ref) | copy-start | bytes 1179652
  24.0 0.6 copy-start.16
  24.6 1.4 %copy-start.7 = (bf16[3,8,128,256]{3,2,1,0:T(8,128)(2,1)S(1)}, bf16[3,8,128,256]{3,2,1,0:T(8,128)(2,1)}, u32[]{:S(2)}) copy-start(bf16[3,8,128,256]{3,2,1,0:T(8,128)(2,1)} %copy-done.6) | copy-start | bytes 4718596
  26.1 1.3 %copy-start.10 = (bf16[3,3,256,256]{3,2,1,0:T(8,128)(2,1)S(1)}, bf16[3,3,256,256]{3,2,1,0:T(8,128)(2,1)}, u32[]{:S(2)}) copy-start(bf16[3,3,256,256]{3,2,1,0:T(8,128)(2,1)} %w_ref.4) | copy-start | bytes 3538948
  27.3 1.0 %copy-start.15 = (f32[3,128,256]{2,1,0:T(8,128)S(1)}, f32[3,128,256]{2,1,0:T(8,128)}, u32[]{:S(2)}) copy-start(f32[3,128,256]{2,1,0:T(8,128)} %copy-done.14) | copy-start | bytes 1179652
  28.3 0.8 %copy-start.17 = (f32[3,2,8,256]{3,2,1,0:T(8,128)S(1)}, f32[3,2,8,256]{3,2,1,0:T(8,128)}, u32[]{:S(2)}) copy-start(f32[3,2,8,256]{3,2,1,0:T(8,128)} %copy-done.16) | copy-start | bytes 147460
  31.9 1.7 %collective-permute-start.2 = (bf16[3,256,256]{2,1,0:T(8,128)(2,1)S(1)}, bf16[3,256,256]{2,1,0:T(8,128)(2,1)S(1)}, u32[]{:S(2)}, u32[]{:S(2)}) collective-permute-start(bf16[3,256,256]{2,1,0:T(8,128)(2,1)S(1)} %get-tuple-element.17), channel_id=1, source_target_pairs={{0,1},{1,0},{2,3},{3,2},{4,5},{5,4},{6,7},{7,6},{8,9},{9,8},{10,11... | collective-permute-start | bytes 1179656 | tf_op jit(solution)/shard_map/ppermute | solution.py:557
  34.5 23.6 %all-to-all-start.1 = ((bf16[8,128,256]{2,1,0:T(8,128)(2,1)}), bf16[8,128,256]{2,1,0:T(8,128)(2,1)S(1)}, u32[]{:S(2)}, u32[]{:S(2)}) async-start(bf16[8,128,256]{2,1,0:T(8,128)(2,1)} %pack_skip.1), calls=%async_computation.1 | async-start | bytes 1048576 | tf_op jit(solution)/shard_map/all_to_all | solution.py:490
  42.0 15.5 %collective-permute-start.3 = (bf16[3,256,256]{2,1,0:T(8,128)(2,1)}, bf16[3,256,256]{2,1,0:T(8,128)(2,1)S(1)}, u32[]{:S(2)}, u32[]{:S(2)}) collective-permute-start(bf16[3,256,256]{2,1,0:T(8,128)(2,1)} %get-tuple-element.18), channel_id=1, source_target_pairs={{1,2},{2,1},{3,4},{4,3},{5,6},{6,5},{7,8},{8,7},{9,10},{10,9},{11,... | collective-permute-start | bytes 1179656 | tf_op jit(solution)/shard_map/ppermute | solution.py:558
  42.5 1.7 %copy-start.4 = (bf16[3,3,512,256]{3,2,1,0:T(8,128)(2,1)S(1)}, bf16[3,3,512,256]{3,2,1,0:T(8,128)(2,1)}, u32[]{:S(2)}) copy-start(bf16[3,3,512,256]{3,2,1,0:T(8,128)(2,1)} %wd_ref.1) | copy-start | bytes 7077892
  44.2 13.9 %copy-start.11 = (bf16[2,2,256,256]{3,2,1,0:T(8,128)(2,1)S(1)}, bf16[2,2,256,256]{3,2,1,0:T(8,128)(2,1)}, u32[]{:S(2)}) copy-start(bf16[2,2,256,256]{3,2,1,0:T(8,128)(2,1)} %u_ref.1) | copy-start | bytes 1572868
  44.2 13.9 %copy-start.19 = (f32[256]{0:T(256)S(1)}, f32[256]{0:T(256)}, u32[]{:S(2)}) copy-start(f32[256]{0:T(256)} %param.17) | copy-start | bytes 3076
  44.2 13.9 %copy-start.20 = (f32[256]{0:T(256)S(1)}, f32[256]{0:T(256)}, u32[]{:S(2)}) copy-start(f32[256]{0:T(256)} %param.19) | copy-start | bytes 3076
  44.2 14.0 %copy-start.21 = (f32[256]{0:T(256)S(1)}, f32[256]{0:T(256)}, u32[]{:S(2)}) copy-start(f32[256]{0:T(256)} %param.21) | copy-start | bytes 3076
  48.5 1.6 %copy-start.2 = (f32[3,8,128,256]{3,2,1,0:T(8,128)}, f32[3,8,128,256]{3,2,1,0:T(8,128)S(1)}, u32[]{:S(2)}) copy-start(f32[3,8,128,256]{3,2,1,0:T(8,128)S(1)} %decode_skip.1.pre_ref) | copy-start | bytes 9437188
  57.4 0.7 copy-start.12
  58.2 1.9 %copy-start.3 = (f32[3,8,128,256]{3,2,1,0:T(8,128)S(1)}, f32[3,8,128,256]{3,2,1,0:T(8,128)}, u32[]{:S(2)}) copy-start(f32[3,8,128,256]{3,2,1,0:T(8,128)} %copy-done.2) | copy-start | bytes 9437188
  60.1 1.7 %copy-start.5 = (bf16[3,3,512,256]{3,2,1,0:T(8,128)(2,1)S(1)}, bf16[3,3,512,256]{3,2,1,0:T(8,128)(2,1)}, u32[]{:S(2)}) copy-start(bf16[3,3,512,256]{3,2,1,0:T(8,128)(2,1)} %wd_ref.1) | copy-start | bytes 7077892
  61.7 1.3 %copy-start.8 = (bf16[3,3,256,256]{3,2,1,0:T(8,128)(2,1)S(1)}, bf16[3,3,256,256]{3,2,1,0:T(8,128)(2,1)}, u32[]{:S(2)}) copy-start(bf16[3,3,256,256]{3,2,1,0:T(8,128)(2,1)} %wm_ref.1) | copy-start | bytes 3538948
  63.0 1.0 %copy-start.13 = (bf16[3,256,256]{2,1,0:T(8,128)(2,1)S(1)}, bf16[3,256,256]{2,1,0:T(8,128)(2,1)}, u32[]{:S(2)}) copy-start(bf16[3,256,256]{2,1,0:T(8,128)(2,1)} %copy-done.12) | copy-start | bytes 1179652

commit v2 on v0

v2 whole, which is shorter than its diff:
```python
import functools

import jax
import jax.numpy as jnp
from jax import lax
from jax.experimental import pallas as pl
from jax.experimental.pallas import tpu as pltpu
from jax.sharding import PartitionSpec as P

F32 = jnp.float32
BF16 = jnp.bfloat16
FACES = 4
MIB = 1 << 20


def dot(a, b):
    return jnp.dot(a, b, preferred_element_type=F32)


def gelu(x):
    return 0.5 * x * (1.0 + jnp.tanh(0.7978845608 * (x + 0.044715 * x * x * x)))


def rows_iota(n):
    return lax.broadcasted_iota(jnp.int32, (n, 1), 0)


class Layout:
    def __init__(self, tiles, height, depth, columns, own, near, tail):
        self.tiles = tiles
        self.strips = tiles // FACES
        self.joint = self.strips == 4
        self.height = height
        self.depth = depth
        self.columns = columns
        self.own = own
        self.near = near
        self.far = near + tail
        self.payload = 0

    def source(self, strip, flip, face, column, row):
        height, last = self.height, self.strips - 1
        strip = jnp.where(flip == 1, last - strip, strip)
        row = jnp.where(flip == 1, height - 1 - row, row)
        upper = jnp.where(strip >= self.strips // 2, 1, 0)
        odd = lax.rem(strip, 2)
        above = row < 0
        below = row >= height
        away = jnp.where(above, -row, row - (height - 1)) - 1
        near = (above & (odd == 1)) | (below & (odd == 0))
        missing = (above & (strip == 0)) | (below & (strip == last))
        member = (face * 2 + upper) * self.payload
        inside = member + self.own + column * height + row
        beside = member + self.near + column * self.depth + away
        if self.joint:
            across = (face * 2 + 1 - upper) * self.payload + self.own + column * height
            far = across + jnp.where(above, height - 1 - away, away)
        else:
            far = member + self.far + column * self.depth + away
        place = jnp.where(above | below, jnp.where(near, beside, far), inside)
        return jnp.where(missing, -1, place)


def strip_of(tiles):
    strips = tiles // FACES
    return lax.rem(lax.axis_index("tile") + strips // 2, strips)


def seam_of(tile_ref, code_ref, tiles, cycle, side):
    strips = tiles // FACES
    partner = tile_ref[0, side, cycle]
    code = code_ref[0, side, cycle]
    other = lax.div(partner, tiles)
    place = partner - other * tiles + strips // 2
    face = lax.rem(lax.div(place, strips), FACES)
    return other, face, lax.rem(code, 2), lax.div(code, 2)


def pick(targets, table):
    wanted = jnp.concatenate(targets, axis=0)
    shape = (wanted.shape[0], table.shape[0])
    lanes = lax.broadcasted_iota(jnp.int32, shape, 1)
    chooser = jnp.where(lanes == wanted, 1.0, 0.0).astype(BF16)
    return dot(chooser, table).astype(BF16)


def shifted_sum(taps, cols):
    left, middle, right = taps
    n = middle.shape[0]
    place = lax.broadcasted_iota(jnp.int32, middle.shape, 0) & (cols - 1)
    left = jnp.where(place == 0, 0.0, pltpu.roll(left, 1, 0))
    right = jnp.where(place == cols - 1, 0.0, pltpu.roll(right, n - 1, 0))
    return middle + left + right


def stack_taps(stacked, row_of, rows):
    depth = stacked.shape[-1] // 3
    for row in range(-1, rows + 1):
        value = row_of(row)
        for tap in range(3):
            at = row + 1 - tap
            if 0 <= at < rows:
                stacked[at, :, tap * depth : (tap + 1) * depth] = value


def column_taps(lhs, weight_ref):
    depth = weight_ref.shape[2]
    return [
        dot(lhs, weight_ref[:, tap].reshape(3 * depth, weight_ref.shape[3]))
        for tap in range(3)
    ]


def halo_rows(rows_ref, top, bottom):
    def row_of(row):
        if row < 0:
            return top
        if row >= rows_ref.shape[0]:
            return bottom
        return rows_ref[row]

    return row_of


def top_and_bottom(near, far, odd, ends):
    far = jnp.where(ends, jnp.zeros_like(far), far)
    return jnp.where(odd == 1, near, far), jnp.where(odd == 1, far, near)


def column_sum(parts, cycle, height):
    at = cycle * 16
    return sum(parts[tap][at + tap : at + tap + height] for tap in range(3))


def lift(layout, x_hbm, tile_ref, code_ref, own_hbm, near_tail_hbm, far_tail_hbm, near_hbm, far_hbm,
         edges, rows, own, tails, own16, tails16, in_sems, out_sems):
    height = layout.height
    cycles, cols = x_hbm.shape[0], x_hbm.shape[2]
    upper = lax.rem(strip_of(layout.tiles), 2) * (height - 1)
    nearest = (height - 1 - upper, upper)
    pairs = [(x_hbm.at[:, :, pl.ds(first, 16)], edges.at[side]) for side, first in enumerate((0, cols - 16))]
    arriving = fetch(pairs + [(x_hbm.at[:, nearest[k]], rows.at[k]) for k in range(2)], in_sems)
    lanes = lax.broadcasted_iota(jnp.int32, (1, own.shape[1]), 1)
    noted = jnp.zeros((1, own.shape[1]), F32)
    for cycle in range(cycles):
        for side in range(2):
            other, face, side_bit, flip = seam_of(tile_ref, code_ref, layout.tiles, cycle, side)
            number = (other * FACES + face) * 4 + flip * 2 + side_bit
            noted = jnp.where(lanes == cycle * 2 + side, number.astype(F32), noted)
    tails[...] = jnp.zeros_like(tails)
    for k in range(2):
        tails[k, layout.columns : layout.columns + 1] = noted
    for side in range(2):
        arriving[side].wait()
        at = 15 * side
        for cycle in range(cycles):
            column = cycle * 2 + side
            for row in range(height):
                value = edges[side, cycle, row].astype(F32)[at : at + 1]
                own[column * height + row : column * height + row + 1] = value
            for k in range(2):
                value = edges[side, cycle, nearest[k]].astype(F32)[at : at + 1]
                tails[k, column : column + 1] = value
    own16[...] = own[...].astype(BF16)
    tails16[...] = tails[...].astype(BF16)
    pairs = [(tails16.at[0], near_tail_hbm), (tails16.at[1], far_tail_hbm), (own16, own_hbm)]
    for copy in arriving[2:]:
        copy.wait()
    leaving = fetch(pairs + [(rows.at[0], near_hbm), (rows.at[1], far_hbm)], out_sems)
    for copy in leaving:
        copy.wait()


def fetch(pairs, sems):
    copies = [pltpu.make_async_copy(src, dst, sems.at[k]) for k, (src, dst) in enumerate(pairs)]
    for copy in copies:
        copy.start()
    return copies


def encode(tiles, x_hbm, near_ref, far_ref, w_hbm, b_hbm, skip_hbm, pooled_hbm, near_hbm, far_hbm, pre_hbm,
           x_ref, w_ref, b_ref, stacked, skip_ref, pooled_ref, rows_ref, pre_ref, paired, in_sems, out_sems):
    cycles, height, cols, chans = x_ref.shape
    half = cols // 2
    pairs = [(b_hbm, b_ref), (x_hbm.at[0], x_ref.at[0])]
    pairs += [(w_hbm.at[:, tap], w_ref.at[tap]) for tap in range(3)]
    arriving = fetch(pairs, in_sems.at[pl.ds(0, 5)])
    strip = strip_of(tiles)
    odd = lax.rem(strip, 2)
    ends = (strip == 0) | (strip == tiles // FACES - 1)
    arriving[0].wait()
    arriving[1].wait()
    leaving = []
    for cycle in range(cycles):
        if cycle > 0:
            arriving[4 + cycle].wait()
        top, bottom = top_and_bottom(near_ref[cycle], far_ref[cycle], odd, ends)
        stack_taps(stacked, halo_rows(x_ref.at[cycle], top, bottom), height)
        for row in range(height):
            taps = []
            for tap in range(3):
                if cycle == 0 and row == 0:
                    arriving[2 + tap].wait()
                taps.append(dot(stacked[row], w_ref[tap].reshape(3 * chans, chans)))
            if cycle == 0 and row == 0:
                pairs = [(x_hbm.at[k], x_ref.at[k]) for k in range(1, cycles)]
                arriving += fetch(pairs, in_sems.at[pl.ds(5, cycles - 1)])
            total = shifted_sum(taps, cols) + b_ref[...]
            value = gelu(total).astype(BF16)
            skip_ref[cycle, row] = value
            pre_ref[cycle, 0, row : row + 1] = total[:1]
            pre_ref[cycle, 1, row : row + 1] = total[cols - 1 :]
            if row % 2 == 0:
                before = value.astype(F32)
            else:
                pair = 0.25 * (before + value.astype(F32))
                for lane in range(0, chans, 128):
                    paired[...] = pair[:, lane : lane + 128]
                    mean = paired[pl.ds(0, half, 2), :] + paired[pl.ds(1, half, 2), :]
                    pooled_ref[cycle, row // 2, :, lane : lane + 128] = mean.astype(BF16)
            if row % 4 == 3:
                rows = (cycle, pl.ds(row - 3, 4))
                leaving += fetch([(skip_ref.at[rows], skip_hbm.at[rows])], out_sems.at[cycle, pl.ds(row // 4, 1)])
        low = height // 2 - 1
        for k, at_top in ((0, odd == 1), (1, odd == 0)):
            rows_ref[k, cycle, :cols] = skip_ref[cycle, jnp.where(at_top, 0, height - 1)]
            rows_ref[k, cycle, cols : cols + half] = pooled_ref[cycle, jnp.where(at_top, 0, low)]
            rows_ref[k, cycle, cols + half :] = pooled_ref[cycle, jnp.where(at_top, 1, low - 1)]
        pairs = [(rows_ref.at[0, cycle], near_hbm.at[cycle]), (rows_ref.at[1, cycle], far_hbm.at[cycle])]
        pairs += [(pooled_ref.at[cycle], pooled_hbm.at[cycle]), (pre_ref.at[cycle], pre_hbm.at[cycle])]
        leaving += fetch(pairs, out_sems.at[cycle, pl.ds(height // 4, 4)])
    for copy in leaving:
        copy.wait()


def mend(layout, coarse, fine, recv_ref, w_hbm, skip_in, pooled_in, near_in, far_in, pre_hbm, tile_ref, code_ref,
         skip_hbm, pooled_hbm, near_hbm, far_hbm, own_hbm, near_tail_hbm, far_tail_hbm, table_hbm,
         w_ref, pre_ref, edges, pools, own, tails, own16, tails16, table_ref, in_sems, out_sems):
    tiles, height, low = layout.tiles, layout.height, coarse.height
    cycles, cols, chans = skip_in.shape[0], skip_in.shape[2], skip_in.shape[3]
    half = cols // 2
    pairs = [(w_hbm.at[:, 2 * side], w_ref.at[side]) for side in range(2)] + [(pre_hbm, pre_ref)]
    for side in range(2):
        pairs.append((skip_in.at[:, :, pl.ds((cols - 16) * side, 16)], edges.at[side]))
        pairs.append((pooled_in.at[:, :, pl.ds((half - 16) * side, 16)], pools.at[side]))
    arriving = fetch(pairs, in_sems)
    strip = strip_of(tiles)
    odd = lax.rem(strip, 2)
    row_iota = rows_iota(16) - 1
    targets = []
    for side in range(2):
        for cycle in range(cycles):
            other, face, side_bit, flip = seam_of(tile_ref, code_ref, tiles, cycle, side)
            place = layout.source(strip, flip, face, other * 2 + side_bit, row_iota)
            targets.append(jnp.where(row_iota <= height, place, -1))
    pads = pick(targets, recv_ref[...])
    noted = layout.near + layout.columns
    for member in range(2 * FACES):
        at = member * layout.payload + noted // 16 * 16
        block = recv_ref[at : at + 16, :128].astype(F32)
        table_ref[member : member + 1] = block[noted % 16 : noted % 16 + 1].astype(jnp.int32)
    part = pads.shape[0] // 2
    for copy in arriving[:3]:
        copy.wait()
    seams = [
        [dot(pads[side * part : (side + 1) * part], w_ref[side, tap]) for tap in range(3)] for side in range(2)
    ]
    iota16 = lax.broadcasted_iota(jnp.int32, (16, chans), 0)
    tails[...] = jnp.zeros_like(tails)
    for copy in arriving[3:]:
        copy.wait()
    at_top = (odd == 1, odd == 0)
    skip_at = [jnp.where(t, 0, height - 1) for t in at_top]
    pool_at = [(jnp.where(t, 0, low - 1), jnp.where(t, 1, low - 2)) for t in at_top]
    for cycle in range(cycles):
        for side in range(2):
            column = cycle * 2 + side
            at, inward = (0, 1) if side == 0 else (15, 14)
            total = gelu(pre_ref[cycle, side] + column_sum(seams[side], cycle, height))
            start = fine.own + column * height
            own[start : start + height] = total
            for row in range(height):
                block = edges[side, cycle, row].astype(F32)
                block = jnp.where(iota16 == at, total[row : row + 1], block).astype(BF16)
                edges[side, cycle, row] = block
                if row % 2 == 0:
                    before = block.astype(F32)
                else:
                    pair = before + block.astype(F32)
                    mean = 0.25 * (pair[at : at + 1] + pair[inward : inward + 1])
                    block = pools[side, cycle, row // 2].astype(F32)
                    block = jnp.where(iota16 == at, mean, block)
                    pools[side, cycle, row // 2] = block.astype(BF16)
                    for depth, place in enumerate((at, inward)):
                        start = coarse.own + (column * 2 + depth) * low + row // 2
                        own[start : start + 1] = block[place : place + 1]
            for k in range(2):
                start = fine.near - coarse.near + column
                value = edges[side, cycle, skip_at[k]].astype(F32)
                tails[k, start : start + 1] = value[at : at + 1]
                for away in range(2):
                    value = pools[side, cycle, pool_at[k][away]].astype(F32)
                    for depth, place in enumerate((at, inward)):
                        start = (column * 2 + depth) * 2 + away
                        tails[k, start : start + 1] = value[place : place + 1]
    own16[...] = own[...].astype(BF16)
    tails16[...] = tails[...].astype(BF16)
    pairs = [(tails16.at[0], near_tail_hbm), (own16, own_hbm), (tails16.at[1], far_tail_hbm), (table_ref, table_hbm)]
    for side in range(2):
        pairs.append((edges.at[side], skip_hbm.at[:, :, pl.ds((cols - 16) * side, 16)]))
        pairs.append((pools.at[side], pooled_hbm.at[:, :, pl.ds((half - 16) * side, 16)]))
        for k, ref in enumerate((near_hbm, far_hbm)):
            pairs.append((edges.at[side, :, skip_at[k]], ref.at[:, pl.ds((cols - 16) * side, 16)]))
            for away in range(2):
                first = cols + away * half + (half - 16) * side
                pairs.append((pools.at[side, :, pool_at[k][away]], ref.at[:, pl.ds(first, 16)]))
    leaving = fetch(pairs, out_sems)
    for copy in leaving:
        copy.wait()


def decode(tiles, skip_hbm, pooled_hbm, near_ref, far_ref, wm_hbm, bm_hbm, u_hbm, bu_hbm, wd_hbm, bd_hbm,
           out_hbm, edge_hbm, coarse_hbm, skip_ref, pooled_ref, wm_ref, bm_ref, u_ref, bu_ref, wd_ref,
           bd_ref, out_ref, edge_ref, coarse_ref, stacked, upper, joined, in_sems, out_sems):
    strips = tiles // FACES
    cycles, height, cols, chans = skip_ref.shape
    low, half = height // 2, cols // 2
    pairs = [(bm_hbm, bm_ref), (bu_hbm, bu_ref), (bd_hbm, bd_ref), (pooled_hbm, pooled_ref)]
    pairs += [(wm_hbm, wm_ref), (u_hbm, u_ref), (skip_hbm.at[0], skip_ref.at[0])]
    for tap in range(3):
        for part in range(2):
            source = wd_hbm.at[:, tap, pl.ds(part * chans, chans)]
            pairs.append((source, wd_ref.at[tap, pl.ds(3 * part, 3)]))
    pairs += [(skip_hbm.at[cycle], skip_ref.at[cycle]) for cycle in range(1, cycles)]
    arriving = fetch(pairs, in_sems)
    strip = strip_of(tiles)
    odd = lax.rem(strip, 2)
    first_strip, last_strip = strip == 0, strip == strips - 1
    ends = first_strip | last_strip
    place = lax.broadcasted_iota(jnp.int32, (cols, chans), 0)
    inner = (place > 1) & (place < cols - 2)
    coarse_ref[...] = jnp.zeros_like(coarse_ref)
    chunk = 1
    leaving = []
    for copy in arriving[:4]:
        copy.wait()
    for cycle in range(cycles):
        top, bottom = top_and_bottom(near_ref[cycle], far_ref[cycle], odd, ends)

        def pooled_row(row):
            if row < -1:
                return top[cols + half :]
            if row < 0:
                return top[cols : cols + half]
            if row < low:
                return pooled_ref[cycle, row]
            if row == low:
                return bottom[cols : cols + half]
            return bottom[cols + half :]

        stack_taps(upper, lambda row: pooled_row(row - 1), low + 2)
        lhs = upper[...].reshape((low + 2) * half, 3 * chans)
        if cycle == 0:
            arriving[4].wait()
        total = shifted_sum(column_taps(lhs, wm_ref), half) + bm_ref[...]
        for row in range(low + 2):
            coarse_ref[cycle, 0, row + 1 : row + 2] = total[row * half : row * half + 1]
            coarse_ref[cycle, 1, row + 1 : row + 2] = total[(row + 1) * half - 1 : (row + 1) * half]
        coarse = gelu(total).astype(BF16)
        if cycle == 0:
            arriving[5].wait()
        for a in range(2):
            part = coarse[half:] if a == 0 else coarse[:-half]
            for b in range(2):
                value = dot(part, u_ref[a, b]) + bu_ref[...]
                for k in range(low + 1):
                    at = 2 * k + 1 - a
                    for lane in range(0, chans, 128):
                        part_of = value[k * half : (k + 1) * half, lane : lane + 128]
                        joined[at, lane // 128, pl.ds(b, half, 2), :] = part_of
        arriving[6 if cycle == 0 else 12 + cycle].wait()

        def joined_row(row):
            value = jnp.concatenate([joined[row + 1, k] for k in range(chans // 128)], axis=1)
            keep = inner
            if row < 0:
                keep = keep & jnp.logical_not(first_strip)
            if row >= height:
                keep = keep & jnp.logical_not(last_strip)
            return jnp.where(keep, value, 0.0).astype(BF16)

        stack_taps(stacked.at[:, :, pl.ds(0, 3 * chans)], joined_row, height)
        skip_row = halo_rows(skip_ref.at[cycle], top[:cols], bottom[:cols])
        stack_taps(stacked.at[:, :, pl.ds(3 * chans, 3 * chans)], skip_row, height)
        for first in range(0, height, chunk):
            lhs = stacked[first : first + chunk].reshape(chunk * cols, 6 * chans)
            taps = []
            for tap in range(3):
                if cycle == 0 and first == 0:
                    arriving[7 + 2 * tap].wait()
                    arriving[8 + 2 * tap].wait()
                taps.append(dot(lhs, wd_ref[tap].reshape(6 * chans, chans)))
            total = (shifted_sum(taps, cols) + bd_ref[...]).reshape(chunk, cols, chans)
            out_ref[cycle, first : first + chunk] = total.astype(BF16)
            edge_ref[cycle, 0, first : first + chunk] = total[:, :16]
            edge_ref[cycle, 1, first : first + chunk] = total[:, cols - 16 :]
            rows = (cycle, pl.ds(first, chunk))
            leaving += fetch([(out_ref.at[rows], out_hbm.at[rows])], out_sems.at[cycle, pl.ds(first // chunk, 1)])
    leaving += fetch([(edge_ref, edge_hbm), (coarse_ref, coarse_hbm)], out_sems.at[cycles, pl.ds(0, 2)])
    for copy in leaving:
        copy.wait()


def seal(coarse_at, fine_at, tab_ref, tile_ref, code_ref, recv_ref, coarse_hbm, edge_hbm, wm_hbm, bm_hbm, u_hbm,
         bu_hbm, wd_hbm, out_in, out_hbm, coarse_ref, edge_ref, wm_ref, bm_ref, u_ref, bu_ref, wu_ref, ws_ref, out_ref,
         in_sems, out_sems):
    tiles, strips, height = coarse_at.tiles, coarse_at.strips, fine_at.height
    cycles, _, _, _, chans = edge_ref.shape
    cols = out_hbm.shape[2]
    low = height // 2
    pairs = [(bm_hbm, bm_ref), (bu_hbm, bu_ref), (coarse_hbm, coarse_ref), (wm_hbm, wm_ref), (u_hbm, u_ref)]
    pairs += [(wd_hbm.at[:, :, pl.ds(0, chans)], wu_ref), (edge_hbm, edge_ref)]
    pairs += [(wd_hbm.at[:, 2 * side, pl.ds(chans, chans)], ws_ref.at[side]) for side in range(2)]
    arriving = fetch(pairs, in_sems)
    strip = strip_of(tiles)
    rows8 = rows_iota(8) - 2
    rows16 = rows_iota(16) - 1
    aligned, taps, skips, sides, flips, strips_at = [], [[], [], []], [], [], [], []
    for side in range(2):
        for cycle in range(cycles):
            other, face, side_bit, flip = seam_of(tile_ref, code_ref, tiles, cycle, side)
            column = other * 2 + side_bit
            aligned.append(coarse_at.source(strip, flip, face, column * 2, rows8))
            place = fine_at.source(strip, flip, face, column, rows16)
            skips.append(jnp.where(rows16 <= height, place, -1))
            there = jnp.where(flip == 1, strips - 1 - strip, strip)
            number = tab_ref[face * 2, column]
            beyond = lax.div(number, 4)
            code = lax.rem(number, 4)
            other2, face2 = lax.div(beyond, FACES), lax.rem(beyond, FACES)
            column2 = other2 * 2 + lax.rem(code, 2)
            pad = coarse_at.source(there, lax.div(code, 2), face2, column2 * 2, rows8)
            edge = coarse_at.source(there, 0, face, column * 2, rows8)
            inner = coarse_at.source(there, 0, face, column * 2 + 1, rows8)
            taps[0].append(jnp.where(side_bit == 0, pad, inner))
            taps[1].append(edge)
            taps[2].append(jnp.where(side_bit == 0, inner, pad))
            sides.append(side_bit)
            flips.append(flip)
            strips_at.append(there)
    got = pick(aligned + taps[0] + taps[1] + taps[2] + skips, recv_ref[...])
    n = 8 * 2 * cycles
    at8 = lax.broadcasted_iota(jnp.int32, (8, chans), 0) - 2

    def on_face(s):
        return jnp.where(((at8 < 0) & (s == 0)) | ((at8 >= low) & (s == strips - 1)), 0.0, 1.0)

    for copy in arriving[:4]:
        copy.wait()
    own = got[:n]
    there = got[n : 4 * n]
    rows = []
    for row in range(3):
        here = [dot(own[side * n // 2 : (side + 1) * n // 2], wm_ref[row, 2 * side]) for side in range(2)]
        away = sum(dot(there[tap * n : (tap + 1) * n], wm_ref[row, tap]) for tap in range(3))
        rows.append(jnp.concatenate(here + [away], axis=0))
    total = pltpu.roll(rows[0], 1, 0) + rows[1] + pltpu.roll(rows[2], 2 * n - 1, 0)
    mine = [
        total[(side * cycles + cycle) * 8 : (side * cycles + cycle + 1) * 8] + coarse_ref[cycle, side]
        for side in range(2)
        for cycle in range(cycles)
    ]
    total = jnp.concatenate(mine + [total[n:] + bm_ref[...]], axis=0)
    keep = jnp.concatenate([on_face(s) for s in [strip] * (2 * cycles) + strips_at], axis=0)
    column = (gelu(total) * keep).astype(BF16)
    arriving[4].wait()
    phases = [
        [((dot(column, u_ref[a, b]) + bu_ref[...]) * keep).astype(BF16) for b in range(2)] for a in range(2)
    ]
    right = jnp.concatenate([jnp.where(at8 > -99, b, 0) for b in sides], axis=0) == 1
    place = lax.shift_right_arithmetic(rows16 - (rows16 & 1), 1) + 2
    fine_own = [jnp.where(rows16 <= height, (rows16 & 1) * n + k * 8 + place, -1) for k in range(2 * cycles)]
    fine_there = []
    for k in range(2 * cycles):
        fine = jnp.where(flips[k] == 1, height - 1 - rows16, rows16)
        a = fine & 1
        place = a * n + k * 8 + lax.shift_right_arithmetic(fine - a, 1) + 2
        fine_there.append(jnp.where(rows16 <= height, place, -1))
    beyond = [jnp.where(right, phases[a][1][n:], phases[a][0][n:]) for a in range(2)]
    outer = pick(fine_there, jnp.concatenate(beyond, axis=0))
    inside = [pick(fine_own, jnp.concatenate([phases[a][b][:n] for a in range(2)], axis=0)) for b in range(2)]
    skip_pad = got[4 * n :]
    m = 16 * cycles
    lines = [[outer[:m], inside[0][:m], inside[1][:m]], [outer[m:], inside[1][m:], inside[0][m:]]]
    for copy in arriving[5:]:
        copy.wait()
    sums = [[[], [], []], [[], [], []]]
    for row in range(3):
        found = [[0.0, 0.0, 0.0], [0.0, 0.0, 0.0]]
        for tap in range(3):
            uses = []
            for side in range(2):
                offset = tap if side == 0 else 2 - tap
                uses += [(side, line, line - offset) for line in range(3) if line >= offset]
            value = dot(jnp.concatenate([lines[side][line] for side, line, _ in uses], axis=0), wu_ref[row, tap])
            for k, (side, _, into) in enumerate(uses):
                found[side][into] = found[side][into] + value[k * m : (k + 1) * m]
        for side in range(2):
            found[side][0] = found[side][0] + dot(skip_pad[side * m : (side + 1) * m], ws_ref[side, row])
            for into in range(3):
                sums[side][into].append(found[side][into])
    iota16 = lax.broadcasted_iota(jnp.int32, (16, chans), 0)
    for side in range(2):
        for cycle in range(cycles):
            extra = [column_sum(sums[side][into], cycle, height) for into in range(3)]
            for row in range(height):
                value = edge_ref[cycle, side, row]
                for into in range(3):
                    at = into if side == 0 else 15 - into
                    value = value + jnp.where(iota16 == at, extra[into][row : row + 1], 0.0)
                out_ref[side, cycle, row] = value.astype(BF16)
    leaving = fetch(
        [(out_ref.at[side], out_hbm.at[:, :, pl.ds((cols - 16) * side, 16)]) for side in range(2)], out_sems
    )
    for copy in leaving:
        copy.wait()


def on_device(tiles, fields, seam_tile, seam_code, encoder_weight, encoder_bias, middle_weight,
              middle_bias, upconv_weight, upconv_bias, decoder_weight, decoder_offset_bias):
    cycles, height, cols, chans = fields.shape
    low, half = height // 2, cols // 2
    strips = tiles // FACES
    joint = strips == 4

    def strip(t):
        return (t + strips // 2) % strips

    near_pairs, far_pairs = [], []
    for t in range(tiles):
        pairs = near_pairs if strip(t) % 2 == 0 else far_pairs
        after = (t + 1) % tiles
        pairs += [(t, after), (after, t)]

    def tile_at(face, s):
        return (face * strips + s - strips // 2) % tiles

    groups = [
        [tile_at(face, s) for face in range(FACES) for s in (k, strips - 1 - k)]
        for k in range(strips // 2)
    ]
    members = 2 * FACES

    def share(x):
        return lax.all_to_all(x, "tile", 0, 0, tiled=True, axis_index_groups=groups)

    columns = 2 * cycles
    tail1 = (columns + 1 + 15) // 16 * 16
    spec = Layout(tiles, height, 1, columns, 0, columns * height, tail1)
    own2 = 2 * columns * low + columns * height
    tail2 = (4 * columns + columns + 15) // 16 * 16
    coarse_at = Layout(tiles, low, 2, 2 * columns, 0, own2, tail2)
    fine_at = Layout(tiles, height, 1, columns, 2 * columns * low, own2 + 4 * columns, tail2)
    halos = 1 if joint else 2
    spec.payload = columns * height + halos * tail1
    payload = own2 + halos * tail2
    coarse_at.payload = fine_at.payload = payload

    def to_near(x):
        return lax.ppermute(x, "tile", near_pairs)

    def to_far(x):
        return lax.ppermute(x, "tile", far_pairs)

    def pack(own, near_tail, far_tail):
        parts = [own, to_near(near_tail)] + ([] if joint else [to_far(far_tail)])
        parts = [jnp.broadcast_to(part[None], (members,) + part.shape) for part in parts]
        return share(jnp.concatenate(parts, axis=1))

    seams = (jnp.transpose(seam_tile, (1, 2, 0)), jnp.transpose(seam_code, (1, 2, 0)))
    eb, mb, ub, db = (b.reshape(1, chans) for b in (encoder_bias, middle_bias, upconv_bias, decoder_offset_bias))

    hbm = pl.BlockSpec(memory_space=pltpu.HBM)
    vmem = pl.BlockSpec(memory_space=pltpu.VMEM)
    smem = pl.BlockSpec(memory_space=pltpu.SMEM)
    dma = pltpu.SemaphoreType.DMA
    tall = (cycles, height, cols, chans)
    row_shape = (cycles, cols, chans)
    wide = (cycles, 2 * cols, chans)
    square = (chans, chans)
    wshape = (3, 3) + square
    pooled_shape = (cycles, low, half, chans)
    edge_shape = (2, cycles, height, 16, chans)

    def call(body, name, outs, in_specs, out_specs, scratch, *args, **options):
        return pl.pallas_call(
            body,
            out_shape=[jax.ShapeDtypeStruct(shape, dtype) for shape, dtype in outs],
            in_specs=in_specs,
            out_specs=out_specs,
            scratch_shapes=[pltpu.VMEM(*x) if isinstance(x, tuple) else x for x in scratch],
            compiler_params=pltpu.CompilerParams(vmem_limit_bytes=56 * MIB),
            name=name,
            **options,
        )(*args)

    far_cost = pl.CostEstimate(flops=10**12, bytes_accessed=10**9, transcendentals=0)
    vector = (1, chans)
    own, near_tail, far_tail, near, far = call(
        functools.partial(lift, spec), "lift",
        [((columns * height, chans), BF16)] + [((tail1, chans), BF16)] * 2 + [(row_shape, BF16)] * 2,
        [hbm, smem, smem], [hbm] * 5,
        [(edge_shape, BF16), ((2,) + row_shape, BF16), ((columns * height, chans), F32), ((2, tail1, chans), F32),
         ((columns * height, chans), BF16), ((2, tail1, chans), BF16), dma((4,)), dma((5,))],
        fields, *seams,
    )
    recv = pack(own, near_tail, far_tail)
    near, far = to_near(near), to_far(far)
    pre_shape = (cycles, 2, height, chans)
    skip, pooled, near, far, pre_col = call(
        functools.partial(encode, tiles), "encode",
        [(tall, BF16), (pooled_shape, BF16), (wide, BF16), (wide, BF16), (pre_shape, F32)],
        [hbm, vmem, vmem, hbm, hbm], [hbm] * 5,
        [(tall, BF16), (wshape, BF16), (vector, F32), ((height, cols, 3 * chans), BF16), (tall, BF16),
         (pooled_shape, BF16), ((2,) + wide, BF16), (pre_shape, F32), ((cols, 128), F32),
         dma((4 + cycles,)), dma((cycles, height // 4 + 4))],
        fields, near, far, encoder_weight, eb,
        cost_estimate=far_cost,
    )
    pool_edges = (2, cycles, low, 16, chans)
    skip, pooled, near, far, own, near_tail, far_tail, table = call(
        functools.partial(mend, spec, coarse_at, fine_at), "mend",
        [(tall, BF16), (pooled_shape, BF16), (wide, BF16), (wide, BF16), ((own2, chans), BF16)]
        + [((tail2, chans), BF16)] * 2 + [((members, 128), jnp.int32)],
        [vmem] + [hbm] * 6 + [smem, smem], [hbm] * 8,
        [((2, 3) + square, BF16), (pre_shape, F32), (edge_shape, BF16), (pool_edges, BF16), ((own2, chans), F32),
         ((2, tail2, chans), F32), ((own2, chans), BF16), ((2, tail2, chans), BF16), ((members, 128), jnp.int32),
         dma((7,)), dma((20,))],
        recv.reshape(-1, chans), encoder_weight, skip, pooled, near, far, pre_col, *seams,
        input_output_aliases={2: 0, 3: 1, 4: 2, 5: 3},
    )
    recv2 = pack(own, near_tail, far_tail)
    near2, far2 = to_near(near), to_far(far)
    edges = (cycles, 2, height, 16, chans)
    coarse_edges = (cycles, 2, 8, chans)
    out, edge, coarse = call(
        functools.partial(decode, tiles), "decode",
        [(tall, BF16), (edges, F32), (coarse_edges, F32)],
        [hbm, hbm, vmem, vmem] + [hbm] * 6, [hbm, hbm, hbm],
        [(tall, BF16), (pooled_shape, BF16), (wshape, BF16), (vector, F32), ((2, 2) + square, BF16),
         (vector, F32), ((3, 6) + square, BF16), (vector, F32), (tall, BF16), (edges, F32), (coarse_edges, F32),
         ((height, cols, 6 * chans), BF16), ((low + 2, half, 3 * chans), BF16),
         ((height + 2, chans // 128, cols, 128), F32), dma((12 + cycles,)), dma((cycles + 1, height))],
        skip, pooled, near2, far2, middle_weight, mb, upconv_weight, ub, decoder_weight, db,
        cost_estimate=far_cost,
    )
    (out,) = call(
        functools.partial(seal, coarse_at, fine_at), "seal",
        [(tall, BF16)],
        [smem, smem, smem, vmem] + [hbm] * 8, [hbm],
        [(coarse_edges, F32), (edges, F32), (wshape, BF16), (vector, F32), ((2, 2) + square, BF16), (vector, F32),
         (wshape, BF16), ((2, 3) + square, BF16), (edge_shape, BF16), dma((9,)), dma((2,))],
        table, *seams, recv2.reshape(-1, chans), coarse, edge, middle_weight, mb, upconv_weight, ub, decoder_weight, out,
        input_output_aliases={11: 0},
    )
    return out


def solution(mesh):
    return jax.shard_map(
        functools.partial(on_device, mesh.shape["tile"]),
        mesh=mesh,
        in_specs=(P("grp", "tile", None, None), P(None, "tile", None), P(None, "tile", None)) + (P(),) * 8,
        out_specs=P("grp", "tile", None, None),
        check_vma=False,
    )
```

time: 165 us -> 64.6 us (0.39)
  blocking collectives: 65.3 us -> 0 us
  matrix products: 50.2 us -> 0 us
  Pallas kernels: 0 us -> 35.6 us
  local copies, waits for them, and re-layouts: 20.2 us -> 3.1 us
  starting transfers between devices: 5.01 us -> 21 us
  other arithmetic: 12.4 us -> 1.54 us
  waiting for transfers between devices: 10.8 us -> 2.39 us
    all_gather x3 -> x0, blocking collectives: 65.3 us -> none  [the longest x2 43.8 us: on_device(): lax.all_gather(boundary_columns(extended)[:, None], 'tile', axis=1, tiled...]
    dot_general x31 -> x0, matrix products: 50.2 us -> none  [the longest x27 49.1 us: convolve(): jnp.dot(window.reshape(-1, chans_in), weight[row_tap, col_tap], preferred...]
    pallas_call x0 -> x5, Pallas kernels: none -> 35.6 us  [call(): pl.pallas_call(body, out_shape=[jax.ShapeDtypeStruct(shape, dtype) for sh...]
    all_to_all x0 -> x2, starting transfers between devices: none -> 13.5 us  [share(): return lax.all_to_all(x, 'tile', 0, 0, tiled=True, axis_index_groups=groups)]
    ppermute x6, waiting for transfers between devices: 10.8 us -> 2.39 us  [the longest x4 2.09 us: to_near(): return lax.ppermute(x, 'tile', near_pairs)]
    reshape x4 -> x0, local copies, waits for them, and re-layouts: 6.49 us -> none  [the longest x3 3.5 us: flatten_gathered(): return gathered.reshape((-1,) + gathered.shape[2:])]
    reduce_sum x1 -> x0, other arithmetic: 4.28 us -> none  [coarsen_grid(): return jnp.mean(values, axis=(-4, -2)).astype(jnp.bfloat16)]
    gather x3 -> x0, local copies, waits for them, and re-layouts: 4.01 us -> none  [pick_partner(): chosen = flattened[partners]]
  transfers between devices with their start and end apart: 6 -> 8, of which waited for: 3 -> 3; matrix products, arithmetic and copies ran while one was open for 10% -> 5% of each run, Pallas kernels for 0% -> 37%
where the time goes in v2:
time: 64.6 us; the launch traced here: 63.9 us
  Pallas kernels  35.6 us (55%)
  starting transfers between devices  21 us (33%)
  local copies, waits for them, and re-layouts  3.1 us (5%)
  waiting for transfers between devices  2.39 us (4%)
  other arithmetic  1.54 us (2%)
    pallas_call x5, Pallas kernels, call(): pl.pallas_call(body, out_shape=[jax.ShapeDtypeStruct(shape, dtype) for sh...  35.6 us
    all_to_all x2, starting transfers between devices, share(): return lax.all_to_all(x, 'tile', 0, 0, tiled=True, axis_index_groups=groups)  13.5 us
    ppermute x4, starting transfers between devices, to_near(): return lax.ppermute(x, 'tile', near_pairs)  4.51 us
    ppermute x2, starting transfers between devices, to_far(): return lax.ppermute(x, 'tile', far_pairs)  2.92 us
    ppermute x4, waiting for transfers between devices, to_near(): return lax.ppermute(x, 'tile', near_pairs)  2.09 us
    broadcast_in_dim x4, local copies, waits for them, and re-layouts, pack(): jnp.broadcast_to(part[None], (members,) + part.shape)  1.59 us
    concatenate x2, other arithmetic, pack(): return share(jnp.concatenate(parts, axis=1))  1.54 us
    unnamed x8, local copies, waits for them, and re-layouts  1.51 us
  transfers between devices with their start and end apart: 8, of which 3 were waited for; matrix products, arithmetic and copies ran while one was open for 5% of the time, Pallas kernels for 37%

profile of v2, /device:TPU:1, one launch (start us, length us, event | category | flops | bytes accessed | tf_op | source)
XLA Modules:
  0.0 63.9 jit_solution(15415620889637957224)
XLA Ops:
  0.0 2.8 %lift.1 = (bf16[48,256]{1,0:T(8,128)(2,1)}, bf16[16,256]{1,0:T(8,128)(2,1)}, bf16[16,256]{1,0:T(8,128)(2,1)}, bf16[3,128,256]{2,1,0:T(8,128)(2,1)}, bf16[3,128,256]{2,1,0:T(8,128)(2,1)}) custom-call(bf16[3,8,128,256]{3,2,1,0:T(8,128)(2,1)} %x_hbm.3, s32[1,2,3]{2,1,0:T(2,128)} %bitcast.8, s32[1,2,3]{2,1,0:T(2,128)} %bitcast.11), custom_call_target="tpu_custom_call" | custom-call | tf_op jit(solution)/shard_map/lift/pallas_call | solution.py:596
  2.8 0.1 collective-permute-start.1
  2.9 2.6 %collective-permute-start.2 = (bf16[3,128,256]{2,1,0:T(8,128)(2,1)}, bf16[3,128,256]{2,1,0:T(8,128)(2,1)S(1)}, u32[]{:S(2)}, u32[]{:S(2)}) collective-permute-start(bf16[3,128,256]{2,1,0:T(8,128)(2,1)} %get-tuple-element.27), channel_id=1, source_target_pairs={{1,2},{2,1},{3,4},{4,3},{5,6},{6,5},{7,8},{8,7},{9,10},{10,9},{11,... | collective-permute-start | bytes 589832 | tf_op jit(solution)/shard_map/ppermute | solution.py:573
  5.5 3.5 %collective-permute-start = (bf16[16,256]{1,0:T(8,128)(2,1)}, bf16[16,256]{1,0:T(8,128)(2,1)S(1)}, u32[]{:S(2)}, u32[]{:S(2)}) collective-permute-start(bf16[16,256]{1,0:T(8,128)(2,1)} %get-tuple-element.25), channel_id=1, source_target_pairs={{0,1},{1,0},{2,3},{3,2},{4,5},{5,4},{6,7},{7,6},{8,9},{9,8},{10,11... | collective-permute-start | bytes 24584 | tf_op jit(solution)/shard_map/ppermute | solution.py:570
  9.0 1.0 %collective-permute-done = bf16[16,256]{1,0:T(8,128)(2,1)S(1)} collective-permute-done((bf16[16,256]{1,0:T(8,128)(2,1)}, bf16[16,256]{1,0:T(8,128)(2,1)S(1)}, u32[]{:S(2)}, u32[]{:S(2)}) %collective-permute-start) | collective-permute-done | bytes 8224 | tf_op jit(solution)/shard_map/ppermute | solution.py:570
  10.0 0.8 %broadcast_in_dim.8 = bf16[8,48,256]{2,1,0:T(8,128)(2,1)S(1)} broadcast(bf16[48,256]{1,0:T(8,128)(2,1)} %get-tuple-element.24), dimensions={1,2} | broadcast | bytes 221184 | tf_op jit(solution)/shard_map/broadcast_in_dim | solution.py:577
  10.8 0.7 %pad_maximum_fusion.1 = bf16[8,64,256]{2,1,0:T(8,128)(2,1)} fusion(bf16[8,16,256]{2,1,0:T(8,128)(2,1)S(1)} %broadcast_in_dim.9, bf16[8,48,256]{2,1,0:T(8,128)(2,1)S(1)} %broadcast_in_dim.8), kind=kLoop, calls=%fused_computation.1 | loop fusion | flops 524288 | bytes 524288 | tf_op jit(solution)/shard_map/concatenate | solution.py:578
  11.5 5.7 %all-to-all-start = ((bf16[8,64,256]{2,1,0:T(8,128)(2,1)}), bf16[8,64,256]{2,1,0:T(8,128)(2,1)}, u32[]{:S(2)}, u32[]{:S(2)}) async-start(bf16[8,64,256]{2,1,0:T(8,128)(2,1)} %pad_maximum_fusion.1), calls=%async_computation | async-start | bytes 524288 | tf_op jit(solution)/shard_map/all_to_all | solution.py:555
  17.2 0.0 collective-permute-done.1.near_ref
  17.2 0.0 copy-start.2
  17.2 0.0 collective-permute-done.2.far_ref
  17.2 0.0 copy-start.3
  17.2 0.7 %copy-done.2 = bf16[3,128,256]{2,1,0:T(8,128)(2,1)} copy-done((bf16[3,128,256]{2,1,0:T(8,128)(2,1)}, bf16[3,128,256]{2,1,0:T(8,128)(2,1)S(1)}, u32[]{:S(2)}) %copy-start.2) | copy-done | bytes 196632
  17.9 0.1 copy-done.3
  18.0 8.3 %encode.1 = (bf16[3,8,128,256]{3,2,1,0:T(8,128)(2,1)}, bf16[3,4,64,256]{3,2,1,0:T(8,128)(2,1)}, bf16[3,256,256]{2,1,0:T(8,128)(2,1)}, bf16[3,256,256]{2,1,0:T(8,128)(2,1)}, f32[3,2,8,256]{3,2,1,0:T(8,128)}) custom-call(bf16[3,8,128,256]{3,2,1,0:T(8,128)(2,1)} %x_hbm.3, bf16[3,128,256]{2,1,0:T(8,128)(2,1)} %copy-done.2, bf16[3,128,256]{2,1,0:T(8,128)(2,1)} %copy-done.3, ...), custom_call_target="tpu_custom_call" | custom-call | flops 999999995904 | bytes 1000000000 | tf_op jit(solution)/shard_map/encode/pallas_call | solution.py:596
  26.3 0.0 all-to-all-done
  26.3 3.9 %mend.1 = (bf16[3,8,128,256]{3,2,1,0:T(8,128)(2,1)}, bf16[3,4,64,256]{3,2,1,0:T(8,128)(2,1)}, bf16[3,256,256]{2,1,0:T(8,128)(2,1)}, bf16[3,256,256]{2,1,0:T(8,12...) custom-call(bf16[512,256]{1,0:T(8,128)(2,1)} %bitcast.2.recv_ref, ...), custom_call_target="tpu_custom_call", output_to_operand_aliasing={{0}: (2, {}), {1}: (3, {}), {2}: (4, {}), {3}: (5, {})} | custom-call | tf_op jit(solution)/shard_map/mend/pallas_call | solution.py:596
  30.2 0.4 collective-permute-start.4
  30.6 0.3 collective-permute-start.5
  30.9 0.5 collective-permute-start.3
  31.4 1.0 %collective-permute-done.3 = bf16[32,256]{1,0:T(8,128)(2,1)S(1)} collective-permute-done((bf16[32,256]{1,0:T(8,128)(2,1)}, bf16[32,256]{1,0:T(8,128)(2,1)S(1)}, u32[]{:S(2)}, u32[]{:S(2)}) %collective-permute-start.3) | collective-permute-done | bytes 16416 | tf_op jit(solution)/shard_map/ppermute | solution.py:570
  32.5 0.8 %broadcast_in_dim.10 = bf16[8,96,256]{2,1,0:T(8,128)(2,1)S(1)} broadcast(bf16[96,256]{1,0:T(8,128)(2,1)} %get-tuple-element.34), dimensions={1,2} | broadcast | bytes 442368 | tf_op jit(solution)/shard_map/broadcast_in_dim | solution.py:577
  33.3 0.8 %pad_maximum_fusion = bf16[8,128,256]{2,1,0:T(8,128)(2,1)} fusion(bf16[8,32,256]{2,1,0:T(8,128)(2,1)S(1)} %broadcast_in_dim.11, bf16[8,96,256]{2,1,0:T(8,128)(2,1)S(1)} %broadcast_in_dim.10), kind=kLoop, calls=%fused_computation | loop fusion | flops 1048576 | bytes 1048576 | tf_op jit(solution)/shard_map/concatenate | solution.py:578
  34.2 7.8 %all-to-all-start.1 = ((bf16[8,128,256]{2,1,0:T(8,128)(2,1)}), bf16[8,128,256]{2,1,0:T(8,128)(2,1)}, u32[]{:S(2)}, u32[]{:S(2)}) async-start(bf16[8,128,256]{2,1,0:T(8,128)(2,1)} %pad_maximum_fusion), calls=%async_computation.1 | async-start | bytes 1048576 | tf_op jit(solution)/shard_map/all_to_all | solution.py:555
  42.0 0.0 collective-permute-done.4.near_ref
  42.0 0.0 copy-start
  42.0 0.3 collective-permute-done.5.far_ref
  42.3 0.0 copy-start.1
  42.3 0.4 copy-done
  42.7 0.3 copy-done.1
  43.0 15.5 %decode.1 = (bf16[3,8,128,256]{3,2,1,0:T(8,128)(2,1)}, f32[3,2,8,16,256]{4,3,2,1,0:T(8,128)}, f32[3,2,8,256]{3,2,1,0:T(8,128)}) custom-call(bf16[3,8,128,256]{3,2,1,0:T(8,128)(2,1)} %get-tuple-element.36.skip_hbm, bf16[3,4,64,256]{3,2,1,0:T(8,128)(2,1)} %get-tuple-element.37.pooled_hbm, bf16[3,256,256]{2,1,0:T(8,128)(2,1)} %copy-done, ...), custom_call_target="tpu_custom_call" | custom-call | flops 999999995904 | bytes 1000000000 | tf_op jit(solution)/shard_map/decode/pallas_call | solution.py:596
  58.5 0.0 all-to-all-done.1
  58.5 5.2 %seal.1 = bf16[3,8,128,256]{3,2,1,0:T(8,128)(2,1)} custom-call(s32[8,128]{1,0:T(8,128)} %get-tuple-element.33.tab_ref, s32[1,2,3]{2,1,0:T(2,128)} %bitcast.10, s32[1,2,3]{2,1,0:T(2,128)} %bitcast.13, bf16[1024,256]{1,0:T(8,128)(2,1)} %bitcast.4.recv_ref, f32[3,2,8,256]{3,2,1,0:T(8,128)} %get-tuple-element.40.coarse_hbm, ...), custom_call_target="tpu_custom_call", output_to_operand_aliasing={{}: (11, {})} | custom-call | tf_op jit(solution)/shard_map/seal/pallas_call | solution.py:596
  (2 shorter events, 0.0 us)
Async XLA Ops:
  2.8 14.4 %collective-permute-start.1 = (bf16[3,128,256]{2,1,0:T(8,128)(2,1)}, bf16[3,128,256]{2,1,0:T(8,128)(2,1)S(1)}, u32[]{:S(2)}, u32[]{:S(2)}) collective-permute-start(bf16[3,128,256]{2,1,0:T(8,128)(2,1)} %get-tuple-element.26), channel_id=1, source_target_pairs={{0,1},{1,0},{2,3},{3,2},{4,5},{5,4},{6,7},{7,6},{8,9},{9,8},{10,11... | collective-permute-start | bytes 589832 | tf_op jit(solution)/shard_map/ppermute | solution.py:570
  2.9 14.3 %collective-permute-start.2 = (bf16[3,128,256]{2,1,0:T(8,128)(2,1)}, bf16[3,128,256]{2,1,0:T(8,128)(2,1)S(1)}, u32[]{:S(2)}, u32[]{:S(2)}) collective-permute-start(bf16[3,128,256]{2,1,0:T(8,128)(2,1)} %get-tuple-element.27), channel_id=1, source_target_pairs={{1,2},{2,1},{3,4},{4,3},{5,6},{6,5},{7,8},{8,7},{9,10},{10,9},{11,... | collective-permute-start | bytes 589832 | tf_op jit(solution)/shard_map/ppermute | solution.py:573
  5.5 4.5 %collective-permute-start = (bf16[16,256]{1,0:T(8,128)(2,1)}, bf16[16,256]{1,0:T(8,128)(2,1)S(1)}, u32[]{:S(2)}, u32[]{:S(2)}) collective-permute-start(bf16[16,256]{1,0:T(8,128)(2,1)} %get-tuple-element.25), channel_id=1, source_target_pairs={{0,1},{1,0},{2,3},{3,2},{4,5},{5,4},{6,7},{7,6},{8,9},{9,8},{10,11... | collective-permute-start | bytes 24584 | tf_op jit(solution)/shard_map/ppermute | solution.py:570
  11.5 14.8 %all-to-all-start = ((bf16[8,64,256]{2,1,0:T(8,128)(2,1)}), bf16[8,64,256]{2,1,0:T(8,128)(2,1)}, u32[]{:S(2)}, u32[]{:S(2)}) async-start(bf16[8,64,256]{2,1,0:T(8,128)(2,1)} %pad_maximum_fusion.1), calls=%async_computation | async-start | bytes 524288 | tf_op jit(solution)/shard_map/all_to_all | solution.py:555
  17.2 0.7 %copy-start.2 = (bf16[3,128,256]{2,1,0:T(8,128)(2,1)}, bf16[3,128,256]{2,1,0:T(8,128)(2,1)S(1)}, u32[]{:S(2)}) copy-start(bf16[3,128,256]{2,1,0:T(8,128)(2,1)S(1)} %collective-permute-done.1.near_ref) | copy-start | bytes 589828
  17.2 0.7 %copy-start.3 = (bf16[3,128,256]{2,1,0:T(8,128)(2,1)}, bf16[3,128,256]{2,1,0:T(8,128)(2,1)S(1)}, u32[]{:S(2)}) copy-start(bf16[3,128,256]{2,1,0:T(8,128)(2,1)S(1)} %collective-permute-done.2.far_ref) | copy-start | bytes 589828
  30.2 11.7 %collective-permute-start.4 = (bf16[3,256,256]{2,1,0:T(8,128)(2,1)}, bf16[3,256,256]{2,1,0:T(8,128)(2,1)S(1)}, u32[]{:S(2)}, u32[]{:S(2)}) collective-permute-start(bf16[3,256,256]{2,1,0:T(8,128)(2,1)} %get-tuple-element.38), channel_id=1, source_target_pairs={{0,1},{1,0},{2,3},{3,2},{4,5},{5,4},{6,7},{7,6},{8,9},{9,8},{10,11... | collective-permute-start | bytes 1179656 | tf_op jit(solution)/shard_map/ppermute | solution.py:570
  30.6 11.6 %collective-permute-start.5 = (bf16[3,256,256]{2,1,0:T(8,128)(2,1)}, bf16[3,256,256]{2,1,0:T(8,128)(2,1)S(1)}, u32[]{:S(2)}, u32[]{:S(2)}) collective-permute-start(bf16[3,256,256]{2,1,0:T(8,128)(2,1)} %get-tuple-element.39), channel_id=1, source_target_pairs={{1,2},{2,1},{3,4},{4,3},{5,6},{6,5},{7,8},{8,7},{9,10},{10,9},{11,... | collective-permute-start | bytes 1179656 | tf_op jit(solution)/shard_map/ppermute | solution.py:573
  30.9 1.6 %collective-permute-start.3 = (bf16[32,256]{1,0:T(8,128)(2,1)}, bf16[32,256]{1,0:T(8,128)(2,1)S(1)}, u32[]{:S(2)}, u32[]{:S(2)}) collective-permute-start(bf16[32,256]{1,0:T(8,128)(2,1)} %get-tuple-element.35), channel_id=1, source_target_pairs={{0,1},{1,0},{2,3},{3,2},{4,5},{5,4},{6,7},{7,6},{8,9},{9,8},{10,11... | collective-permute-start | bytes 49160 | tf_op jit(solution)/shard_map/ppermute | solution.py:570
  34.2 24.4 %all-to-all-start.1 = ((bf16[8,128,256]{2,1,0:T(8,128)(2,1)}), bf16[8,128,256]{2,1,0:T(8,128)(2,1)}, u32[]{:S(2)}, u32[]{:S(2)}) async-start(bf16[8,128,256]{2,1,0:T(8,128)(2,1)} %pad_maximum_fusion), calls=%async_computation.1 | async-start | bytes 1048576 | tf_op jit(solution)/shard_map/all_to_all | solution.py:555
  42.0 0.7 %copy-start = (bf16[3,256,256]{2,1,0:T(8,128)(2,1)}, bf16[3,256,256]{2,1,0:T(8,128)(2,1)S(1)}, u32[]{:S(2)}) copy-start(bf16[3,256,256]{2,1,0:T(8,128)(2,1)S(1)} %collective-permute-done.4.near_ref) | copy-start | bytes 1179652
  42.3 0.8 %copy-start.1 = (bf16[3,256,256]{2,1,0:T(8,128)(2,1)}, bf16[3,256,256]{2,1,0:T(8,128)(2,1)S(1)}, u32[]{:S(2)}) copy-start(bf16[3,256,256]{2,1,0:T(8,128)(2,1)S(1)} %collective-permute-done.5.far_ref) | copy-start | bytes 1179652

commit v3 on v2

--- a/solution.py
+++ b/solution.py
@@ -163,7 +163,8 @@
                 tails[k, column : column + 1] = value
     own16[...] = own[...].astype(BF16)
     tails16[...] = tails[...].astype(BF16)
-    pairs = [(tails16.at[0], near_tail_hbm), (tails16.at[1], far_tail_hbm), (own16, own_hbm)]
+    pairs = [(tails16.at[0], near_tail_hbm), (tails16.at[1], far_tail_hbm)]
+    pairs += [(own16, own_hbm.at[k, pl.ds(0, own16.shape[0])]) for k in range(2 * FACES)]
     for copy in arriving[2:]:
         copy.wait()
     leaving = fetch(pairs + [(rows.at[0], near_hbm), (rows.at[1], far_hbm)], out_sems)
@@ -305,7 +306,8 @@
                         tails[k, start : start + 1] = value[place : place + 1]
     own16[...] = own[...].astype(BF16)
     tails16[...] = tails[...].astype(BF16)
-    pairs = [(tails16.at[0], near_tail_hbm), (own16, own_hbm), (tails16.at[1], far_tail_hbm), (table_ref, table_hbm)]
+    pairs = [(tails16.at[0], near_tail_hbm), (tails16.at[1], far_tail_hbm), (table_ref, table_hbm)]
+    pairs += [(own16, own_hbm.at[k, pl.ds(0, own16.shape[0])]) for k in range(2 * FACES)]
     for side in range(2):
         pairs.append((edges.at[side], skip_hbm.at[:, :, pl.ds((cols - 16) * side, 16)]))
         pairs.append((pools.at[side], pooled_hbm.at[:, :, pl.ds((half - 16) * side, 16)]))
@@ -319,14 +321,16 @@
         copy.wait()
 
 
-def decode(tiles, skip_hbm, pooled_hbm, near_ref, far_ref, wm_hbm, bm_hbm, u_hbm, bu_hbm, wd_hbm, bd_hbm,
-           out_hbm, edge_hbm, coarse_hbm, skip_ref, pooled_ref, wm_ref, bm_ref, u_ref, bu_ref, wd_ref,
-           bd_ref, out_ref, edge_ref, coarse_ref, stacked, upper, joined, in_sems, out_sems):
+def decode(tiles, skip_hbm, pooled_hbm, near_hbm, far_hbm, wm_hbm, bm_hbm, u_hbm, bu_hbm, wd_hbm, bd_hbm,
+           out_hbm, edge_hbm, coarse_hbm, skip_ref, pooled_ref, near_ref, far_ref, wm_ref, bm_ref, u_ref, bu_ref,
+           wd_ref, bd_ref, out_ref, edge_ref, coarse_ref, stacked_a, stacked_b, upper_a, upper_b, joined_a, joined_b,
+           in_sems, out_sems):
     strips = tiles // FACES
     cycles, height, cols, chans = skip_ref.shape
     low, half = height // 2, cols // 2
-    pairs = [(bm_hbm, bm_ref), (bu_hbm, bu_ref), (bd_hbm, bd_ref), (pooled_hbm, pooled_ref)]
-    pairs += [(wm_hbm, wm_ref), (u_hbm, u_ref), (skip_hbm.at[0], skip_ref.at[0])]
+    pairs = [(near_hbm, near_ref), (far_hbm, far_ref), (pooled_hbm, pooled_ref), (bm_hbm, bm_ref)]
+    pairs += [(wm_hbm.at[:, tap], wm_ref.at[tap]) for tap in range(3)]
+    pairs += [(bu_hbm, bu_ref), (u_hbm, u_ref), (skip_hbm.at[0], skip_ref.at[0]), (bd_hbm, bd_ref)]
     for tap in range(3):
         for part in range(2):
             source = wd_hbm.at[:, tap, pl.ds(part * chans, chans)]
@@ -340,12 +344,13 @@
     place = lax.broadcasted_iota(jnp.int32, (cols, chans), 0)
     inner = (place > 1) & (place < cols - 2)
     coarse_ref[...] = jnp.zeros_like(coarse_ref)
-    chunk = 1
     leaving = []
     for copy in arriving[:4]:
         copy.wait()
-    for cycle in range(cycles):
+
+    def prepare(cycle):
         top, bottom = top_and_bottom(near_ref[cycle], far_ref[cycle], odd, ends)
+        stacked, upper, joined = (stacked_a, upper_a, joined_a) if cycle % 2 == 0 else (stacked_b, upper_b, joined_b)
 
         def pooled_row(row):
             if row < -1:
@@ -359,18 +364,27 @@
             return bottom[cols + half :]
 
         stack_taps(upper, lambda row: pooled_row(row - 1), low + 2)
+        yield
         lhs = upper[...].reshape((low + 2) * half, 3 * chans)
+        taps = []
+        for tap in range(3):
+            if cycle == 0:
+                arriving[4 + tap].wait()
+            taps.append(dot(lhs, wm_ref[tap].reshape(3 * chans, chans)))
+        total = shifted_sum(taps, half) + bm_ref[...]
+        yield
+        coarse = []
+        for row in range(low + 2):
+            at = row * half
+            coarse_ref[cycle, 0, row + 1 : row + 2] = total[at : at + 1]
+            coarse_ref[cycle, 1, row + 1 : row + 2] = total[at + half - 1 : at + half]
+            coarse.append(gelu(total[at : at + half]).astype(BF16))
         if cycle == 0:
-            arriving[4].wait()
-        total = shifted_sum(column_taps(lhs, wm_ref), half) + bm_ref[...]
-        for row in range(low + 2):
-            coarse_ref[cycle, 0, row + 1 : row + 2] = total[row * half : row * half + 1]
-            coarse_ref[cycle, 1, row + 1 : row + 2] = total[(row + 1) * half - 1 : (row + 1) * half]
-        coarse = gelu(total).astype(BF16)
-        if cycle == 0:
-            arriving[5].wait()
+            arriving[7].wait()
+            arriving[8].wait()
+        yield
         for a in range(2):
-            part = coarse[half:] if a == 0 else coarse[:-half]
+            part = jnp.concatenate(coarse[1:] if a == 0 else coarse[:-1], axis=0)
             for b in range(2):
                 value = dot(part, u_ref[a, b]) + bu_ref[...]
                 for k in range(low + 1):
@@ -378,47 +392,69 @@
                     for lane in range(0, chans, 128):
                         part_of = value[k * half : (k + 1) * half, lane : lane + 128]
                         joined[at, lane // 128, pl.ds(b, half, 2), :] = part_of
-        arriving[6 if cycle == 0 else 12 + cycle].wait()
-
-        def joined_row(row):
+                yield
+        arriving[9 if cycle == 0 else 16 + cycle].wait()
+        skip_row = halo_rows(skip_ref.at[cycle], top[:cols], bottom[:cols])
+        stack_taps(stacked.at[:, :, pl.ds(3 * chans, 3 * chans)], skip_row, height)
+        for row in range(-1, height + 1):
             value = jnp.concatenate([joined[row + 1, k] for k in range(chans // 128)], axis=1)
             keep = inner
             if row < 0:
                 keep = keep & jnp.logical_not(first_strip)
             if row >= height:
                 keep = keep & jnp.logical_not(last_strip)
-            return jnp.where(keep, value, 0.0).astype(BF16)
-
-        stack_taps(stacked.at[:, :, pl.ds(0, 3 * chans)], joined_row, height)
-        skip_row = halo_rows(skip_ref.at[cycle], top[:cols], bottom[:cols])
-        stack_taps(stacked.at[:, :, pl.ds(3 * chans, 3 * chans)], skip_row, height)
-        for first in range(0, height, chunk):
-            lhs = stacked[first : first + chunk].reshape(chunk * cols, 6 * chans)
+            value = jnp.where(keep, value, 0.0).astype(BF16)
+            for tap in range(3):
+                at = row + 1 - tap
+                if 0 <= at < height:
+                    stacked[at, :, tap * chans : (tap + 1) * chans] = value
+            if row % 5 == 3:
+                yield
+
+    def convolve(cycle):
+        stacked = stacked_a if cycle % 2 == 0 else stacked_b
+        for row in range(height):
             taps = []
             for tap in range(3):
-                if cycle == 0 and first == 0:
-                    arriving[7 + 2 * tap].wait()
-                    arriving[8 + 2 * tap].wait()
-                taps.append(dot(lhs, wd_ref[tap].reshape(6 * chans, chans)))
-            total = (shifted_sum(taps, cols) + bd_ref[...]).reshape(chunk, cols, chans)
-            out_ref[cycle, first : first + chunk] = total.astype(BF16)
-            edge_ref[cycle, 0, first : first + chunk] = total[:, :16]
-            edge_ref[cycle, 1, first : first + chunk] = total[:, cols - 16 :]
-            rows = (cycle, pl.ds(first, chunk))
-            leaving += fetch([(out_ref.at[rows], out_hbm.at[rows])], out_sems.at[cycle, pl.ds(first // chunk, 1)])
-    leaving += fetch([(edge_ref, edge_hbm), (coarse_ref, coarse_hbm)], out_sems.at[cycles, pl.ds(0, 2)])
+                if cycle == 0 and row == 0:
+                    for k in range(10 if tap == 0 else 11 + 2 * tap, 13 + 2 * tap):
+                        arriving[k].wait()
+                taps.append(dot(stacked[row], wd_ref[tap].reshape(6 * chans, chans)))
+            total = shifted_sum(taps, cols) + bd_ref[...]
+            out_ref[cycle, row] = total.astype(BF16)
+            edge_ref[cycle, 0, row] = total[:16]
+            edge_ref[cycle, 1, row] = total[cols - 16 :]
+            copies = []
+            if row % 4 == 3:
+                rows = (cycle, pl.ds(row - 3, 4))
+                copies = [(out_ref.at[rows], out_hbm.at[rows])]
+            if row == height - 1:
+                copies.append((edge_ref.at[cycle], edge_hbm.at[cycle]))
+            yield fetch(copies, out_sems.at[cycle, pl.ds(row // 4, len(copies))]) if copies else []
+
+    for _ in prepare(0):
+        pass
+    for cycle in range(cycles):
+        ahead = prepare(cycle + 1) if cycle + 1 < cycles else iter(())
+        for copies in convolve(cycle):
+            leaving += copies
+            next(ahead, None)
+            next(ahead, None)
+        for _ in ahead:
+            pass
+    leaving += fetch([(coarse_ref, coarse_hbm)], out_sems.at[cycles, pl.ds(0, 1)])
     for copy in leaving:
         copy.wait()
 
 
-def seal(coarse_at, fine_at, tab_ref, tile_ref, code_ref, recv_ref, coarse_hbm, edge_hbm, wm_hbm, bm_hbm, u_hbm,
-         bu_hbm, wd_hbm, out_in, out_hbm, coarse_ref, edge_ref, wm_ref, bm_ref, u_ref, bu_ref, wu_ref, ws_ref, out_ref,
+def seal(coarse_at, fine_at, tab_ref, tile_ref, code_ref, recv_hbm, coarse_hbm, edge_hbm, wm_hbm, bm_hbm, u_hbm,
+         bu_hbm, wd_hbm, out_in, out_hbm, recv_ref, coarse_ref, edge_ref, wm_ref, bm_ref, u_ref, bu_ref, wu_ref, ws_ref, out_ref,
          in_sems, out_sems):
     tiles, strips, height = coarse_at.tiles, coarse_at.strips, fine_at.height
     cycles, _, _, _, chans = edge_ref.shape
     cols = out_hbm.shape[2]
     low = height // 2
-    pairs = [(bm_hbm, bm_ref), (bu_hbm, bu_ref), (coarse_hbm, coarse_ref), (wm_hbm, wm_ref), (u_hbm, u_ref)]
+    pairs = [(recv_hbm, recv_ref), (bm_hbm, bm_ref), (bu_hbm, bu_ref), (coarse_hbm, coarse_ref), (wm_hbm, wm_ref), (u_hbm, u_ref)]
     pairs += [(wd_hbm.at[:, :, pl.ds(0, chans)], wu_ref), (edge_hbm, edge_ref)]
     pairs += [(wd_hbm.at[:, 2 * side, pl.ds(chans, chans)], ws_ref.at[side]) for side in range(2)]
     arriving = fetch(pairs, in_sems)
@@ -448,6 +484,7 @@
             sides.append(side_bit)
             flips.append(flip)
             strips_at.append(there)
+    arriving[0].wait()
     got = pick(aligned + taps[0] + taps[1] + taps[2] + skips, recv_ref[...])
     n = 8 * 2 * cycles
     at8 = lax.broadcasted_iota(jnp.int32, (8, chans), 0) - 2
@@ -455,7 +492,7 @@
     def on_face(s):
         return jnp.where(((at8 < 0) & (s == 0)) | ((at8 >= low) & (s == strips - 1)), 0.0, 1.0)
 
-    for copy in arriving[:4]:
+    for copy in arriving[1:5]:
         copy.wait()
     own = got[:n]
     there = got[n : 4 * n]
@@ -473,7 +510,7 @@
     total = jnp.concatenate(mine + [total[n:] + bm_ref[...]], axis=0)
     keep = jnp.concatenate([on_face(s) for s in [strip] * (2 * cycles) + strips_at], axis=0)
     column = (gelu(total) * keep).astype(BF16)
-    arriving[4].wait()
+    arriving[5].wait()
     phases = [
         [((dot(column, u_ref[a, b]) + bu_ref[...]) * keep).astype(BF16) for b in range(2)] for a in range(2)
     ]
@@ -492,7 +529,7 @@
     skip_pad = got[4 * n :]
     m = 16 * cycles
     lines = [[outer[:m], inside[0][:m], inside[1][:m]], [outer[m:], inside[1][m:], inside[0][m:]]]
-    for copy in arriving[5:]:
+    for copy in arriving[6:]:
         copy.wait()
     sums = [[[], [], []], [[], [], []]]
     for row in range(3):
@@ -573,9 +610,13 @@
         return lax.ppermute(x, "tile", far_pairs)
 
     def pack(own, near_tail, far_tail):
-        parts = [own, to_near(near_tail)] + ([] if joint else [to_far(far_tail)])
-        parts = [jnp.broadcast_to(part[None], (members,) + part.shape) for part in parts]
-        return share(jnp.concatenate(parts, axis=1))
+        tails = [to_near(near_tail)] + ([] if joint else [to_far(far_tail)])
+        rows = own.shape[1] - sum(tail.shape[0] for tail in tails)
+        for tail in tails:
+            tail = jnp.broadcast_to(tail[None], (members,) + tail.shape)
+            own = lax.dynamic_update_slice(own, tail, (0, rows, 0))
+            rows += tail.shape[1]
+        return share(own)
 
     seams = (jnp.transpose(seam_tile, (1, 2, 0)), jnp.transpose(seam_code, (1, 2, 0)))
     eb, mb, ub, db = (b.reshape(1, chans) for b in (encoder_bias, middle_bias, upconv_bias, decoder_offset_bias))
@@ -608,10 +649,10 @@
     vector = (1, chans)
     own, near_tail, far_tail, near, far = call(
         functools.partial(lift, spec), "lift",
-        [((columns * height, chans), BF16)] + [((tail1, chans), BF16)] * 2 + [(row_shape, BF16)] * 2,
+        [((members, spec.payload, chans), BF16)] + [((tail1, chans), BF16)] * 2 + [(row_shape, BF16)] * 2,
         [hbm, smem, smem], [hbm] * 5,
         [(edge_shape, BF16), ((2,) + row_shape, BF16), ((columns * height, chans), F32), ((2, tail1, chans), F32),
-         ((columns * height, chans), BF16), ((2, tail1, chans), BF16), dma((4,)), dma((5,))],
+         ((columns * height, chans), BF16), ((2, tail1, chans), BF16), dma((4,)), dma((4 + members,))],
         fields, *seams,
     )
     recv = pack(own, near_tail, far_tail)
@@ -630,12 +671,12 @@
     pool_edges = (2, cycles, low, 16, chans)
     skip, pooled, near, far, own, near_tail, far_tail, table = call(
         functools.partial(mend, spec, coarse_at, fine_at), "mend",
-        [(tall, BF16), (pooled_shape, BF16), (wide, BF16), (wide, BF16), ((own2, chans), BF16)]
+        [(tall, BF16), (pooled_shape, BF16), (wide, BF16), (wide, BF16), ((members, payload, chans), BF16)]
         + [((tail2, chans), BF16)] * 2 + [((members, 128), jnp.int32)],
         [vmem] + [hbm] * 6 + [smem, smem], [hbm] * 8,
         [((2, 3) + square, BF16), (pre_shape, F32), (edge_shape, BF16), (pool_edges, BF16), ((own2, chans), F32),
          ((2, tail2, chans), F32), ((own2, chans), BF16), ((2, tail2, chans), BF16), ((members, 128), jnp.int32),
-         dma((7,)), dma((20,))],
+         dma((7,)), dma((19 + members,))],
         recv.reshape(-1, chans), encoder_weight, skip, pooled, near, far, pre_col, *seams,
         input_output_aliases={2: 0, 3: 1, 4: 2, 5: 3},
     )
@@ -646,20 +687,22 @@
     out, edge, coarse = call(
         functools.partial(decode, tiles), "decode",
         [(tall, BF16), (edges, F32), (coarse_edges, F32)],
-        [hbm, hbm, vmem, vmem] + [hbm] * 6, [hbm, hbm, hbm],
-        [(tall, BF16), (pooled_shape, BF16), (wshape, BF16), (vector, F32), ((2, 2) + square, BF16),
-         (vector, F32), ((3, 6) + square, BF16), (vector, F32), (tall, BF16), (edges, F32), (coarse_edges, F32),
-         ((height, cols, 6 * chans), BF16), ((low + 2, half, 3 * chans), BF16),
-         ((height + 2, chans // 128, cols, 128), F32), dma((12 + cycles,)), dma((cycles + 1, height))],
+        [hbm] * 10, [hbm, hbm, hbm],
+        [(tall, BF16), (pooled_shape, BF16), (wide, BF16), (wide, BF16), (wshape, BF16), (vector, F32),
+         ((2, 2) + square, BF16), (vector, F32), ((3, 6) + square, BF16), (vector, F32), (tall, BF16), (edges, F32),
+         (coarse_edges, F32)]
+        + [((height, cols, 6 * chans), BF16)] * 2 + [((low + 2, half, 3 * chans), BF16)] * 2
+        + [((height + 2, chans // 128, cols, 128), F32)] * 2
+        + [dma((16 + cycles,)), dma((cycles + 1, height // 4 + 1))],
         skip, pooled, near2, far2, middle_weight, mb, upconv_weight, ub, decoder_weight, db,
         cost_estimate=far_cost,
     )
     (out,) = call(
         functools.partial(seal, coarse_at, fine_at), "seal",
         [(tall, BF16)],
-        [smem, smem, smem, vmem] + [hbm] * 8, [hbm],
-        [(coarse_edges, F32), (edges, F32), (wshape, BF16), (vector, F32), ((2, 2) + square, BF16), (vector, F32),
-         (wshape, BF16), ((2, 3) + square, BF16), (edge_shape, BF16), dma((9,)), dma((2,))],
+        [smem, smem, smem] + [hbm] * 9, [hbm],
+        [((members * payload, chans), BF16), (coarse_edges, F32), (edges, F32), (wshape, BF16), (vector, F32), ((2, 2) + square, BF16), (vector, F32),
+         (wshape, BF16), ((2, 3) + square, BF16), (edge_shape, BF16), dma((10,)), dma((2,))],
         table, *seams, recv2.reshape(-1, chans), coarse, edge, middle_weight, mb, upconv_weight, ub, decoder_weight, out,
         input_output_aliases={11: 0},
     )

time: 64.6 us -> 60.5 us (0.937)
  Pallas kernels: 35.6 us -> 34 us
  other arithmetic: 1.54 us -> 0 us
    pallas_call x5, Pallas kernels: 35.6 us -> 34 us  [call(): pl.pallas_call(body, out_shape=[jax.ShapeDtypeStruct(shape, dtype) for sh...]
    broadcast_in_dim x4 -> x0, local copies, waits for them, and re-layouts: 1.59 us -> none  [pack(): jnp.broadcast_to(part[None], (members,) + part.shape)]
    concatenate x2 -> x0, other arithmetic: 1.54 us -> none  [pack(): return share(jnp.concatenate(parts, axis=1))]
    ppermute x4, starting transfers between devices: 4.51 us -> 3.02 us  [to_near(): return lax.ppermute(x, 'tile', near_pairs)]
    dynamic_update_slice x0 -> x2, local copies, waits for them, and re-layouts: none -> 1.31 us  [pack(): own = lax.dynamic_update_slice(own, tail, (0, rows, 0))]
    all_to_all x2, starting transfers between devices: 13.5 us -> 14.7 us  [share(): return lax.all_to_all(x, 'tile', 0, 0, tiled=True, axis_index_groups=groups)]
    ppermute x2, waiting for transfers between devices: 0.29 us -> 1.34 us  [to_far(): return lax.ppermute(x, 'tile', far_pairs)]
    ppermute x4, waiting for transfers between devices: 2.09 us -> 1.06 us  [to_near(): return lax.ppermute(x, 'tile', near_pairs)]
  transfers between devices with their start and end apart: 8 -> 8, of which waited for: 3 -> 2; matrix products, arithmetic and copies ran while one was open for 5% -> 2% of each run, Pallas kernels for 37% -> 37%
where the time goes in v3:
time: 60.5 us; the launch traced here: 60.1 us
  Pallas kernels  34 us (56%)
  starting transfers between devices  20.6 us (34%)
  local copies, waits for them, and re-layouts  2.82 us (5%)
  waiting for transfers between devices  2.4 us (4%)
    pallas_call x5, Pallas kernels, call(): pl.pallas_call(body, out_shape=[jax.ShapeDtypeStruct(shape, dtype) for sh...  34 us
    all_to_all x2, starting transfers between devices, share(): return lax.all_to_all(x, 'tile', 0, 0, tiled=True, axis_index_groups=groups)  14.7 us
    ppermute x4, starting transfers between devices, to_near(): return lax.ppermute(x, 'tile', near_pairs)  3.02 us
    ppermute x2, starting transfers between devices, to_far(): return lax.ppermute(x, 'tile', far_pairs)  2.88 us
    unnamed x8, local copies, waits for them, and re-layouts  1.51 us
    ppermute x2, waiting for transfers between devices, to_far(): return lax.ppermute(x, 'tile', far_pairs)  1.34 us
    dynamic_update_slice x2, local copies, waits for them, and re-layouts, pack(): own = lax.dynamic_update_slice(own, tail, (0, rows, 0))  1.31 us
  transfers between devices with their start and end apart: 8, of which 2 were waited for; matrix products, arithmetic and copies ran while one was open for 2% of the time, Pallas kernels for 37%

profile of v3, /device:TPU:1, one launch (start us, length us, event | category | flops | bytes accessed | tf_op | source)
XLA Modules:
  0.0 60.1 jit_solution(5605014330262656924)
XLA Ops:
  0.0 2.9 %lift.1 = (bf16[8,64,256]{2,1,0:T(8,128)(2,1)}, bf16[16,256]{1,0:T(8,128)(2,1)}, bf16[16,256]{1,0:T(8,128)(2,1)}, bf16[3,128,256]{2,1,0:T(8,128)(2,1)}, bf16[3,128,256]{2,1,0:T(8,128)(2,1)}) custom-call(bf16[3,8,128,256]{3,2,1,0:T(8,128)(2,1)} %x_hbm.3, s32[1,2,3]{2,1,0:T(2,128)} %bitcast.8, s32[1,2,3]{2,1,0:T(2,128)} %bitcast.11), custom_call_target="tpu_custom_call" | custom-call | tf_op jit(solution)/shard_map/lift/pallas_call | solution.py:637
  2.9 0.1 collective-permute-start
  3.0 0.5 collective-permute-start.1
  3.5 2.6 %collective-permute-start.2 = (bf16[3,128,256]{2,1,0:T(8,128)(2,1)}, bf16[3,128,256]{2,1,0:T(8,128)(2,1)S(1)}, u32[]{:S(2)}, u32[]{:S(2)}) collective-permute-start(bf16[3,128,256]{2,1,0:T(8,128)(2,1)} %get-tuple-element.27), channel_id=1, source_target_pairs={{1,2},{2,1},{3,4},{4,3},{5,6},{6,5},{7,8},{8,7},{9,10},{10,9},{11,... | collective-permute-start | bytes 589832 | tf_op jit(solution)/shard_map/ppermute | solution.py:610
  6.1 0.0 collective-permute-done
  6.1 0.6 %broadcast_dynamic-update-slice_fusion.1 = bf16[8,64,256]{2,1,0:T(8,128)(2,1)} fusion(bf16[8,64,256]{2,1,0:T(8,128)(2,1)} %get-tuple-element.24, bf16[16,256]{1,0:T(8,128)(2,1)S(1)} %collective-permute-done), kind=kLoop, calls=%fused_computation.1 | loop fusion | bytes 73728 | tf_op jit(solution)/shard_map/dynamic_update_slice | solution.py:617
  6.7 7.8 %all-to-all-start = ((bf16[8,64,256]{2,1,0:T(8,128)(2,1)}), bf16[8,64,256]{2,1,0:T(8,128)(2,1)}, u32[]{:S(2)}, u32[]{:S(2)}) async-start(bf16[8,64,256]{2,1,0:T(8,128)(2,1)} %broadcast_dynamic-update-slice_fusion.1), calls=%async_computation | async-start | bytes 524288 | tf_op jit(solution)/shard_map/all_to_all | solution.py:592
  14.5 0.0 collective-permute-done.1.near_ref
  14.5 0.0 copy-start.2
  14.5 0.0 collective-permute-done.2.far_ref
  14.5 0.0 copy-start.3
  14.5 0.7 %copy-done.2 = bf16[3,128,256]{2,1,0:T(8,128)(2,1)} copy-done((bf16[3,128,256]{2,1,0:T(8,128)(2,1)}, bf16[3,128,256]{2,1,0:T(8,128)(2,1)S(1)}, u32[]{:S(2)}) %copy-start.2) | copy-done | bytes 196632
  15.2 0.1 copy-done.3
  15.3 8.3 %encode.1 = (bf16[3,8,128,256]{3,2,1,0:T(8,128)(2,1)}, bf16[3,4,64,256]{3,2,1,0:T(8,128)(2,1)}, bf16[3,256,256]{2,1,0:T(8,128)(2,1)}, bf16[3,256,256]{2,1,0:T(8,128)(2,1)}, f32[3,2,8,256]{3,2,1,0:T(8,128)}) custom-call(bf16[3,8,128,256]{3,2,1,0:T(8,128)(2,1)} %x_hbm.3, bf16[3,128,256]{2,1,0:T(8,128)(2,1)} %copy-done.2, bf16[3,128,256]{2,1,0:T(8,128)(2,1)} %copy-done.3, ...), custom_call_target="tpu_custom_call" | custom-call | flops 999999995904 | bytes 1000000000 | tf_op jit(solution)/shard_map/encode/pallas_call | solution.py:637
  23.6 0.0 all-to-all-done
  23.6 4.1 %mend.1 = (bf16[3,8,128,256]{3,2,1,0:T(8,128)(2,1)}, bf16[3,4,64,256]{3,2,1,0:T(8,128)(2,1)}, bf16[3,256,256]{2,1,0:T(8,128)(2,1)}, bf16[3,256,256]{2,1,0:T(8,12...) custom-call(bf16[512,256]{1,0:T(8,128)(2,1)} %bitcast.2.recv_ref, ...), custom_call_target="tpu_custom_call", output_to_operand_aliasing={{0}: (2, {}), {1}: (3, {}), {2}: (4, {}), {3}: (5, {})} | custom-call | tf_op jit(solution)/shard_map/mend/pallas_call | solution.py:637
  27.7 1.1 %collective-permute-start.4 = (bf16[3,256,256]{2,1,0:T(8,128)(2,1)}, bf16[3,256,256]{2,1,0:T(8,128)(2,1)S(1)}, u32[]{:S(2)}, u32[]{:S(2)}) collective-permute-start(bf16[3,256,256]{2,1,0:T(8,128)(2,1)} %get-tuple-element.38), channel_id=1, source_target_pairs={{0,1},{1,0},{2,3},{3,2},{4,5},{5,4},{6,7},{7,6},{8,9},{9,8},{10,11... | collective-permute-start | bytes 1179656 | tf_op jit(solution)/shard_map/ppermute | solution.py:607
  28.8 0.3 collective-permute-start.5
  29.1 1.4 %collective-permute-start.3 = (bf16[32,256]{1,0:T(8,128)(2,1)}, bf16[32,256]{1,0:T(8,128)(2,1)S(1)}, u32[]{:S(2)}, u32[]{:S(2)}) collective-permute-start(bf16[32,256]{1,0:T(8,128)(2,1)} %get-tuple-element.35), channel_id=1, source_target_pairs={{0,1},{1,0},{2,3},{3,2},{4,5},{5,4},{6,7},{7,6},{8,9},{9,8},{10,11... | collective-permute-start | bytes 49160 | tf_op jit(solution)/shard_map/ppermute | solution.py:607
  30.4 1.0 %collective-permute-done.3 = bf16[32,256]{1,0:T(8,128)(2,1)S(1)} collective-permute-done((bf16[32,256]{1,0:T(8,128)(2,1)}, bf16[32,256]{1,0:T(8,128)(2,1)S(1)}, u32[]{:S(2)}, u32[]{:S(2)}) %collective-permute-start.3) | collective-permute-done | bytes 16416 | tf_op jit(solution)/shard_map/ppermute | solution.py:607
  31.5 0.7 %broadcast_dynamic-update-slice_fusion = bf16[8,128,256]{2,1,0:T(8,128)(2,1)} fusion(bf16[8,128,256]{2,1,0:T(8,128)(2,1)} %get-tuple-element.34, bf16[32,256]{1,0:T(8,128)(2,1)S(1)} %collective-permute-done.3), kind=kLoop, calls=%fused_computation | loop fusion | bytes 147456 | tf_op jit(solution)/shard_map/dynamic_update_slice | solution.py:617
  32.2 6.9 %all-to-all-start.1 = ((bf16[8,128,256]{2,1,0:T(8,128)(2,1)}), bf16[8,128,256]{2,1,0:T(8,128)(2,1)}, u32[]{:S(2)}, u32[]{:S(2)}) async-start(bf16[8,128,256]{2,1,0:T(8,128)(2,1)} %broadcast_dynamic-update-slice_fusion), calls=%async_computation.1 | async-start | bytes 1048576 | tf_op jit(solution)/shard_map/all_to_all | solution.py:592
  39.1 0.0 collective-permute-done.4.near_hbm
  39.1 0.0 copy-start
  39.1 1.3 %collective-permute-done.5.far_hbm = bf16[3,256,256]{2,1,0:T(8,128)(2,1)S(1)} collective-permute-done((bf16[3,256,256]{2,1,0:T(8,128)(2,1)}, bf16[3,256,256]{2,1,0:T(8,128)(2,1)S(1)}, u32[]{:S(2)}, u32[]{:S(2)}) %collective-permute-start.5) | collective-permute-done | bytes 393248 | tf_op jit(solution)/shard_map/ppermute | solution.py:610
  40.4 0.0 copy-start.1
  40.4 0.0 copy-done
  40.4 0.8 %copy-done.1 = bf16[3,256,256]{2,1,0:T(8,128)(2,1)} copy-done((bf16[3,256,256]{2,1,0:T(8,128)(2,1)}, bf16[3,256,256]{2,1,0:T(8,128)(2,1)S(1)}, u32[]{:S(2)}) %copy-start.1) | copy-done | bytes 393240
  41.2 13.9 %decode.1 = (bf16[3,8,128,256]{3,2,1,0:T(8,128)(2,1)}, f32[3,2,8,16,256]{4,3,2,1,0:T(8,128)}, f32[3,2,8,256]{3,2,1,0:T(8,128)}) custom-call(bf16[3,8,128,256]{3,2,1,0:T(8,128)(2,1)} %get-tuple-element.36.skip_hbm, bf16[3,4,64,256]{3,2,1,0:T(8,128)(2,1)} %get-tuple-element.37.pooled_hbm, bf16[3,256,256]{2,1,0:T(8,128)(2,1)} %copy-done, ...), custom_call_target="tpu_custom_call" | custom-call | flops 999999995904 | bytes 1000000000 | tf_op jit(solution)/shard_map/decode/pallas_call | solution.py:637
  55.1 0.0 all-to-all-done.1
  55.1 4.8 %seal.1 = bf16[3,8,128,256]{3,2,1,0:T(8,128)(2,1)} custom-call(s32[8,128]{1,0:T(8,128)} %get-tuple-element.33.tab_ref, s32[1,2,3]{2,1,0:T(2,128)} %bitcast.10, s32[1,2,3]{2,1,0:T(2,128)} %bitcast.13, bf16[1024,256]{1,0:T(8,128)(2,1)} %bitcast.4.recv_hbm, f32[3,2,8,256]{3,2,1,0:T(8,128)} %get-tuple-element.40.coarse_hbm, ...), custom_call_target="tpu_custom_call", output_to_operand_aliasing={{}: (11, {})} | custom-call | tf_op jit(solution)/shard_map/seal/pallas_call | solution.py:637
Async XLA Ops:
  2.9 3.2 %collective-permute-start = (bf16[16,256]{1,0:T(8,128)(2,1)}, bf16[16,256]{1,0:T(8,128)(2,1)S(1)}, u32[]{:S(2)}, u32[]{:S(2)}) collective-permute-start(bf16[16,256]{1,0:T(8,128)(2,1)} %get-tuple-element.25), channel_id=1, source_target_pairs={{0,1},{1,0},{2,3},{3,2},{4,5},{5,4},{6,7},{7,6},{8,9},{9,8},{10,11... | collective-permute-start | bytes 24584 | tf_op jit(solution)/shard_map/ppermute | solution.py:607
  3.0 11.5 %collective-permute-start.1 = (bf16[3,128,256]{2,1,0:T(8,128)(2,1)}, bf16[3,128,256]{2,1,0:T(8,128)(2,1)S(1)}, u32[]{:S(2)}, u32[]{:S(2)}) collective-permute-start(bf16[3,128,256]{2,1,0:T(8,128)(2,1)} %get-tuple-element.26), channel_id=1, source_target_pairs={{0,1},{1,0},{2,3},{3,2},{4,5},{5,4},{6,7},{7,6},{8,9},{9,8},{10,11... | collective-permute-start | bytes 589832 | tf_op jit(solution)/shard_map/ppermute | solution.py:607
  3.5 11.1 %collective-permute-start.2 = (bf16[3,128,256]{2,1,0:T(8,128)(2,1)}, bf16[3,128,256]{2,1,0:T(8,128)(2,1)S(1)}, u32[]{:S(2)}, u32[]{:S(2)}) collective-permute-start(bf16[3,128,256]{2,1,0:T(8,128)(2,1)} %get-tuple-element.27), channel_id=1, source_target_pairs={{1,2},{2,1},{3,4},{4,3},{5,6},{6,5},{7,8},{8,7},{9,10},{10,9},{11,... | collective-permute-start | bytes 589832 | tf_op jit(solution)/shard_map/ppermute | solution.py:610
  6.7 16.9 %all-to-all-start = ((bf16[8,64,256]{2,1,0:T(8,128)(2,1)}), bf16[8,64,256]{2,1,0:T(8,128)(2,1)}, u32[]{:S(2)}, u32[]{:S(2)}) async-start(bf16[8,64,256]{2,1,0:T(8,128)(2,1)} %broadcast_dynamic-update-slice_fusion.1), calls=%async_computation | async-start | bytes 524288 | tf_op jit(solution)/shard_map/all_to_all | solution.py:592
  14.5 0.7 %copy-start.2 = (bf16[3,128,256]{2,1,0:T(8,128)(2,1)}, bf16[3,128,256]{2,1,0:T(8,128)(2,1)S(1)}, u32[]{:S(2)}) copy-start(bf16[3,128,256]{2,1,0:T(8,128)(2,1)S(1)} %collective-permute-done.1.near_ref) | copy-start | bytes 589828
  14.5 0.7 %copy-start.3 = (bf16[3,128,256]{2,1,0:T(8,128)(2,1)}, bf16[3,128,256]{2,1,0:T(8,128)(2,1)S(1)}, u32[]{:S(2)}) copy-start(bf16[3,128,256]{2,1,0:T(8,128)(2,1)S(1)} %collective-permute-done.2.far_ref) | copy-start | bytes 589828
  27.7 11.4 %collective-permute-start.4 = (bf16[3,256,256]{2,1,0:T(8,128)(2,1)}, bf16[3,256,256]{2,1,0:T(8,128)(2,1)S(1)}, u32[]{:S(2)}, u32[]{:S(2)}) collective-permute-start(bf16[3,256,256]{2,1,0:T(8,128)(2,1)} %get-tuple-element.38), channel_id=1, source_target_pairs={{0,1},{1,0},{2,3},{3,2},{4,5},{5,4},{6,7},{7,6},{8,9},{9,8},{10,11... | collective-permute-start | bytes 1179656 | tf_op jit(solution)/shard_map/ppermute | solution.py:607
  28.8 11.6 %collective-permute-start.5 = (bf16[3,256,256]{2,1,0:T(8,128)(2,1)}, bf16[3,256,256]{2,1,0:T(8,128)(2,1)S(1)}, u32[]{:S(2)}, u32[]{:S(2)}) collective-permute-start(bf16[3,256,256]{2,1,0:T(8,128)(2,1)} %get-tuple-element.39), channel_id=1, source_target_pairs={{1,2},{2,1},{3,4},{4,3},{5,6},{6,5},{7,8},{8,7},{9,10},{10,9},{11,... | collective-permute-start | bytes 1179656 | tf_op jit(solution)/shard_map/ppermute | solution.py:610
  29.1 2.4 %collective-permute-start.3 = (bf16[32,256]{1,0:T(8,128)(2,1)}, bf16[32,256]{1,0:T(8,128)(2,1)S(1)}, u32[]{:S(2)}, u32[]{:S(2)}) collective-permute-start(bf16[32,256]{1,0:T(8,128)(2,1)} %get-tuple-element.35), channel_id=1, source_target_pairs={{0,1},{1,0},{2,3},{3,2},{4,5},{5,4},{6,7},{7,6},{8,9},{9,8},{10,11... | collective-permute-start | bytes 49160 | tf_op jit(solution)/shard_map/ppermute | solution.py:607
  32.2 22.9 %all-to-all-start.1 = ((bf16[8,128,256]{2,1,0:T(8,128)(2,1)}), bf16[8,128,256]{2,1,0:T(8,128)(2,1)}, u32[]{:S(2)}, u32[]{:S(2)}) async-start(bf16[8,128,256]{2,1,0:T(8,128)(2,1)} %broadcast_dynamic-update-slice_fusion), calls=%async_computation.1 | async-start | bytes 1048576 | tf_op jit(solution)/shard_map/all_to_all | solution.py:592
  39.1 1.3 %copy-start = (bf16[3,256,256]{2,1,0:T(8,128)(2,1)}, bf16[3,256,256]{2,1,0:T(8,128)(2,1)S(1)}, u32[]{:S(2)}) copy-start(bf16[3,256,256]{2,1,0:T(8,128)(2,1)S(1)} %collective-permute-done.4.near_hbm) | copy-start | bytes 1179652
  40.4 0.8 %copy-start.1 = (bf16[3,256,256]{2,1,0:T(8,128)(2,1)}, bf16[3,256,256]{2,1,0:T(8,128)(2,1)S(1)}, u32[]{:S(2)}) copy-start(bf16[3,256,256]{2,1,0:T(8,128)(2,1)S(1)} %collective-permute-done.5.far_hbm) | copy-start | bytes 1179652

commit v4 on v3

--- a/solution.py
+++ b/solution.py
@@ -132,24 +132,16 @@
     return sum(parts[tap][at + tap : at + tap + height] for tap in range(3))
 
 
-def lift(layout, x_hbm, tile_ref, code_ref, own_hbm, near_tail_hbm, far_tail_hbm, near_hbm, far_hbm,
-         edges, rows, own, tails, own16, tails16, in_sems, out_sems):
+def lift(layout, x_hbm, tile_hbm, code_hbm, own_hbm, near_tail_hbm, far_tail_hbm, near_hbm, far_hbm,
+         edges, rows, own, tails, own16, tails16, tile_ref, code_ref, in_sems, out_sems):
     height = layout.height
     cycles, cols = x_hbm.shape[0], x_hbm.shape[2]
     upper = lax.rem(strip_of(layout.tiles), 2) * (height - 1)
     nearest = (height - 1 - upper, upper)
     pairs = [(x_hbm.at[:, :, pl.ds(first, 16)], edges.at[side]) for side, first in enumerate((0, cols - 16))]
-    arriving = fetch(pairs + [(x_hbm.at[:, nearest[k]], rows.at[k]) for k in range(2)], in_sems)
-    lanes = lax.broadcasted_iota(jnp.int32, (1, own.shape[1]), 1)
-    noted = jnp.zeros((1, own.shape[1]), F32)
-    for cycle in range(cycles):
-        for side in range(2):
-            other, face, side_bit, flip = seam_of(tile_ref, code_ref, layout.tiles, cycle, side)
-            number = (other * FACES + face) * 4 + flip * 2 + side_bit
-            noted = jnp.where(lanes == cycle * 2 + side, number.astype(F32), noted)
+    pairs += [(x_hbm.at[:, nearest[k]], rows.at[k]) for k in range(2)]
+    arriving = fetch(pairs + [(tile_hbm, tile_ref), (code_hbm, code_ref)], in_sems)
     tails[...] = jnp.zeros_like(tails)
-    for k in range(2):
-        tails[k, layout.columns : layout.columns + 1] = noted
     for side in range(2):
         arriving[side].wait()
         at = 15 * side
@@ -161,11 +153,22 @@
             for k in range(2):
                 value = edges[side, cycle, nearest[k]].astype(F32)[at : at + 1]
                 tails[k, column : column + 1] = value
+    for copy in arriving[4:]:
+        copy.wait()
+    lanes = lax.broadcasted_iota(jnp.int32, (1, own.shape[1]), 1)
+    noted = jnp.zeros((1, own.shape[1]), F32)
+    for cycle in range(cycles):
+        for side in range(2):
+            other, face, side_bit, flip = seam_of(tile_ref, code_ref, layout.tiles, cycle, side)
+            number = (other * FACES + face) * 4 + flip * 2 + side_bit
+            noted = jnp.where(lanes == cycle * 2 + side, number.astype(F32), noted)
+    for k in range(2):
+        tails[k, layout.columns : layout.columns + 1] = noted
     own16[...] = own[...].astype(BF16)
     tails16[...] = tails[...].astype(BF16)
     pairs = [(tails16.at[0], near_tail_hbm), (tails16.at[1], far_tail_hbm)]
     pairs += [(own16, own_hbm.at[k, pl.ds(0, own16.shape[0])]) for k in range(2 * FACES)]
-    for copy in arriving[2:]:
+    for copy in arriving[2:4]:
         copy.wait()
     leaving = fetch(pairs + [(rows.at[0], near_hbm), (rows.at[1], far_hbm)], out_sems)
     for copy in leaving:
@@ -179,33 +182,33 @@
     return copies
 
 
-def encode(tiles, x_hbm, near_ref, far_ref, w_hbm, b_hbm, skip_hbm, pooled_hbm, near_hbm, far_hbm, pre_hbm,
-           x_ref, w_ref, b_ref, stacked, skip_ref, pooled_ref, rows_ref, pre_ref, paired, in_sems, out_sems):
+def encode(tiles, x_hbm, near_in, far_in, w_hbm, b_hbm, skip_hbm, pooled_hbm, near_hbm, far_hbm, pre_hbm,
+           x_ref, near_ref, far_ref, w_ref, b_ref, stacked, skip_ref, pooled_ref, rows_ref, pre_ref, paired, in_sems, out_sems):
     cycles, height, cols, chans = x_ref.shape
     half = cols // 2
-    pairs = [(b_hbm, b_ref), (x_hbm.at[0], x_ref.at[0])]
+    pairs = [(x_hbm.at[0], x_ref.at[0]), (near_in, near_ref), (far_in, far_ref), (b_hbm, b_ref)]
     pairs += [(w_hbm.at[:, tap], w_ref.at[tap]) for tap in range(3)]
-    arriving = fetch(pairs, in_sems.at[pl.ds(0, 5)])
+    arriving = fetch(pairs, in_sems.at[pl.ds(0, 7)])
     strip = strip_of(tiles)
     odd = lax.rem(strip, 2)
     ends = (strip == 0) | (strip == tiles // FACES - 1)
-    arriving[0].wait()
-    arriving[1].wait()
+    for copy in arriving[:4]:
+        copy.wait()
     leaving = []
     for cycle in range(cycles):
         if cycle > 0:
-            arriving[4 + cycle].wait()
+            arriving[6 + cycle].wait()
         top, bottom = top_and_bottom(near_ref[cycle], far_ref[cycle], odd, ends)
         stack_taps(stacked, halo_rows(x_ref.at[cycle], top, bottom), height)
         for row in range(height):
             taps = []
             for tap in range(3):
                 if cycle == 0 and row == 0:
-                    arriving[2 + tap].wait()
+                    arriving[4 + tap].wait()
                 taps.append(dot(stacked[row], w_ref[tap].reshape(3 * chans, chans)))
             if cycle == 0 and row == 0:
                 pairs = [(x_hbm.at[k], x_ref.at[k]) for k in range(1, cycles)]
-                arriving += fetch(pairs, in_sems.at[pl.ds(5, cycles - 1)])
+                arriving += fetch(pairs, in_sems.at[pl.ds(7, cycles - 1)])
             total = shifted_sum(taps, cols) + b_ref[...]
             value = gelu(total).astype(BF16)
             skip_ref[cycle, row] = value
@@ -234,13 +237,14 @@
         copy.wait()
 
 
-def mend(layout, coarse, fine, recv_ref, w_hbm, skip_in, pooled_in, near_in, far_in, pre_hbm, tile_ref, code_ref,
+def mend(layout, coarse, fine, recv_ref, w_hbm, skip_in, pooled_in, near_in, far_in, pre_hbm, tile_hbm, code_hbm,
          skip_hbm, pooled_hbm, near_hbm, far_hbm, own_hbm, near_tail_hbm, far_tail_hbm, table_hbm,
-         w_ref, pre_ref, edges, pools, own, tails, own16, tails16, table_ref, in_sems, out_sems):
+         w_ref, pre_ref, edges, pools, own, tails, own16, tails16, table_ref, tile_ref, code_ref, in_sems, out_sems):
     tiles, height, low = layout.tiles, layout.height, coarse.height
     cycles, cols, chans = skip_in.shape[0], skip_in.shape[2], skip_in.shape[3]
     half = cols // 2
-    pairs = [(w_hbm.at[:, 2 * side], w_ref.at[side]) for side in range(2)] + [(pre_hbm, pre_ref)]
+    pairs = [(tile_hbm, tile_ref), (code_hbm, code_ref)]
+    pairs += [(w_hbm.at[:, 2 * side], w_ref.at[side]) for side in range(2)] + [(pre_hbm, pre_ref)]
     for side in range(2):
         pairs.append((skip_in.at[:, :, pl.ds((cols - 16) * side, 16)], edges.at[side]))
         pairs.append((pooled_in.at[:, :, pl.ds((half - 16) * side, 16)], pools.at[side]))
@@ -249,6 +253,8 @@
     odd = lax.rem(strip, 2)
     row_iota = rows_iota(16) - 1
     targets = []
+    for copy in arriving[:2]:
+        copy.wait()
     for side in range(2):
         for cycle in range(cycles):
             other, face, side_bit, flip = seam_of(tile_ref, code_ref, tiles, cycle, side)
@@ -261,14 +267,14 @@
         block = recv_ref[at : at + 16, :128].astype(F32)
         table_ref[member : member + 1] = block[noted % 16 : noted % 16 + 1].astype(jnp.int32)
     part = pads.shape[0] // 2
-    for copy in arriving[:3]:
+    for copy in arriving[2:5]:
         copy.wait()
     seams = [
         [dot(pads[side * part : (side + 1) * part], w_ref[side, tap]) for tap in range(3)] for side in range(2)
     ]
     iota16 = lax.broadcasted_iota(jnp.int32, (16, chans), 0)
     tails[...] = jnp.zeros_like(tails)
-    for copy in arriving[3:]:
+    for copy in arriving[5:]:
         copy.wait()
     at_top = (odd == 1, odd == 0)
     skip_at = [jnp.where(t, 0, height - 1) for t in at_top]
@@ -328,7 +334,8 @@
     strips = tiles // FACES
     cycles, height, cols, chans = skip_ref.shape
     low, half = height // 2, cols // 2
-    pairs = [(near_hbm, near_ref), (far_hbm, far_ref), (pooled_hbm, pooled_ref), (bm_hbm, bm_ref)]
+    halos = ((near_hbm, near_ref), (far_hbm, far_ref), (pooled_hbm, pooled_ref))
+    pairs = [(src.at[0], dst.at[0]) for src, dst in halos] + [(bm_hbm, bm_ref)]
     pairs += [(wm_hbm.at[:, tap], wm_ref.at[tap]) for tap in range(3)]
     pairs += [(bu_hbm, bu_ref), (u_hbm, u_ref), (skip_hbm.at[0], skip_ref.at[0]), (bd_hbm, bd_ref)]
     for tap in range(3):
@@ -336,6 +343,8 @@
             source = wd_hbm.at[:, tap, pl.ds(part * chans, chans)]
             pairs.append((source, wd_ref.at[tap, pl.ds(3 * part, 3)]))
     pairs += [(skip_hbm.at[cycle], skip_ref.at[cycle]) for cycle in range(1, cycles)]
+    rest = pl.ds(1, cycles - 1)
+    pairs += [(src.at[rest], dst.at[rest]) for src, dst in halos]
     arriving = fetch(pairs, in_sems)
     strip = strip_of(tiles)
     odd = lax.rem(strip, 2)
@@ -349,6 +358,9 @@
         copy.wait()
 
     def prepare(cycle):
+        if cycle == 1:
+            for copy in arriving[16 + cycles :]:
+                copy.wait()
         top, bottom = top_and_bottom(near_ref[cycle], far_ref[cycle], odd, ends)
         stacked, upper, joined = (stacked_a, upper_a, joined_a) if cycle % 2 == 0 else (stacked_b, upper_b, joined_b)
 
@@ -447,9 +459,9 @@
         copy.wait()
 
 
-def seal(coarse_at, fine_at, tab_ref, tile_ref, code_ref, recv_hbm, coarse_hbm, edge_hbm, wm_hbm, bm_hbm, u_hbm,
+def seal(coarse_at, fine_at, tab_hbm, tile_hbm, code_hbm, recv_hbm, coarse_hbm, edge_hbm, wm_hbm, bm_hbm, u_hbm,
          bu_hbm, wd_hbm, out_in, out_hbm, recv_ref, coarse_ref, edge_ref, wm_ref, bm_ref, u_ref, bu_ref, wu_ref, ws_ref, out_ref,
-         in_sems, out_sems):
+         tab_ref, tile_ref, code_ref, in_sems, out_sems):
     tiles, strips, height = coarse_at.tiles, coarse_at.strips, fine_at.height
     cycles, _, _, _, chans = edge_ref.shape
     cols = out_hbm.shape[2]
@@ -457,7 +469,10 @@
     pairs = [(recv_hbm, recv_ref), (bm_hbm, bm_ref), (bu_hbm, bu_ref), (coarse_hbm, coarse_ref), (wm_hbm, wm_ref), (u_hbm, u_ref)]
     pairs += [(wd_hbm.at[:, :, pl.ds(0, chans)], wu_ref), (edge_hbm, edge_ref)]
     pairs += [(wd_hbm.at[:, 2 * side, pl.ds(chans, chans)], ws_ref.at[side]) for side in range(2)]
-    arriving = fetch(pairs, in_sems)
+    seams = fetch([(tab_hbm, tab_ref), (tile_hbm, tile_ref), (code_hbm, code_ref)], in_sems.at[pl.ds(10, 3)])
+    arriving = fetch(pairs, in_sems.at[pl.ds(0, 10)])
+    for copy in seams:
+        copy.wait()
     strip = strip_of(tiles)
     rows8 = rows_iota(8) - 2
     rows16 = rows_iota(16) - 1
@@ -609,21 +624,21 @@
     def to_far(x):
         return lax.ppermute(x, "tile", far_pairs)
 
-    def pack(own, near_tail, far_tail):
+    def pack(own, near_tail, far_tail, near):
         tails = [to_near(near_tail)] + ([] if joint else [to_far(far_tail)])
         rows = own.shape[1] - sum(tail.shape[0] for tail in tails)
         for tail in tails:
             tail = jnp.broadcast_to(tail[None], (members,) + tail.shape)
             own = lax.dynamic_update_slice(own, tail, (0, rows, 0))
             rows += tail.shape[1]
-        return share(own)
+        return share(own), to_near(near)
 
     seams = (jnp.transpose(seam_tile, (1, 2, 0)), jnp.transpose(seam_code, (1, 2, 0)))
     eb, mb, ub, db = (b.reshape(1, chans) for b in (encoder_bias, middle_bias, upconv_bias, decoder_offset_bias))
 
     hbm = pl.BlockSpec(memory_space=pltpu.HBM)
     vmem = pl.BlockSpec(memory_space=pltpu.VMEM)
-    smem = pl.BlockSpec(memory_space=pltpu.SMEM)
+    seam_scratch = [pltpu.SMEM((1, 2, cycles), jnp.int32)] * 2
     dma = pltpu.SemaphoreType.DMA
     tall = (cycles, height, cols, chans)
     row_shape = (cycles, cols, chans)
@@ -650,21 +665,21 @@
     own, near_tail, far_tail, near, far = call(
         functools.partial(lift, spec), "lift",
         [((members, spec.payload, chans), BF16)] + [((tail1, chans), BF16)] * 2 + [(row_shape, BF16)] * 2,
-        [hbm, smem, smem], [hbm] * 5,
+        [hbm] * 3, [hbm] * 5,
         [(edge_shape, BF16), ((2,) + row_shape, BF16), ((columns * height, chans), F32), ((2, tail1, chans), F32),
-         ((columns * height, chans), BF16), ((2, tail1, chans), BF16), dma((4,)), dma((4 + members,))],
+         ((columns * height, chans), BF16), ((2, tail1, chans), BF16), *seam_scratch, dma((6,)), dma((4 + members,))],
         fields, *seams,
     )
-    recv = pack(own, near_tail, far_tail)
-    near, far = to_near(near), to_far(far)
+    recv, near = pack(own, near_tail, far_tail, near)
+    far = to_far(far)
     pre_shape = (cycles, 2, height, chans)
     skip, pooled, near, far, pre_col = call(
         functools.partial(encode, tiles), "encode",
         [(tall, BF16), (pooled_shape, BF16), (wide, BF16), (wide, BF16), (pre_shape, F32)],
-        [hbm, vmem, vmem, hbm, hbm], [hbm] * 5,
-        [(tall, BF16), (wshape, BF16), (vector, F32), ((height, cols, 3 * chans), BF16), (tall, BF16),
+        [hbm] * 5, [hbm] * 5,
+        [(tall, BF16), (row_shape, BF16), (row_shape, BF16), (wshape, BF16), (vector, F32), ((height, cols, 3 * chans), BF16), (tall, BF16),
          (pooled_shape, BF16), ((2,) + wide, BF16), (pre_shape, F32), ((cols, 128), F32),
-         dma((4 + cycles,)), dma((cycles, height // 4 + 4))],
+         dma((6 + cycles,)), dma((cycles, height // 4 + 4))],
         fields, near, far, encoder_weight, eb,
         cost_estimate=far_cost,
     )
@@ -673,15 +688,15 @@
         functools.partial(mend, spec, coarse_at, fine_at), "mend",
         [(tall, BF16), (pooled_shape, BF16), (wide, BF16), (wide, BF16), ((members, payload, chans), BF16)]
         + [((tail2, chans), BF16)] * 2 + [((members, 128), jnp.int32)],
-        [vmem] + [hbm] * 6 + [smem, smem], [hbm] * 8,
+        [vmem] + [hbm] * 8, [hbm] * 8,
         [((2, 3) + square, BF16), (pre_shape, F32), (edge_shape, BF16), (pool_edges, BF16), ((own2, chans), F32),
          ((2, tail2, chans), F32), ((own2, chans), BF16), ((2, tail2, chans), BF16), ((members, 128), jnp.int32),
-         dma((7,)), dma((19 + members,))],
+         *seam_scratch, dma((9,)), dma((19 + members,))],
         recv.reshape(-1, chans), encoder_weight, skip, pooled, near, far, pre_col, *seams,
         input_output_aliases={2: 0, 3: 1, 4: 2, 5: 3},
     )
-    recv2 = pack(own, near_tail, far_tail)
-    near2, far2 = to_near(near), to_far(far)
+    recv2, near2 = pack(own, near_tail, far_tail, near)
+    far2 = to_far(far)
     edges = (cycles, 2, height, 16, chans)
     coarse_edges = (cycles, 2, 8, chans)
     out, edge, coarse = call(
@@ -693,16 +708,17 @@
          (coarse_edges, F32)]
         + [((height, cols, 6 * chans), BF16)] * 2 + [((low + 2, half, 3 * chans), BF16)] * 2
         + [((height + 2, chans // 128, cols, 128), F32)] * 2
-        + [dma((16 + cycles,)), dma((cycles + 1, height // 4 + 1))],
+        + [dma((19 + cycles,)), dma((cycles + 1, height // 4 + 1))],
         skip, pooled, near2, far2, middle_weight, mb, upconv_weight, ub, decoder_weight, db,
         cost_estimate=far_cost,
     )
     (out,) = call(
         functools.partial(seal, coarse_at, fine_at), "seal",
         [(tall, BF16)],
-        [smem, smem, smem] + [hbm] * 9, [hbm],
+        [hbm] * 12, [hbm],
         [((members * payload, chans), BF16), (coarse_edges, F32), (edges, F32), (wshape, BF16), (vector, F32), ((2, 2) + square, BF16), (vector, F32),
-         (wshape, BF16), ((2, 3) + square, BF16), (edge_shape, BF16), dma((10,)), dma((2,))],
+         (wshape, BF16), ((2, 3) + square, BF16), (edge_shape, BF16),
+         pltpu.SMEM((members, 128), jnp.int32), *seam_scratch, dma((13,)), dma((2,))],
         table, *seams, recv2.reshape(-1, chans), coarse, edge, middle_weight, mb, upconv_weight, ub, decoder_weight, out,
         input_output_aliases={11: 0},
     )

time: 60.5 us -> 58.1 us (0.960)
  Pallas kernels: 34 us -> 31.6 us
    pallas_call x5, Pallas kernels: 34 us -> 31.6 us  [call(): pl.pallas_call(body, out_shape=[jax.ShapeDtypeStruct(shape, dtype) for sh...]
where the time goes in v4:
time: 58.1 us; the launch traced here: 57.7 us
  Pallas kernels  31.6 us (54%)
  starting transfers between devices  20.6 us (35%)
  local copies, waits for them, and re-layouts  2.82 us (5%)
  waiting for transfers between devices  2.4 us (4%)
    pallas_call x5, Pallas kernels, call(): pl.pallas_call(body, out_shape=[jax.ShapeDtypeStruct(shape, dtype) for sh...  31.6 us
    all_to_all x2, starting transfers between devices, share(): return lax.all_to_all(x, 'tile', 0, 0, tiled=True, axis_index_groups=groups)  14.7 us
    ppermute x4, starting transfers between devices, to_near(): return lax.ppermute(x, 'tile', near_pairs)  3.03 us
    ppermute x2, starting transfers between devices, to_far(): return lax.ppermute(x, 'tile', far_pairs)  2.88 us
    unnamed x8, local copies, waits for them, and re-layouts  1.51 us
    ppermute x2, waiting for transfers between devices, to_far(): return lax.ppermute(x, 'tile', far_pairs)  1.34 us
    dynamic_update_slice x2, local copies, waits for them, and re-layouts, pack(): own = lax.dynamic_update_slice(own, tail, (0, rows, 0))  1.31 us
  transfers between devices with their start and end apart: 8, of which 2 were waited for; matrix products, arithmetic and copies ran while one was open for 2% of the time, Pallas kernels for 37%

profile of v4, /device:TPU:1, one launch (start us, length us, event | category | flops | bytes accessed | tf_op | source)
XLA Modules:
  0.0 57.7 jit_solution(12736337329856648051)
XLA Ops:
  0.0 2.2 %lift.1 = (bf16[8,64,256]{2,1,0:T(8,128)(2,1)}, bf16[16,256]{1,0:T(8,128)(2,1)}, bf16[16,256]{1,0:T(8,128)(2,1)}, bf16[3,128,256]{2,1,0:T(8,128)(2,1)}, bf16[3,128,256]{2,1,0:T(8,128)(2,1)}) custom-call(bf16[3,8,128,256]{3,2,1,0:T(8,128)(2,1)} %x_hbm.3, s32[1,2,3]{2,1,0:T(2,128)} %bitcast.8, s32[1,2,3]{2,1,0:T(2,128)} %bitcast.11), custom_call_target="tpu_custom_call" | custom-call | tf_op jit(solution)/shard_map/lift/pallas_call | solution.py:652
  2.2 0.1 collective-permute-start
  2.3 0.5 collective-permute-start.1
  2.8 2.6 %collective-permute-start.2 = (bf16[3,128,256]{2,1,0:T(8,128)(2,1)}, bf16[3,128,256]{2,1,0:T(8,128)(2,1)S(1)}, u32[]{:S(2)}, u32[]{:S(2)}) collective-permute-start(bf16[3,128,256]{2,1,0:T(8,128)(2,1)} %get-tuple-element.27), channel_id=1, source_target_pairs={{1,2},{2,1},{3,4},{4,3},{5,6},{6,5},{7,8},{8,7},{9,10},{10,9},{11,... | collective-permute-start | bytes 589832 | tf_op jit(solution)/shard_map/ppermute | solution.py:625
  5.4 0.0 collective-permute-done
  5.4 0.6 %broadcast_dynamic-update-slice_fusion.1 = bf16[8,64,256]{2,1,0:T(8,128)(2,1)} fusion(bf16[8,64,256]{2,1,0:T(8,128)(2,1)} %get-tuple-element.24, bf16[16,256]{1,0:T(8,128)(2,1)S(1)} %collective-permute-done), kind=kLoop, calls=%fused_computation.1 | loop fusion | bytes 73728 | tf_op jit(solution)/shard_map/dynamic_update_slice | solution.py:632
  6.0 7.8 %all-to-all-start = ((bf16[8,64,256]{2,1,0:T(8,128)(2,1)}), bf16[8,64,256]{2,1,0:T(8,128)(2,1)}, u32[]{:S(2)}, u32[]{:S(2)}) async-start(bf16[8,64,256]{2,1,0:T(8,128)(2,1)} %broadcast_dynamic-update-slice_fusion.1), calls=%async_computation | async-start | bytes 524288 | tf_op jit(solution)/shard_map/all_to_all | solution.py:607
  13.8 0.0 collective-permute-done.1.near_in
  13.8 0.0 copy-start.2
  13.8 0.0 collective-permute-done.2.far_in
  13.8 0.0 copy-start.3
  13.9 0.7 %copy-done.2 = bf16[3,128,256]{2,1,0:T(8,128)(2,1)} copy-done((bf16[3,128,256]{2,1,0:T(8,128)(2,1)}, bf16[3,128,256]{2,1,0:T(8,128)(2,1)S(1)}, u32[]{:S(2)}) %copy-start.2) | copy-done | bytes 196632
  14.5 0.1 copy-done.3
  14.6 7.4 %encode.1 = (bf16[3,8,128,256]{3,2,1,0:T(8,128)(2,1)}, bf16[3,4,64,256]{3,2,1,0:T(8,128)(2,1)}, bf16[3,256,256]{2,1,0:T(8,128)(2,1)}, bf16[3,256,256]{2,1,0:T(8,128)(2,1)}, f32[3,2,8,256]{3,2,1,0:T(8,128)}) custom-call(bf16[3,8,128,256]{3,2,1,0:T(8,128)(2,1)} %x_hbm.3, bf16[3,128,256]{2,1,0:T(8,128)(2,1)} %copy-done.2, bf16[3,128,256]{2,1,0:T(8,128)(2,1)} %copy-done.3, ...), custom_call_target="tpu_custom_call" | custom-call | flops 999999995904 | bytes 1000000000 | tf_op jit(solution)/shard_map/encode/pallas_call | solution.py:652
  22.0 0.0 all-to-all-done
  22.1 4.0 %mend.1 = (bf16[3,8,128,256]{3,2,1,0:T(8,128)(2,1)}, bf16[3,4,64,256]{3,2,1,0:T(8,128)(2,1)}, bf16[3,256,256]{2,1,0:T(8,128)(2,1)}, bf16[3,256,256]{2,1,0:T(8,12...) custom-call(bf16[512,256]{1,0:T(8,128)(2,1)} %bitcast.2.recv_ref, ...), custom_call_target="tpu_custom_call", output_to_operand_aliasing={{0}: (2, {}), {1}: (3, {}), {2}: (4, {}), {3}: (5, {})} | custom-call | tf_op jit(solution)/shard_map/mend/pallas_call | solution.py:652
  26.0 1.1 %collective-permute-start.4 = (bf16[3,256,256]{2,1,0:T(8,128)(2,1)}, bf16[3,256,256]{2,1,0:T(8,128)(2,1)S(1)}, u32[]{:S(2)}, u32[]{:S(2)}) collective-permute-start(bf16[3,256,256]{2,1,0:T(8,128)(2,1)} %get-tuple-element.38), channel_id=1, source_target_pairs={{0,1},{1,0},{2,3},{3,2},{4,5},{5,4},{6,7},{7,6},{8,9},{9,8},{10,11... | collective-permute-start | bytes 1179656 | tf_op jit(solution)/shard_map/ppermute | solution.py:622
  27.1 0.3 collective-permute-start.5
  27.4 1.4 %collective-permute-start.3 = (bf16[32,256]{1,0:T(8,128)(2,1)}, bf16[32,256]{1,0:T(8,128)(2,1)S(1)}, u32[]{:S(2)}, u32[]{:S(2)}) collective-permute-start(bf16[32,256]{1,0:T(8,128)(2,1)} %get-tuple-element.35), channel_id=1, source_target_pairs={{0,1},{1,0},{2,3},{3,2},{4,5},{5,4},{6,7},{7,6},{8,9},{9,8},{10,11... | collective-permute-start | bytes 49160 | tf_op jit(solution)/shard_map/ppermute | solution.py:622
  28.8 1.0 %collective-permute-done.3 = bf16[32,256]{1,0:T(8,128)(2,1)S(1)} collective-permute-done((bf16[32,256]{1,0:T(8,128)(2,1)}, bf16[32,256]{1,0:T(8,128)(2,1)S(1)}, u32[]{:S(2)}, u32[]{:S(2)}) %collective-permute-start.3) | collective-permute-done | bytes 16416 | tf_op jit(solution)/shard_map/ppermute | solution.py:622
  29.8 0.7 %broadcast_dynamic-update-slice_fusion = bf16[8,128,256]{2,1,0:T(8,128)(2,1)} fusion(bf16[8,128,256]{2,1,0:T(8,128)(2,1)} %get-tuple-element.34, bf16[32,256]{1,0:T(8,128)(2,1)S(1)} %collective-permute-done.3), kind=kLoop, calls=%fused_computation | loop fusion | bytes 147456 | tf_op jit(solution)/shard_map/dynamic_update_slice | solution.py:632
  30.5 6.9 %all-to-all-start.1 = ((bf16[8,128,256]{2,1,0:T(8,128)(2,1)}), bf16[8,128,256]{2,1,0:T(8,128)(2,1)}, u32[]{:S(2)}, u32[]{:S(2)}) async-start(bf16[8,128,256]{2,1,0:T(8,128)(2,1)} %broadcast_dynamic-update-slice_fusion), calls=%async_computation.1 | async-start | bytes 1048576 | tf_op jit(solution)/shard_map/all_to_all | solution.py:607
  37.4 0.0 collective-permute-done.4.near_hbm
  37.4 0.0 copy-start
  37.4 1.3 %collective-permute-done.5.far_hbm = bf16[3,256,256]{2,1,0:T(8,128)(2,1)S(1)} collective-permute-done((bf16[3,256,256]{2,1,0:T(8,128)(2,1)}, bf16[3,256,256]{2,1,0:T(8,128)(2,1)S(1)}, u32[]{:S(2)}, u32[]{:S(2)}) %collective-permute-start.5) | collective-permute-done | bytes 393248 | tf_op jit(solution)/shard_map/ppermute | solution.py:625
  38.7 0.0 copy-start.1
  38.7 0.0 copy-done
  38.7 0.8 %copy-done.1 = bf16[3,256,256]{2,1,0:T(8,128)(2,1)} copy-done((bf16[3,256,256]{2,1,0:T(8,128)(2,1)}, bf16[3,256,256]{2,1,0:T(8,128)(2,1)S(1)}, u32[]{:S(2)}) %copy-start.1) | copy-done | bytes 393240
  39.5 13.9 %decode.1 = (bf16[3,8,128,256]{3,2,1,0:T(8,128)(2,1)}, f32[3,2,8,16,256]{4,3,2,1,0:T(8,128)}, f32[3,2,8,256]{3,2,1,0:T(8,128)}) custom-call(bf16[3,8,128,256]{3,2,1,0:T(8,128)(2,1)} %get-tuple-element.36.skip_hbm, bf16[3,4,64,256]{3,2,1,0:T(8,128)(2,1)} %get-tuple-element.37.pooled_hbm, bf16[3,256,256]{2,1,0:T(8,128)(2,1)} %copy-done, ...), custom_call_target="tpu_custom_call" | custom-call | flops 999999995904 | bytes 1000000000 | tf_op jit(solution)/shard_map/decode/pallas_call | solution.py:652
  53.4 0.0 all-to-all-done.1
  53.4 4.1 %seal.1 = bf16[3,8,128,256]{3,2,1,0:T(8,128)(2,1)} custom-call(s32[8,128]{1,0:T(8,128)} %get-tuple-element.33.tab_hbm, s32[1,2,3]{2,1,0:T(2,128)} %bitcast.10, s32[1,2,3]{2,1,0:T(2,128)} %bitcast.13, bf16[1024,256]{1,0:T(8,128)(2,1)} %bitcast.4.recv_hbm, f32[3,2,8,256]{3,2,1,0:T(8,128)} %get-tuple-element.40.coarse_hbm, ...), custom_call_target="tpu_custom_call", output_to_operand_aliasing={{}: (11, {})} | custom-call | tf_op jit(solution)/shard_map/seal/pallas_call | solution.py:652
Async XLA Ops:
  2.2 3.2 %collective-permute-start = (bf16[16,256]{1,0:T(8,128)(2,1)}, bf16[16,256]{1,0:T(8,128)(2,1)S(1)}, u32[]{:S(2)}, u32[]{:S(2)}) collective-permute-start(bf16[16,256]{1,0:T(8,128)(2,1)} %get-tuple-element.25), channel_id=1, source_target_pairs={{0,1},{1,0},{2,3},{3,2},{4,5},{5,4},{6,7},{7,6},{8,9},{9,8},{10,11... | collective-permute-start | bytes 24584 | tf_op jit(solution)/shard_map/ppermute | solution.py:622
  2.3 11.5 %collective-permute-start.1 = (bf16[3,128,256]{2,1,0:T(8,128)(2,1)}, bf16[3,128,256]{2,1,0:T(8,128)(2,1)S(1)}, u32[]{:S(2)}, u32[]{:S(2)}) collective-permute-start(bf16[3,128,256]{2,1,0:T(8,128)(2,1)} %get-tuple-element.26), channel_id=1, source_target_pairs={{0,1},{1,0},{2,3},{3,2},{4,5},{5,4},{6,7},{7,6},{8,9},{9,8},{10,11... | collective-permute-start | bytes 589832 | tf_op jit(solution)/shard_map/ppermute | solution.py:622
  2.8 11.1 %collective-permute-start.2 = (bf16[3,128,256]{2,1,0:T(8,128)(2,1)}, bf16[3,128,256]{2,1,0:T(8,128)(2,1)S(1)}, u32[]{:S(2)}, u32[]{:S(2)}) collective-permute-start(bf16[3,128,256]{2,1,0:T(8,128)(2,1)} %get-tuple-element.27), channel_id=1, source_target_pairs={{1,2},{2,1},{3,4},{4,3},{5,6},{6,5},{7,8},{8,7},{9,10},{10,9},{11,... | collective-permute-start | bytes 589832 | tf_op jit(solution)/shard_map/ppermute | solution.py:625
  6.0 16.0 %all-to-all-start = ((bf16[8,64,256]{2,1,0:T(8,128)(2,1)}), bf16[8,64,256]{2,1,0:T(8,128)(2,1)}, u32[]{:S(2)}, u32[]{:S(2)}) async-start(bf16[8,64,256]{2,1,0:T(8,128)(2,1)} %broadcast_dynamic-update-slice_fusion.1), calls=%async_computation | async-start | bytes 524288 | tf_op jit(solution)/shard_map/all_to_all | solution.py:607
  13.8 0.7 %copy-start.2 = (bf16[3,128,256]{2,1,0:T(8,128)(2,1)}, bf16[3,128,256]{2,1,0:T(8,128)(2,1)S(1)}, u32[]{:S(2)}) copy-start(bf16[3,128,256]{2,1,0:T(8,128)(2,1)S(1)} %collective-permute-done.1.near_in) | copy-start | bytes 589828
  13.8 0.7 %copy-start.3 = (bf16[3,128,256]{2,1,0:T(8,128)(2,1)}, bf16[3,128,256]{2,1,0:T(8,128)(2,1)S(1)}, u32[]{:S(2)}) copy-start(bf16[3,128,256]{2,1,0:T(8,128)(2,1)S(1)} %collective-permute-done.2.far_in) | copy-start | bytes 589828
  26.0 11.4 %collective-permute-start.4 = (bf16[3,256,256]{2,1,0:T(8,128)(2,1)}, bf16[3,256,256]{2,1,0:T(8,128)(2,1)S(1)}, u32[]{:S(2)}, u32[]{:S(2)}) collective-permute-start(bf16[3,256,256]{2,1,0:T(8,128)(2,1)} %get-tuple-element.38), channel_id=1, source_target_pairs={{0,1},{1,0},{2,3},{3,2},{4,5},{5,4},{6,7},{7,6},{8,9},{9,8},{10,11... | collective-permute-start | bytes 1179656 | tf_op jit(solution)/shard_map/ppermute | solution.py:622
  27.1 11.6 %collective-permute-start.5 = (bf16[3,256,256]{2,1,0:T(8,128)(2,1)}, bf16[3,256,256]{2,1,0:T(8,128)(2,1)S(1)}, u32[]{:S(2)}, u32[]{:S(2)}) collective-permute-start(bf16[3,256,256]{2,1,0:T(8,128)(2,1)} %get-tuple-element.39), channel_id=1, source_target_pairs={{1,2},{2,1},{3,4},{4,3},{5,6},{6,5},{7,8},{8,7},{9,10},{10,9},{11,... | collective-permute-start | bytes 1179656 | tf_op jit(solution)/shard_map/ppermute | solution.py:625
  27.4 2.4 %collective-permute-start.3 = (bf16[32,256]{1,0:T(8,128)(2,1)}, bf16[32,256]{1,0:T(8,128)(2,1)S(1)}, u32[]{:S(2)}, u32[]{:S(2)}) collective-permute-start(bf16[32,256]{1,0:T(8,128)(2,1)} %get-tuple-element.35), channel_id=1, source_target_pairs={{0,1},{1,0},{2,3},{3,2},{4,5},{5,4},{6,7},{7,6},{8,9},{9,8},{10,11... | collective-permute-start | bytes 49160 | tf_op jit(solution)/shard_map/ppermute | solution.py:622
  30.5 22.9 %all-to-all-start.1 = ((bf16[8,128,256]{2,1,0:T(8,128)(2,1)}), bf16[8,128,256]{2,1,0:T(8,128)(2,1)}, u32[]{:S(2)}, u32[]{:S(2)}) async-start(bf16[8,128,256]{2,1,0:T(8,128)(2,1)} %broadcast_dynamic-update-slice_fusion), calls=%async_computation.1 | async-start | bytes 1048576 | tf_op jit(solution)/shard_map/all_to_all | solution.py:607
  37.4 1.3 %copy-start = (bf16[3,256,256]{2,1,0:T(8,128)(2,1)}, bf16[3,256,256]{2,1,0:T(8,128)(2,1)S(1)}, u32[]{:S(2)}) copy-start(bf16[3,256,256]{2,1,0:T(8,128)(2,1)S(1)} %collective-permute-done.4.near_hbm) | copy-start | bytes 1179652
  38.7 0.8 %copy-start.1 = (bf16[3,256,256]{2,1,0:T(8,128)(2,1)}, bf16[3,256,256]{2,1,0:T(8,128)(2,1)S(1)}, u32[]{:S(2)}) copy-start(bf16[3,256,256]{2,1,0:T(8,128)(2,1)S(1)} %collective-permute-done.5.far_hbm) | copy-start | bytes 1179652

commit v5 on v4

--- a/solution.py
+++ b/solution.py
@@ -237,13 +237,13 @@
         copy.wait()
 
 
-def mend(layout, coarse, fine, recv_ref, w_hbm, skip_in, pooled_in, near_in, far_in, pre_hbm, tile_hbm, code_hbm,
+def mend(layout, coarse, fine, recv_hbm, w_hbm, skip_in, pooled_in, near_in, far_in, pre_hbm, tile_hbm, code_hbm,
          skip_hbm, pooled_hbm, near_hbm, far_hbm, own_hbm, near_tail_hbm, far_tail_hbm, table_hbm,
-         w_ref, pre_ref, edges, pools, own, tails, own16, tails16, table_ref, tile_ref, code_ref, in_sems, out_sems):
+         recv_ref, w_ref, pre_ref, edges, pools, own, tails, own16, tails16, table_ref, tile_ref, code_ref, in_sems, out_sems):
     tiles, height, low = layout.tiles, layout.height, coarse.height
     cycles, cols, chans = skip_in.shape[0], skip_in.shape[2], skip_in.shape[3]
     half = cols // 2
-    pairs = [(tile_hbm, tile_ref), (code_hbm, code_ref)]
+    pairs = [(tile_hbm, tile_ref), (code_hbm, code_ref), (recv_hbm, recv_ref)]
     pairs += [(w_hbm.at[:, 2 * side], w_ref.at[side]) for side in range(2)] + [(pre_hbm, pre_ref)]
     for side in range(2):
         pairs.append((skip_in.at[:, :, pl.ds((cols - 16) * side, 16)], edges.at[side]))
@@ -260,6 +260,7 @@
             other, face, side_bit, flip = seam_of(tile_ref, code_ref, tiles, cycle, side)
             place = layout.source(strip, flip, face, other * 2 + side_bit, row_iota)
             targets.append(jnp.where(row_iota <= height, place, -1))
+    arriving[2].wait()
     pads = pick(targets, recv_ref[...])
     noted = layout.near + layout.columns
     for member in range(2 * FACES):
@@ -267,14 +268,14 @@
         block = recv_ref[at : at + 16, :128].astype(F32)
         table_ref[member : member + 1] = block[noted % 16 : noted % 16 + 1].astype(jnp.int32)
     part = pads.shape[0] // 2
-    for copy in arriving[2:5]:
+    for copy in arriving[3:6]:
         copy.wait()
     seams = [
         [dot(pads[side * part : (side + 1) * part], w_ref[side, tap]) for tap in range(3)] for side in range(2)
     ]
     iota16 = lax.broadcasted_iota(jnp.int32, (16, chans), 0)
     tails[...] = jnp.zeros_like(tails)
-    for copy in arriving[5:]:
+    for copy in arriving[6:]:
         copy.wait()
     at_top = (odd == 1, odd == 0)
     skip_at = [jnp.where(t, 0, height - 1) for t in at_top]
@@ -688,10 +689,10 @@
         functools.partial(mend, spec, coarse_at, fine_at), "mend",
         [(tall, BF16), (pooled_shape, BF16), (wide, BF16), (wide, BF16), ((members, payload, chans), BF16)]
         + [((tail2, chans), BF16)] * 2 + [((members, 128), jnp.int32)],
-        [vmem] + [hbm] * 8, [hbm] * 8,
-        [((2, 3) + square, BF16), (pre_shape, F32), (edge_shape, BF16), (pool_edges, BF16), ((own2, chans), F32),
+        [hbm] * 9, [hbm] * 8,
+        [((members * spec.payload, chans), BF16), ((2, 3) + square, BF16), (pre_shape, F32), (edge_shape, BF16), (pool_edges, BF16), ((own2, chans), F32),
          ((2, tail2, chans), F32), ((own2, chans), BF16), ((2, tail2, chans), BF16), ((members, 128), jnp.int32),
-         *seam_scratch, dma((9,)), dma((19 + members,))],
+         *seam_scratch, dma((10,)), dma((19 + members,))],
         recv.reshape(-1, chans), encoder_weight, skip, pooled, near, far, pre_col, *seams,
         input_output_aliases={2: 0, 3: 1, 4: 2, 5: 3},
     )

time: 58.1 us -> 57.2 us (0.985)
  Pallas kernels: 31.6 us -> 30.8 us
    pallas_call x5, Pallas kernels: 31.6 us -> 30.8 us  [call(): pl.pallas_call(body, out_shape=[jax.ShapeDtypeStruct(shape, dtype) for sh...]
  transfers between devices with their start and end apart: 8 -> 8, of which waited for: 2 -> 2; matrix products, arithmetic and copies ran while one was open for 2% -> 2% of each run, Pallas kernels for 37% -> 38%
where the time goes in v5:
time: 57.2 us; the launch traced here: 56.8 us
  Pallas kernels  30.8 us (54%)
  starting transfers between devices  20.6 us (36%)
  local copies, waits for them, and re-layouts  2.82 us (5%)
  waiting for transfers between devices  2.4 us (4%)
    pallas_call x5, Pallas kernels, call(): pl.pallas_call(body, out_shape=[jax.ShapeDtypeStruct(shape, dtype) for sh...  30.8 us
    all_to_all x2, starting transfers between devices, share(): return lax.all_to_all(x, 'tile', 0, 0, tiled=True, axis_index_groups=groups)  14.7 us
    ppermute x4, starting transfers between devices, to_near(): return lax.ppermute(x, 'tile', near_pairs)  3.04 us
    ppermute x2, starting transfers between devices, to_far(): return lax.ppermute(x, 'tile', far_pairs)  2.88 us
    unnamed x8, local copies, waits for them, and re-layouts  1.51 us
    ppermute x2, waiting for transfers between devices, to_far(): return lax.ppermute(x, 'tile', far_pairs)  1.34 us
    dynamic_update_slice x2, local copies, waits for them, and re-layouts, pack(): own = lax.dynamic_update_slice(own, tail, (0, rows, 0))  1.31 us
  transfers between devices with their start and end apart: 8, of which 2 were waited for; matrix products, arithmetic and copies ran while one was open for 2% of the time, Pallas kernels for 38%

profile of v5, /device:TPU:1, one launch (start us, length us, event | category | flops | bytes accessed | tf_op | source)
XLA Modules:
  0.0 56.8 jit_solution(3423924013386050930)
XLA Ops:
  0.0 2.2 %lift.1 = (bf16[8,64,256]{2,1,0:T(8,128)(2,1)}, bf16[16,256]{1,0:T(8,128)(2,1)}, bf16[16,256]{1,0:T(8,128)(2,1)}, bf16[3,128,256]{2,1,0:T(8,128)(2,1)}, bf16[3,128,256]{2,1,0:T(8,128)(2,1)}) custom-call(bf16[3,8,128,256]{3,2,1,0:T(8,128)(2,1)} %x_hbm.3, s32[1,2,3]{2,1,0:T(2,128)} %bitcast.8, s32[1,2,3]{2,1,0:T(2,128)} %bitcast.11), custom_call_target="tpu_custom_call" | custom-call | tf_op jit(solution)/shard_map/lift/pallas_call | solution.py:653
  2.2 0.1 collective-permute-start
  2.3 0.5 collective-permute-start.1
  2.8 2.6 %collective-permute-start.2 = (bf16[3,128,256]{2,1,0:T(8,128)(2,1)}, bf16[3,128,256]{2,1,0:T(8,128)(2,1)S(1)}, u32[]{:S(2)}, u32[]{:S(2)}) collective-permute-start(bf16[3,128,256]{2,1,0:T(8,128)(2,1)} %get-tuple-element.27), channel_id=1, source_target_pairs={{1,2},{2,1},{3,4},{4,3},{5,6},{6,5},{7,8},{8,7},{9,10},{10,9},{11,... | collective-permute-start | bytes 589832 | tf_op jit(solution)/shard_map/ppermute | solution.py:626
  5.4 0.0 collective-permute-done
  5.4 0.6 %broadcast_dynamic-update-slice_fusion.1 = bf16[8,64,256]{2,1,0:T(8,128)(2,1)} fusion(bf16[8,64,256]{2,1,0:T(8,128)(2,1)} %get-tuple-element.24, bf16[16,256]{1,0:T(8,128)(2,1)S(1)} %collective-permute-done), kind=kLoop, calls=%fused_computation.1 | loop fusion | bytes 73728 | tf_op jit(solution)/shard_map/dynamic_update_slice | solution.py:633
  6.0 7.8 %all-to-all-start = ((bf16[8,64,256]{2,1,0:T(8,128)(2,1)}), bf16[8,64,256]{2,1,0:T(8,128)(2,1)}, u32[]{:S(2)}, u32[]{:S(2)}) async-start(bf16[8,64,256]{2,1,0:T(8,128)(2,1)} %broadcast_dynamic-update-slice_fusion.1), calls=%async_computation | async-start | bytes 524288 | tf_op jit(solution)/shard_map/all_to_all | solution.py:608
  13.8 0.0 collective-permute-done.1.near_in
  13.8 0.0 copy-start.2
  13.8 0.0 collective-permute-done.2.far_in
  13.8 0.0 copy-start.3
  13.9 0.7 %copy-done.2 = bf16[3,128,256]{2,1,0:T(8,128)(2,1)} copy-done((bf16[3,128,256]{2,1,0:T(8,128)(2,1)}, bf16[3,128,256]{2,1,0:T(8,128)(2,1)S(1)}, u32[]{:S(2)}) %copy-start.2) | copy-done | bytes 196632
  14.5 0.1 copy-done.3
  14.6 7.4 %encode.1 = (bf16[3,8,128,256]{3,2,1,0:T(8,128)(2,1)}, bf16[3,4,64,256]{3,2,1,0:T(8,128)(2,1)}, bf16[3,256,256]{2,1,0:T(8,128)(2,1)}, bf16[3,256,256]{2,1,0:T(8,128)(2,1)}, f32[3,2,8,256]{3,2,1,0:T(8,128)}) custom-call(bf16[3,8,128,256]{3,2,1,0:T(8,128)(2,1)} %x_hbm.3, bf16[3,128,256]{2,1,0:T(8,128)(2,1)} %copy-done.2, bf16[3,128,256]{2,1,0:T(8,128)(2,1)} %copy-done.3, ...), custom_call_target="tpu_custom_call" | custom-call | flops 999999995904 | bytes 1000000000 | tf_op jit(solution)/shard_map/encode/pallas_call | solution.py:653
  22.0 0.0 all-to-all-done
  22.1 3.1 %mend.1 = (bf16[3,8,128,256]{3,2,1,0:T(8,128)(2,1)}, bf16[3,4,64,256]{3,2,1,0:T(8,128)(2,1)}, bf16[3,256,256]{2,1,0:T(8,128)(2,1)}, bf16[3,256,256]{2,1,0:T(8,12...) custom-call(bf16[512,256]{1,0:T(8,128)(2,1)} %bitcast.2.recv_hbm, ...), custom_call_target="tpu_custom_call", output_to_operand_aliasing={{0}: (2, {}), {1}: (3, {}), {2}: (4, {}), {3}: (5, {})} | custom-call | tf_op jit(solution)/shard_map/mend/pallas_call | solution.py:653
  25.2 1.1 %collective-permute-start.4 = (bf16[3,256,256]{2,1,0:T(8,128)(2,1)}, bf16[3,256,256]{2,1,0:T(8,128)(2,1)S(1)}, u32[]{:S(2)}, u32[]{:S(2)}) collective-permute-start(bf16[3,256,256]{2,1,0:T(8,128)(2,1)} %get-tuple-element.38), channel_id=1, source_target_pairs={{0,1},{1,0},{2,3},{3,2},{4,5},{5,4},{6,7},{7,6},{8,9},{9,8},{10,11... | collective-permute-start | bytes 1179656 | tf_op jit(solution)/shard_map/ppermute | solution.py:623
  26.2 0.3 collective-permute-start.5
  26.5 1.4 %collective-permute-start.3 = (bf16[32,256]{1,0:T(8,128)(2,1)}, bf16[32,256]{1,0:T(8,128)(2,1)S(1)}, u32[]{:S(2)}, u32[]{:S(2)}) collective-permute-start(bf16[32,256]{1,0:T(8,128)(2,1)} %get-tuple-element.35), channel_id=1, source_target_pairs={{0,1},{1,0},{2,3},{3,2},{4,5},{5,4},{6,7},{7,6},{8,9},{9,8},{10,11... | collective-permute-start | bytes 49160 | tf_op jit(solution)/shard_map/ppermute | solution.py:623
  27.9 1.0 %collective-permute-done.3 = bf16[32,256]{1,0:T(8,128)(2,1)S(1)} collective-permute-done((bf16[32,256]{1,0:T(8,128)(2,1)}, bf16[32,256]{1,0:T(8,128)(2,1)S(1)}, u32[]{:S(2)}, u32[]{:S(2)}) %collective-permute-start.3) | collective-permute-done | bytes 16416 | tf_op jit(solution)/shard_map/ppermute | solution.py:623
  28.9 0.7 %broadcast_dynamic-update-slice_fusion = bf16[8,128,256]{2,1,0:T(8,128)(2,1)} fusion(bf16[8,128,256]{2,1,0:T(8,128)(2,1)} %get-tuple-element.34, bf16[32,256]{1,0:T(8,128)(2,1)S(1)} %collective-permute-done.3), kind=kLoop, calls=%fused_computation | loop fusion | bytes 147456 | tf_op jit(solution)/shard_map/dynamic_update_slice | solution.py:633
  29.6 6.9 %all-to-all-start.1 = ((bf16[8,128,256]{2,1,0:T(8,128)(2,1)}), bf16[8,128,256]{2,1,0:T(8,128)(2,1)}, u32[]{:S(2)}, u32[]{:S(2)}) async-start(bf16[8,128,256]{2,1,0:T(8,128)(2,1)} %broadcast_dynamic-update-slice_fusion), calls=%async_computation.1 | async-start | bytes 1048576 | tf_op jit(solution)/shard_map/all_to_all | solution.py:608
  36.5 0.0 collective-permute-done.4.near_hbm
  36.5 0.0 copy-start
  36.5 1.3 %collective-permute-done.5.far_hbm = bf16[3,256,256]{2,1,0:T(8,128)(2,1)S(1)} collective-permute-done((bf16[3,256,256]{2,1,0:T(8,128)(2,1)}, bf16[3,256,256]{2,1,0:T(8,128)(2,1)S(1)}, u32[]{:S(2)}, u32[]{:S(2)}) %collective-permute-start.5) | collective-permute-done | bytes 393248 | tf_op jit(solution)/shard_map/ppermute | solution.py:626
  37.9 0.0 copy-start.1
  37.9 0.0 copy-done
  37.9 0.8 %copy-done.1 = bf16[3,256,256]{2,1,0:T(8,128)(2,1)} copy-done((bf16[3,256,256]{2,1,0:T(8,128)(2,1)}, bf16[3,256,256]{2,1,0:T(8,128)(2,1)S(1)}, u32[]{:S(2)}) %copy-start.1) | copy-done | bytes 393240
  38.6 13.9 %decode.1 = (bf16[3,8,128,256]{3,2,1,0:T(8,128)(2,1)}, f32[3,2,8,16,256]{4,3,2,1,0:T(8,128)}, f32[3,2,8,256]{3,2,1,0:T(8,128)}) custom-call(bf16[3,8,128,256]{3,2,1,0:T(8,128)(2,1)} %get-tuple-element.36.skip_hbm, bf16[3,4,64,256]{3,2,1,0:T(8,128)(2,1)} %get-tuple-element.37.pooled_hbm, bf16[3,256,256]{2,1,0:T(8,128)(2,1)} %copy-done, ...), custom_call_target="tpu_custom_call" | custom-call | flops 999999995904 | bytes 1000000000 | tf_op jit(solution)/shard_map/decode/pallas_call | solution.py:653
  52.6 0.0 all-to-all-done.1
  52.6 4.1 %seal.1 = bf16[3,8,128,256]{3,2,1,0:T(8,128)(2,1)} custom-call(s32[8,128]{1,0:T(8,128)} %get-tuple-element.33.tab_hbm, s32[1,2,3]{2,1,0:T(2,128)} %bitcast.10, s32[1,2,3]{2,1,0:T(2,128)} %bitcast.13, bf16[1024,256]{1,0:T(8,128)(2,1)} %bitcast.4.recv_hbm, f32[3,2,8,256]{3,2,1,0:T(8,128)} %get-tuple-element.40.coarse_hbm, ...), custom_call_target="tpu_custom_call", output_to_operand_aliasing={{}: (11, {})} | custom-call | tf_op jit(solution)/shard_map/seal/pallas_call | solution.py:653
Async XLA Ops:
  2.2 3.2 %collective-permute-start = (bf16[16,256]{1,0:T(8,128)(2,1)}, bf16[16,256]{1,0:T(8,128)(2,1)S(1)}, u32[]{:S(2)}, u32[]{:S(2)}) collective-permute-start(bf16[16,256]{1,0:T(8,128)(2,1)} %get-tuple-element.25), channel_id=1, source_target_pairs={{0,1},{1,0},{2,3},{3,2},{4,5},{5,4},{6,7},{7,6},{8,9},{9,8},{10,11... | collective-permute-start | bytes 24584 | tf_op jit(solution)/shard_map/ppermute | solution.py:623
  2.3 11.5 %collective-permute-start.1 = (bf16[3,128,256]{2,1,0:T(8,128)(2,1)}, bf16[3,128,256]{2,1,0:T(8,128)(2,1)S(1)}, u32[]{:S(2)}, u32[]{:S(2)}) collective-permute-start(bf16[3,128,256]{2,1,0:T(8,128)(2,1)} %get-tuple-element.26), channel_id=1, source_target_pairs={{0,1},{1,0},{2,3},{3,2},{4,5},{5,4},{6,7},{7,6},{8,9},{9,8},{10,11... | collective-permute-start | bytes 589832 | tf_op jit(solution)/shard_map/ppermute | solution.py:623
  2.8 11.1 %collective-permute-start.2 = (bf16[3,128,256]{2,1,0:T(8,128)(2,1)}, bf16[3,128,256]{2,1,0:T(8,128)(2,1)S(1)}, u32[]{:S(2)}, u32[]{:S(2)}) collective-permute-start(bf16[3,128,256]{2,1,0:T(8,128)(2,1)} %get-tuple-element.27), channel_id=1, source_target_pairs={{1,2},{2,1},{3,4},{4,3},{5,6},{6,5},{7,8},{8,7},{9,10},{10,9},{11,... | collective-permute-start | bytes 589832 | tf_op jit(solution)/shard_map/ppermute | solution.py:626
  6.0 16.0 %all-to-all-start = ((bf16[8,64,256]{2,1,0:T(8,128)(2,1)}), bf16[8,64,256]{2,1,0:T(8,128)(2,1)}, u32[]{:S(2)}, u32[]{:S(2)}) async-start(bf16[8,64,256]{2,1,0:T(8,128)(2,1)} %broadcast_dynamic-update-slice_fusion.1), calls=%async_computation | async-start | bytes 524288 | tf_op jit(solution)/shard_map/all_to_all | solution.py:608
  13.8 0.7 %copy-start.2 = (bf16[3,128,256]{2,1,0:T(8,128)(2,1)}, bf16[3,128,256]{2,1,0:T(8,128)(2,1)S(1)}, u32[]{:S(2)}) copy-start(bf16[3,128,256]{2,1,0:T(8,128)(2,1)S(1)} %collective-permute-done.1.near_in) | copy-start | bytes 589828
  13.8 0.7 %copy-start.3 = (bf16[3,128,256]{2,1,0:T(8,128)(2,1)}, bf16[3,128,256]{2,1,0:T(8,128)(2,1)S(1)}, u32[]{:S(2)}) copy-start(bf16[3,128,256]{2,1,0:T(8,128)(2,1)S(1)} %collective-permute-done.2.far_in) | copy-start | bytes 589828
  25.2 11.4 %collective-permute-start.4 = (bf16[3,256,256]{2,1,0:T(8,128)(2,1)}, bf16[3,256,256]{2,1,0:T(8,128)(2,1)S(1)}, u32[]{:S(2)}, u32[]{:S(2)}) collective-permute-start(bf16[3,256,256]{2,1,0:T(8,128)(2,1)} %get-tuple-element.38), channel_id=1, source_target_pairs={{0,1},{1,0},{2,3},{3,2},{4,5},{5,4},{6,7},{7,6},{8,9},{9,8},{10,11... | collective-permute-start | bytes 1179656 | tf_op jit(solution)/shard_map/ppermute | solution.py:623
  26.2 11.6 %collective-permute-start.5 = (bf16[3,256,256]{2,1,0:T(8,128)(2,1)}, bf16[3,256,256]{2,1,0:T(8,128)(2,1)S(1)}, u32[]{:S(2)}, u32[]{:S(2)}) collective-permute-start(bf16[3,256,256]{2,1,0:T(8,128)(2,1)} %get-tuple-element.39), channel_id=1, source_target_pairs={{1,2},{2,1},{3,4},{4,3},{5,6},{6,5},{7,8},{8,7},{9,10},{10,9},{11,... | collective-permute-start | bytes 1179656 | tf_op jit(solution)/shard_map/ppermute | solution.py:626
  26.5 2.4 %collective-permute-start.3 = (bf16[32,256]{1,0:T(8,128)(2,1)}, bf16[32,256]{1,0:T(8,128)(2,1)S(1)}, u32[]{:S(2)}, u32[]{:S(2)}) collective-permute-start(bf16[32,256]{1,0:T(8,128)(2,1)} %get-tuple-element.35), channel_id=1, source_target_pairs={{0,1},{1,0},{2,3},{3,2},{4,5},{5,4},{6,7},{7,6},{8,9},{9,8},{10,11... | collective-permute-start | bytes 49160 | tf_op jit(solution)/shard_map/ppermute | solution.py:623
  29.6 22.9 %all-to-all-start.1 = ((bf16[8,128,256]{2,1,0:T(8,128)(2,1)}), bf16[8,128,256]{2,1,0:T(8,128)(2,1)}, u32[]{:S(2)}, u32[]{:S(2)}) async-start(bf16[8,128,256]{2,1,0:T(8,128)(2,1)} %broadcast_dynamic-update-slice_fusion), calls=%async_computation.1 | async-start | bytes 1048576 | tf_op jit(solution)/shard_map/all_to_all | solution.py:608
  36.5 1.3 %copy-start = (bf16[3,256,256]{2,1,0:T(8,128)(2,1)}, bf16[3,256,256]{2,1,0:T(8,128)(2,1)S(1)}, u32[]{:S(2)}) copy-start(bf16[3,256,256]{2,1,0:T(8,128)(2,1)S(1)} %collective-permute-done.4.near_hbm) | copy-start | bytes 1179652
  37.9 0.8 %copy-start.1 = (bf16[3,256,256]{2,1,0:T(8,128)(2,1)}, bf16[3,256,256]{2,1,0:T(8,128)(2,1)S(1)}, u32[]{:S(2)}) copy-start(bf16[3,256,256]{2,1,0:T(8,128)(2,1)S(1)} %collective-permute-done.5.far_hbm) | copy-start | bytes 1179652

commit v6 on v5

--- a/solution.py
+++ b/solution.py
@@ -168,9 +168,10 @@
     tails16[...] = tails[...].astype(BF16)
     pairs = [(tails16.at[0], near_tail_hbm), (tails16.at[1], far_tail_hbm)]
     pairs += [(own16, own_hbm.at[k, pl.ds(0, own16.shape[0])]) for k in range(2 * FACES)]
+    leaving = fetch(pairs, out_sems.at[pl.ds(0, len(pairs))])
     for copy in arriving[2:4]:
         copy.wait()
-    leaving = fetch(pairs + [(rows.at[0], near_hbm), (rows.at[1], far_hbm)], out_sems)
+    leaving += fetch([(rows.at[0], near_hbm), (rows.at[1], far_hbm)], out_sems.at[pl.ds(len(pairs), 2)])
     for copy in leaving:
         copy.wait()
 
@@ -468,8 +469,9 @@
     cols = out_hbm.shape[2]
     low = height // 2
     pairs = [(recv_hbm, recv_ref), (bm_hbm, bm_ref), (bu_hbm, bu_ref), (coarse_hbm, coarse_ref), (wm_hbm, wm_ref), (u_hbm, u_ref)]
-    pairs += [(wd_hbm.at[:, :, pl.ds(0, chans)], wu_ref), (edge_hbm, edge_ref)]
+    pairs += [(wd_hbm.at[:, :, pl.ds(0, chans)], wu_ref)]
     pairs += [(wd_hbm.at[:, 2 * side, pl.ds(chans, chans)], ws_ref.at[side]) for side in range(2)]
+    pairs += [(edge_hbm, edge_ref)]
     seams = fetch([(tab_hbm, tab_ref), (tile_hbm, tile_ref), (code_hbm, code_ref)], in_sems.at[pl.ds(10, 3)])
     arriving = fetch(pairs, in_sems.at[pl.ds(0, 10)])
     for copy in seams:
@@ -545,7 +547,7 @@
     skip_pad = got[4 * n :]
     m = 16 * cycles
     lines = [[outer[:m], inside[0][:m], inside[1][:m]], [outer[m:], inside[1][m:], inside[0][m:]]]
-    for copy in arriving[6:]:
+    for copy in arriving[6:9]:
         copy.wait()
     sums = [[[], [], []], [[], [], []]]
     for row in range(3):
@@ -563,6 +565,7 @@
             for into in range(3):
                 sums[side][into].append(found[side][into])
     iota16 = lax.broadcasted_iota(jnp.int32, (16, chans), 0)
+    arriving[9].wait()
     for side in range(2):
         for cycle in range(cycles):
             extra = [column_sum(sums[side][into], cycle, height) for into in range(3)]

time: 57.2 us -> 57.2 us (level)
  no operation moved by 1% of the time
where the time goes in v6:
time: 57.2 us; the launch traced here: 56.9 us
  Pallas kernels  30.8 us (54%)
  starting transfers between devices  20.6 us (36%)
  local copies, waits for them, and re-layouts  2.82 us (5%)
  waiting for transfers between devices  2.4 us (4%)
    pallas_call x5, Pallas kernels, call(): pl.pallas_call(body, out_shape=[jax.ShapeDtypeStruct(shape, dtype) for sh...  30.8 us
    all_to_all x2, starting transfers between devices, share(): return lax.all_to_all(x, 'tile', 0, 0, tiled=True, axis_index_groups=groups)  14.7 us
    ppermute x4, starting transfers between devices, to_near(): return lax.ppermute(x, 'tile', near_pairs)  3.04 us
    ppermute x2, starting transfers between devices, to_far(): return lax.ppermute(x, 'tile', far_pairs)  2.88 us
    unnamed x8, local copies, waits for them, and re-layouts  1.51 us
    ppermute x2, waiting for transfers between devices, to_far(): return lax.ppermute(x, 'tile', far_pairs)  1.34 us
    dynamic_update_slice x2, local copies, waits for them, and re-layouts, pack(): own = lax.dynamic_update_slice(own, tail, (0, rows, 0))  1.31 us
  transfers between devices with their start and end apart: 8, of which 2 were waited for; matrix products, arithmetic and copies ran while one was open for 2% of the time, Pallas kernels for 38%

profile of v6, /device:TPU:1, one launch (start us, length us, event | category | flops | bytes accessed | tf_op | source)
XLA Modules:
  0.0 56.9 jit_solution(9243068689935987816)
XLA Ops:
  0.0 2.1 %lift.1 = (bf16[8,64,256]{2,1,0:T(8,128)(2,1)}, bf16[16,256]{1,0:T(8,128)(2,1)}, bf16[16,256]{1,0:T(8,128)(2,1)}, bf16[3,128,256]{2,1,0:T(8,128)(2,1)}, bf16[3,128,256]{2,1,0:T(8,128)(2,1)}) custom-call(bf16[3,8,128,256]{3,2,1,0:T(8,128)(2,1)} %x_hbm.3, s32[1,2,3]{2,1,0:T(2,128)} %bitcast.8, s32[1,2,3]{2,1,0:T(2,128)} %bitcast.11), custom_call_target="tpu_custom_call" | custom-call | tf_op jit(solution)/shard_map/lift/pallas_call | solution.py:656
  2.1 0.1 collective-permute-start
  2.2 0.5 collective-permute-start.1
  2.7 2.6 %collective-permute-start.2 = (bf16[3,128,256]{2,1,0:T(8,128)(2,1)}, bf16[3,128,256]{2,1,0:T(8,128)(2,1)S(1)}, u32[]{:S(2)}, u32[]{:S(2)}) collective-permute-start(bf16[3,128,256]{2,1,0:T(8,128)(2,1)} %get-tuple-element.27), channel_id=1, source_target_pairs={{1,2},{2,1},{3,4},{4,3},{5,6},{6,5},{7,8},{8,7},{9,10},{10,9},{11,... | collective-permute-start | bytes 589832 | tf_op jit(solution)/shard_map/ppermute | solution.py:629
  5.3 0.0 collective-permute-done
  5.3 0.6 %broadcast_dynamic-update-slice_fusion.1 = bf16[8,64,256]{2,1,0:T(8,128)(2,1)} fusion(bf16[8,64,256]{2,1,0:T(8,128)(2,1)} %get-tuple-element.24, bf16[16,256]{1,0:T(8,128)(2,1)S(1)} %collective-permute-done), kind=kLoop, calls=%fused_computation.1 | loop fusion | bytes 73728 | tf_op jit(solution)/shard_map/dynamic_update_slice | solution.py:636
  5.9 7.8 %all-to-all-start = ((bf16[8,64,256]{2,1,0:T(8,128)(2,1)}), bf16[8,64,256]{2,1,0:T(8,128)(2,1)}, u32[]{:S(2)}, u32[]{:S(2)}) async-start(bf16[8,64,256]{2,1,0:T(8,128)(2,1)} %broadcast_dynamic-update-slice_fusion.1), calls=%async_computation | async-start | bytes 524288 | tf_op jit(solution)/shard_map/all_to_all | solution.py:611
  13.8 0.0 collective-permute-done.1.near_in
  13.8 0.0 copy-start.2
  13.8 0.0 collective-permute-done.2.far_in
  13.8 0.0 copy-start.3
  13.8 0.7 %copy-done.2 = bf16[3,128,256]{2,1,0:T(8,128)(2,1)} copy-done((bf16[3,128,256]{2,1,0:T(8,128)(2,1)}, bf16[3,128,256]{2,1,0:T(8,128)(2,1)S(1)}, u32[]{:S(2)}) %copy-start.2) | copy-done | bytes 196632
  14.4 0.1 copy-done.3
  14.5 7.4 %encode.1 = (bf16[3,8,128,256]{3,2,1,0:T(8,128)(2,1)}, bf16[3,4,64,256]{3,2,1,0:T(8,128)(2,1)}, bf16[3,256,256]{2,1,0:T(8,128)(2,1)}, bf16[3,256,256]{2,1,0:T(8,128)(2,1)}, f32[3,2,8,256]{3,2,1,0:T(8,128)}) custom-call(bf16[3,8,128,256]{3,2,1,0:T(8,128)(2,1)} %x_hbm.3, bf16[3,128,256]{2,1,0:T(8,128)(2,1)} %copy-done.2, bf16[3,128,256]{2,1,0:T(8,128)(2,1)} %copy-done.3, ...), custom_call_target="tpu_custom_call" | custom-call | flops 999999995904 | bytes 1000000000 | tf_op jit(solution)/shard_map/encode/pallas_call | solution.py:656
  22.0 0.0 all-to-all-done
  22.0 3.1 %mend.1 = (bf16[3,8,128,256]{3,2,1,0:T(8,128)(2,1)}, bf16[3,4,64,256]{3,2,1,0:T(8,128)(2,1)}, bf16[3,256,256]{2,1,0:T(8,128)(2,1)}, bf16[3,256,256]{2,1,0:T(8,12...) custom-call(bf16[512,256]{1,0:T(8,128)(2,1)} %bitcast.2.recv_hbm, ...), custom_call_target="tpu_custom_call", output_to_operand_aliasing={{0}: (2, {}), {1}: (3, {}), {2}: (4, {}), {3}: (5, {})} | custom-call | tf_op jit(solution)/shard_map/mend/pallas_call | solution.py:656
  25.1 1.1 %collective-permute-start.4 = (bf16[3,256,256]{2,1,0:T(8,128)(2,1)}, bf16[3,256,256]{2,1,0:T(8,128)(2,1)S(1)}, u32[]{:S(2)}, u32[]{:S(2)}) collective-permute-start(bf16[3,256,256]{2,1,0:T(8,128)(2,1)} %get-tuple-element.38), channel_id=1, source_target_pairs={{0,1},{1,0},{2,3},{3,2},{4,5},{5,4},{6,7},{7,6},{8,9},{9,8},{10,11... | collective-permute-start | bytes 1179656 | tf_op jit(solution)/shard_map/ppermute | solution.py:626
  26.2 0.3 collective-permute-start.5
  26.4 1.4 %collective-permute-start.3 = (bf16[32,256]{1,0:T(8,128)(2,1)}, bf16[32,256]{1,0:T(8,128)(2,1)S(1)}, u32[]{:S(2)}, u32[]{:S(2)}) collective-permute-start(bf16[32,256]{1,0:T(8,128)(2,1)} %get-tuple-element.35), channel_id=1, source_target_pairs={{0,1},{1,0},{2,3},{3,2},{4,5},{5,4},{6,7},{7,6},{8,9},{9,8},{10,11... | collective-permute-start | bytes 49160 | tf_op jit(solution)/shard_map/ppermute | solution.py:626
  27.8 1.0 %collective-permute-done.3 = bf16[32,256]{1,0:T(8,128)(2,1)S(1)} collective-permute-done((bf16[32,256]{1,0:T(8,128)(2,1)}, bf16[32,256]{1,0:T(8,128)(2,1)S(1)}, u32[]{:S(2)}, u32[]{:S(2)}) %collective-permute-start.3) | collective-permute-done | bytes 16416 | tf_op jit(solution)/shard_map/ppermute | solution.py:626
  28.9 0.7 %broadcast_dynamic-update-slice_fusion = bf16[8,128,256]{2,1,0:T(8,128)(2,1)} fusion(bf16[8,128,256]{2,1,0:T(8,128)(2,1)} %get-tuple-element.34, bf16[32,256]{1,0:T(8,128)(2,1)S(1)} %collective-permute-done.3), kind=kLoop, calls=%fused_computation | loop fusion | bytes 147456 | tf_op jit(solution)/shard_map/dynamic_update_slice | solution.py:636
  29.6 6.9 %all-to-all-start.1 = ((bf16[8,128,256]{2,1,0:T(8,128)(2,1)}), bf16[8,128,256]{2,1,0:T(8,128)(2,1)}, u32[]{:S(2)}, u32[]{:S(2)}) async-start(bf16[8,128,256]{2,1,0:T(8,128)(2,1)} %broadcast_dynamic-update-slice_fusion), calls=%async_computation.1 | async-start | bytes 1048576 | tf_op jit(solution)/shard_map/all_to_all | solution.py:611
  36.4 0.0 collective-permute-done.4.near_hbm
  36.5 0.0 copy-start
  36.5 1.3 %collective-permute-done.5.far_hbm = bf16[3,256,256]{2,1,0:T(8,128)(2,1)S(1)} collective-permute-done((bf16[3,256,256]{2,1,0:T(8,128)(2,1)}, bf16[3,256,256]{2,1,0:T(8,128)(2,1)S(1)}, u32[]{:S(2)}, u32[]{:S(2)}) %collective-permute-start.5) | collective-permute-done | bytes 393248 | tf_op jit(solution)/shard_map/ppermute | solution.py:629
  37.8 0.0 copy-start.1
  37.8 0.0 copy-done
  37.8 0.8 %copy-done.1 = bf16[3,256,256]{2,1,0:T(8,128)(2,1)} copy-done((bf16[3,256,256]{2,1,0:T(8,128)(2,1)}, bf16[3,256,256]{2,1,0:T(8,128)(2,1)S(1)}, u32[]{:S(2)}) %copy-start.1) | copy-done | bytes 393240
  38.6 13.9 %decode.1 = (bf16[3,8,128,256]{3,2,1,0:T(8,128)(2,1)}, f32[3,2,8,16,256]{4,3,2,1,0:T(8,128)}, f32[3,2,8,256]{3,2,1,0:T(8,128)}) custom-call(bf16[3,8,128,256]{3,2,1,0:T(8,128)(2,1)} %get-tuple-element.36.skip_hbm, bf16[3,4,64,256]{3,2,1,0:T(8,128)(2,1)} %get-tuple-element.37.pooled_hbm, bf16[3,256,256]{2,1,0:T(8,128)(2,1)} %copy-done, ...), custom_call_target="tpu_custom_call" | custom-call | flops 999999995904 | bytes 1000000000 | tf_op jit(solution)/shard_map/decode/pallas_call | solution.py:656
  52.5 0.0 all-to-all-done.1
  52.5 4.2 %seal.1 = bf16[3,8,128,256]{3,2,1,0:T(8,128)(2,1)} custom-call(s32[8,128]{1,0:T(8,128)} %get-tuple-element.33.tab_hbm, s32[1,2,3]{2,1,0:T(2,128)} %bitcast.10, s32[1,2,3]{2,1,0:T(2,128)} %bitcast.13, bf16[1024,256]{1,0:T(8,128)(2,1)} %bitcast.4.recv_hbm, f32[3,2,8,256]{3,2,1,0:T(8,128)} %get-tuple-element.40.coarse_hbm, ...), custom_call_target="tpu_custom_call", output_to_operand_aliasing={{}: (11, {})} | custom-call | tf_op jit(solution)/shard_map/seal/pallas_call | solution.py:656
Async XLA Ops:
  2.1 3.2 %collective-permute-start = (bf16[16,256]{1,0:T(8,128)(2,1)}, bf16[16,256]{1,0:T(8,128)(2,1)S(1)}, u32[]{:S(2)}, u32[]{:S(2)}) collective-permute-start(bf16[16,256]{1,0:T(8,128)(2,1)} %get-tuple-element.25), channel_id=1, source_target_pairs={{0,1},{1,0},{2,3},{3,2},{4,5},{5,4},{6,7},{7,6},{8,9},{9,8},{10,11... | collective-permute-start | bytes 24584 | tf_op jit(solution)/shard_map/ppermute | solution.py:626
  2.2 11.5 %collective-permute-start.1 = (bf16[3,128,256]{2,1,0:T(8,128)(2,1)}, bf16[3,128,256]{2,1,0:T(8,128)(2,1)S(1)}, u32[]{:S(2)}, u32[]{:S(2)}) collective-permute-start(bf16[3,128,256]{2,1,0:T(8,128)(2,1)} %get-tuple-element.26), channel_id=1, source_target_pairs={{0,1},{1,0},{2,3},{3,2},{4,5},{5,4},{6,7},{7,6},{8,9},{9,8},{10,11... | collective-permute-start | bytes 589832 | tf_op jit(solution)/shard_map/ppermute | solution.py:626
  2.7 11.1 %collective-permute-start.2 = (bf16[3,128,256]{2,1,0:T(8,128)(2,1)}, bf16[3,128,256]{2,1,0:T(8,128)(2,1)S(1)}, u32[]{:S(2)}, u32[]{:S(2)}) collective-permute-start(bf16[3,128,256]{2,1,0:T(8,128)(2,1)} %get-tuple-element.27), channel_id=1, source_target_pairs={{1,2},{2,1},{3,4},{4,3},{5,6},{6,5},{7,8},{8,7},{9,10},{10,9},{11,... | collective-permute-start | bytes 589832 | tf_op jit(solution)/shard_map/ppermute | solution.py:629
  5.9 16.1 %all-to-all-start = ((bf16[8,64,256]{2,1,0:T(8,128)(2,1)}), bf16[8,64,256]{2,1,0:T(8,128)(2,1)}, u32[]{:S(2)}, u32[]{:S(2)}) async-start(bf16[8,64,256]{2,1,0:T(8,128)(2,1)} %broadcast_dynamic-update-slice_fusion.1), calls=%async_computation | async-start | bytes 524288 | tf_op jit(solution)/shard_map/all_to_all | solution.py:611
  13.8 0.7 %copy-start.2 = (bf16[3,128,256]{2,1,0:T(8,128)(2,1)}, bf16[3,128,256]{2,1,0:T(8,128)(2,1)S(1)}, u32[]{:S(2)}) copy-start(bf16[3,128,256]{2,1,0:T(8,128)(2,1)S(1)} %collective-permute-done.1.near_in) | copy-start | bytes 589828
  13.8 0.7 %copy-start.3 = (bf16[3,128,256]{2,1,0:T(8,128)(2,1)}, bf16[3,128,256]{2,1,0:T(8,128)(2,1)S(1)}, u32[]{:S(2)}) copy-start(bf16[3,128,256]{2,1,0:T(8,128)(2,1)S(1)} %collective-permute-done.2.far_in) | copy-start | bytes 589828
  25.1 11.4 %collective-permute-start.4 = (bf16[3,256,256]{2,1,0:T(8,128)(2,1)}, bf16[3,256,256]{2,1,0:T(8,128)(2,1)S(1)}, u32[]{:S(2)}, u32[]{:S(2)}) collective-permute-start(bf16[3,256,256]{2,1,0:T(8,128)(2,1)} %get-tuple-element.38), channel_id=1, source_target_pairs={{0,1},{1,0},{2,3},{3,2},{4,5},{5,4},{6,7},{7,6},{8,9},{9,8},{10,11... | collective-permute-start | bytes 1179656 | tf_op jit(solution)/shard_map/ppermute | solution.py:626
  26.2 11.6 %collective-permute-start.5 = (bf16[3,256,256]{2,1,0:T(8,128)(2,1)}, bf16[3,256,256]{2,1,0:T(8,128)(2,1)S(1)}, u32[]{:S(2)}, u32[]{:S(2)}) collective-permute-start(bf16[3,256,256]{2,1,0:T(8,128)(2,1)} %get-tuple-element.39), channel_id=1, source_target_pairs={{1,2},{2,1},{3,4},{4,3},{5,6},{6,5},{7,8},{8,7},{9,10},{10,9},{11,... | collective-permute-start | bytes 1179656 | tf_op jit(solution)/shard_map/ppermute | solution.py:629
  26.4 2.4 %collective-permute-start.3 = (bf16[32,256]{1,0:T(8,128)(2,1)}, bf16[32,256]{1,0:T(8,128)(2,1)S(1)}, u32[]{:S(2)}, u32[]{:S(2)}) collective-permute-start(bf16[32,256]{1,0:T(8,128)(2,1)} %get-tuple-element.35), channel_id=1, source_target_pairs={{0,1},{1,0},{2,3},{3,2},{4,5},{5,4},{6,7},{7,6},{8,9},{9,8},{10,11... | collective-permute-start | bytes 49160 | tf_op jit(solution)/shard_map/ppermute | solution.py:626
  29.6 22.9 %all-to-all-start.1 = ((bf16[8,128,256]{2,1,0:T(8,128)(2,1)}), bf16[8,128,256]{2,1,0:T(8,128)(2,1)}, u32[]{:S(2)}, u32[]{:S(2)}) async-start(bf16[8,128,256]{2,1,0:T(8,128)(2,1)} %broadcast_dynamic-update-slice_fusion), calls=%async_computation.1 | async-start | bytes 1048576 | tf_op jit(solution)/shard_map/all_to_all | solution.py:611
  36.5 1.3 %copy-start = (bf16[3,256,256]{2,1,0:T(8,128)(2,1)}, bf16[3,256,256]{2,1,0:T(8,128)(2,1)S(1)}, u32[]{:S(2)}) copy-start(bf16[3,256,256]{2,1,0:T(8,128)(2,1)S(1)} %collective-permute-done.4.near_hbm) | copy-start | bytes 1179652
  37.8 0.8 %copy-start.1 = (bf16[3,256,256]{2,1,0:T(8,128)(2,1)}, bf16[3,256,256]{2,1,0:T(8,128)(2,1)S(1)}, u32[]{:S(2)}) copy-start(bf16[3,256,256]{2,1,0:T(8,128)(2,1)S(1)} %collective-permute-done.5.far_hbm) | copy-start | bytes 1179652
